TPU v7x, 32 devices: a whole 2x2x4 slice. The times are simulated.
32 devices in a mesh: gx: 4 (over z), gy: 8 (over y, x, core).
Axes of the slice: x: 2, y: 2, z: 4, core: 2. Of those that a mesh axis runs over, the one named last changes fastest.
Arguments:
- tokens: bfloat16 [64, 216, 512], P(('gx', 'gy')), may hold values from -6 to 6
- segment_ids: int32 [64, 216], P(('gx', 'gy')), may hold values from 0 to 3, never falling along the last dimension, each value on 1 to 108 neighbouring positions
- pack_task: int32 [64], replicated, may hold values from 0 to 23
- task_experts: int32 [24, 2], replicated, may hold values from 0 to 31, all different within a row
- w_qkv: bfloat16 [512, 1536], P(('gx', 'gy')), may hold values from -0.25 to 0.25
- w_attn_out: bfloat16 [512, 512], P(('gx', 'gy')), may hold values from -2 to 2
- w_router: bfloat16 [512, 32], P(('gx', 'gy')), may hold values from -0.1875 to 0.1875
- w_expert_in: bfloat16 [32, 512, 2048], P(None, ('gx', 'gy')), may hold values from -0.25 to 0.25
- w_expert_out: bfloat16 [32, 2048, 512], P(None, ('gx', 'gy')), may hold values from -0.125 to 0.125
- norm1_gain: bfloat16 [512], P(('gx', 'gy')), may hold values from 0.099609375 to 1.8984375
- norm1_bias: bfloat16 [512], P(('gx', 'gy')), may hold values from -3 to 3
- norm2_gain: bfloat16 [512], P(('gx', 'gy')), may hold values from 0.099609375 to 1.8984375
- norm2_bias: bfloat16 [512], P(('gx', 'gy')), may hold values from -3 to 3
- cotangent: bfloat16 [64, 216, 512], P(('gx', 'gy')), may hold values from -6 to 6
Outputs:
- mixed: bfloat16 [64, 216, 512], P(('gx', 'gy'))
- d_tokens: bfloat16 [64, 216, 512], P(('gx', 'gy'))
- d_qkv: float32 [512, 1536], P(('gx', 'gy'))
- d_attn_out: float32 [512, 512], P(('gx', 'gy'))
- d_router: float32 [512, 32], P(('gx', 'gy'))
- d_expert_in: float32 [32, 512, 2048], P(None, ('gx', 'gy'))
- d_expert_out: float32 [32, 2048, 512], P(None, ('gx', 'gy'))
- d_gain1: float32 [512], P(('gx', 'gy'))
- d_bias1: float32 [512], P(('gx', 'gy'))
- d_gain2: float32 [512], P(('gx', 'gy'))
- d_bias2: float32 [512], P(('gx', 'gy'))
Inputs may be any that keep to these rules, and one draw needn't show every extreme that they name: `segment_ids`: within a pack the ids never fall, the pack has 4 segments of 1 to 108 tokens, one of exactly that many. `task_experts`: each task names two different experts; every expert is named by some task.
All inputs are finite; a program needn't handle non-finite values.
Results may differ from a plain program's by a relative error of at most 0.012.
Values may be sent and summed in bfloat16 or wider, within the bound.
A program may use at most 192 MiB of HBM per device.

v0:
```python
import math

import jax
import jax.numpy as jnp
from jax import lax
from jax.sharding import PartitionSpec as P

HEADS = 8


EPS = 1e-05
MASK_FILL = -1e30
HIGH = lax.Precision.HIGHEST


def shortened(value):

    def short(part):
        return part.astype(jnp.bfloat16) if part.dtype == jnp.float32 else part

    return jax.tree.map(short, value)


def layer_norm(values, gain, bias):
    center = values - jnp.mean(values, -1, keepdims=True)
    spread = jnp.mean(center * center, -1, keepdims=True)
    return center * lax.rsqrt(spread + EPS) * gain + bias


def contract_rows(left, right):
    return lax.dot_general(
        left, right, (((0,), (0,)), ((), ())), preferred_element_type=jnp.float32
    )


def contract_cols(left, right):
    return lax.dot_general(
        left, right, (((1,), (1,)), ((), ())), preferred_element_type=jnp.float32
    )


def shards(
    tokens,
    segment_ids,
    pack_task,
    task_experts,
    w_qkv,
    w_attn_out,
    w_router,
    w_expert_in,
    w_expert_out,
    norm1_gain,
    norm1_bias,
    norm2_gain,
    norm2_bias,
    cotangent,
):
    outer = lax.axis_size("gx")
    inner = lax.axis_size("gy")
    devices = outer * inner
    micro, length, width = tokens.shape
    experts, slab_in, hidden = w_expert_in.shape
    slab_out = w_expert_out.shape[1]
    head_size = width // HEADS
    scale = 1.0 / math.sqrt(head_size)
    device = lax.axis_index("gx") * inner + lax.axis_index("gy")
    gathered = (
        lax.all_gather(w_qkv, ("gx", "gy"), axis=0, tiled=True),
        lax.all_gather(w_attn_out, ("gx", "gy"), axis=0, tiled=True),
        lax.all_gather(w_router, ("gx", "gy"), axis=0, tiled=True),
        lax.all_gather(norm1_gain, ("gx", "gy"), axis=0, tiled=True),
        lax.all_gather(norm1_bias, ("gx", "gy"), axis=0, tiled=True),
        lax.all_gather(norm2_gain, ("gx", "gy"), axis=0, tiled=True),
        lax.all_gather(norm2_bias, ("gx", "gy"), axis=0, tiled=True),
    )
    qkv_full, attn_full, route_full = (gathered[0], gathered[1], gathered[2])
    gain_one, bias_one, gain_two, bias_two = tuple(
        (piece.astype(jnp.float32) for piece in gathered[3:])
    )
    route_float = route_full.astype(jnp.float32)
    pack_pairs = task_experts[pack_task]
    needs = jnp.transpose(pack_pairs.reshape(outer, inner, micro, 2), (2, 3, 0, 1))
    route_pairs = jnp.transpose(pack_pairs.reshape(devices, micro, 2), (1, 0, 2))
    own_pairs = lax.dynamic_slice_in_dim(pack_pairs, device * micro, micro, 0)
    expert_ids = jnp.arange(experts, dtype=jnp.int32)

    def slabs(need):
        return (w_expert_in[need], w_expert_out[need])

    def joined(pieces):
        return (
            pieces[0].reshape(pieces[0].shape[0], width, hidden),
            pieces[1].reshape(pieces[1].shape[0], hidden, width),
        )

    def attention_probs(project, segment):
        queries = project[:, :width].reshape(length, HEADS, head_size)
        keys_all = project[:, width : 2 * width].reshape(length, HEADS, head_size)
        scores = (
            jnp.einsum("qhd,khd->hqk", queries, keys_all, preferred_element_type=jnp.float32)
            * scale
        )
        same_doc = segment[:, None] == segment[None, :]
        return jnp.where(same_doc[None], scores, MASK_FILL)

    def forward_step(carry, inputs):
        block, segment, need, pair, senders = inputs
        block_float = block.astype(jnp.float32)
        normed = layer_norm(block_float, gain_one, bias_one).astype(jnp.bfloat16)
        project = jnp.dot(normed, qkv_full, preferred_element_type=jnp.float32).astype(jnp.bfloat16)
        masked = attention_probs(project, segment)
        peak = jnp.max(masked, -1, keepdims=True)
        raised = jnp.exp(masked - peak)
        totals = jnp.sum(raised, -1, keepdims=True)
        log_total = peak + jnp.log(totals)
        attn_low = (raised / totals).astype(jnp.bfloat16)
        values_all = project[:, 2 * width :].reshape(length, HEADS, head_size)
        heads_out = (
            jnp.einsum("hqk,khd->qhd", attn_low, values_all, preferred_element_type=jnp.float32)
            .reshape(length, width)
            .astype(jnp.bfloat16)
        )
        middle = block_float + jnp.dot(heads_out, attn_full, preferred_element_type=jnp.float32)
        routed = layer_norm(middle, gain_two, bias_two).astype(jnp.bfloat16)
        logits = jnp.dot(routed, route_full, preferred_element_type=jnp.float32)
        select = (expert_ids[None, :] == pair[:, None]).astype(jnp.float32)
        chosen = jnp.sum(logits[:, None, :] * select[None], -1)
        raised_gate = jnp.exp(chosen - jnp.max(chosen, -1, keepdims=True))
        gates = raised_gate / jnp.sum(raised_gate, -1, keepdims=True)
        weights_in, weights_out = joined(
            lax.all_to_all(
                lax.all_to_all(
                    shortened(slabs(need)), "gx", split_axis=1, concat_axis=1, tiled=True
                ),
                "gy",
                split_axis=2,
                concat_axis=2,
                tiled=True,
            )
        )
        hidden_pre = jnp.einsum(
            "ld,kdf->klf", routed, weights_in, preferred_element_type=jnp.float32
        )
        hidden_low = jax.nn.gelu(hidden_pre).astype(jnp.bfloat16)
        expert_out = jnp.einsum(
            "klf,kfd->kld", hidden_low, weights_out, preferred_element_type=jnp.float32
        )
        saved = ()
        mixed = middle + gates[:, 0:1] * expert_out[0] + gates[:, 1:2] * expert_out[1]
        kept = (
            normed,
            project,
            log_total,
            heads_out,
            middle,
            routed,
            gates,
            hidden_pre,
            hidden_low,
            expert_out,
            saved,
        )
        return (carry, (mixed.astype(jnp.bfloat16), kept))

    start = jnp.zeros((), jnp.float32)
    unused, (mixed_all, kept_all) = lax.scan(
        forward_step, start, (tokens, segment_ids, needs, own_pairs, route_pairs)
    )

    def backward_step(carry, inputs):
        dense_acc, shard_in, shard_out, holding = carry
        block, grad_top, segment, need, pair, kept = inputs
        (
            normed,
            project,
            log_total,
            heads_out,
            middle,
            routed,
            gates,
            hidden_pre,
            hidden_low,
            expert_out,
            saved,
        ) = kept
        grad_float = grad_top.astype(jnp.float32)
        grad_gate = jnp.sum(grad_float[None] * expert_out, -1).T
        grad_chosen = gates * (grad_gate - jnp.sum(gates * grad_gate, -1, keepdims=True))
        select = (expert_ids[None, :] == pair[:, None]).astype(jnp.float32)
        grad_logits = jnp.sum(grad_chosen[:, :, None] * select[None], 1)
        routed_float = routed.astype(jnp.float32)
        grad_route = jnp.dot(routed_float.T, grad_logits, precision=HIGH)
        grad_routed = jnp.dot(grad_logits, route_float.T, precision=HIGH)
        grad_eout = (gates.T[:, :, None] * grad_float[None]).astype(jnp.bfloat16)
        slot = ()
        weights_in, weights_out = joined(
            lax.all_to_all(
                lax.all_to_all(
                    shortened(slabs(need)), "gx", split_axis=1, concat_axis=1, tiled=True
                ),
                "gy",
                split_axis=2,
                concat_axis=2,
                tiled=True,
            )
        )
        grad_act = jnp.einsum(
            "kld,kfd->klf", grad_eout, weights_out, preferred_element_type=jnp.float32
        )
        unused_act, gelu_back = jax.vjp(jax.nn.gelu, hidden_pre)
        grad_pre = gelu_back(grad_act)[0].astype(jnp.bfloat16)
        grad_in = jnp.einsum("ld,klf->kdf", routed, grad_pre, preferred_element_type=jnp.float32)
        grad_out = jnp.einsum(
            "klf,kld->kfd", hidden_low, grad_eout, preferred_element_type=jnp.float32
        )
        grad_routed = grad_routed + jnp.einsum(
            "klf,kdf->ld", grad_pre, weights_in, preferred_element_type=jnp.float32
        )
        slot = (grad_in, grad_out)
        unused_two, norm_two_back = jax.vjp(layer_norm, middle, gain_two, bias_two)
        grad_mid_norm, grad_gain_two, grad_bias_two = norm_two_back(grad_routed)
        grad_middle = grad_float + grad_mid_norm
        grad_attended = grad_middle.astype(jnp.bfloat16)
        grad_attn_w = contract_rows(heads_out, grad_attended)
        grad_heads = (
            contract_cols(grad_attended, attn_full)
            .astype(jnp.bfloat16)
            .reshape(length, HEADS, head_size)
        )
        masked = attention_probs(project, segment)
        probs_float = jnp.exp(masked - log_total)
        probs_low = probs_float.astype(jnp.bfloat16)
        queries = project[:, :width].reshape(length, HEADS, head_size)
        keys_all = project[:, width : 2 * width].reshape(length, HEADS, head_size)
        values_all = project[:, 2 * width :].reshape(length, HEADS, head_size)
        grad_values = jnp.einsum(
            "hqk,qhd->khd", probs_low, grad_heads, preferred_element_type=jnp.float32
        )
        grad_probs = jnp.einsum(
            "qhd,khd->hqk", grad_heads, values_all, preferred_element_type=jnp.float32
        )
        row_dot = jnp.sum(probs_float * grad_probs, -1, keepdims=True)
        grad_scores = (probs_float * (grad_probs - row_dot)).astype(jnp.bfloat16)
        grad_queries = (
            jnp.einsum("hqk,khd->qhd", grad_scores, keys_all, preferred_element_type=jnp.float32)
            * scale
        )
        grad_keys = (
            jnp.einsum("hqk,qhd->khd", grad_scores, queries, preferred_element_type=jnp.float32)
            * scale
        )
        grad_qkv = jnp.concatenate(
            [
                grad_queries.reshape(length, width),
                grad_keys.reshape(length, width),
                grad_values.reshape(length, width),
            ],
            -1,
        ).astype(jnp.bfloat16)
        grad_qkv_w = contract_rows(normed, grad_qkv)
        grad_normed = contract_cols(grad_qkv, qkv_full)
        unused_one, norm_one_back = jax.vjp(
            layer_norm, block.astype(jnp.float32), gain_one, bias_one
        )
        grad_in_norm, grad_gain_one, grad_bias_one = norm_one_back(grad_normed)
        grad_tokens = (grad_middle + grad_in_norm).astype(jnp.bfloat16)
        terms = (
            grad_qkv_w,
            grad_attn_w,
            grad_route,
            grad_gain_one,
            grad_bias_one,
            grad_gain_two,
            grad_bias_two,
        )
        dense_acc = tuple((total + term for total, term in zip(dense_acc, terms)))
        return ((dense_acc, shard_in, shard_out, holding), (grad_tokens, slot))

    dense_zero = (
        jnp.zeros((width, 3 * width), jnp.float32),
        jnp.zeros((width, width), jnp.float32),
        jnp.zeros((width, experts), jnp.float32),
        jnp.zeros((width,), jnp.float32),
        jnp.zeros((width,), jnp.float32),
        jnp.zeros((width,), jnp.float32),
        jnp.zeros((width,), jnp.float32),
    )
    shard_zero_in = jnp.zeros((experts, slab_in, hidden), jnp.float32)
    shard_zero_out = jnp.zeros((experts, slab_out, width), jnp.float32)
    holding_zero = ()
    (dense_acc, shard_in, shard_out, holding), (grad_tokens_all, slots) = lax.scan(
        backward_step,
        (dense_zero, shard_zero_in, shard_zero_out, holding_zero),
        (tokens, cotangent, segment_ids, needs, own_pairs, kept_all),
    )
    slot_in = slots[0].reshape(micro * 2, width, hidden)
    slot_out = slots[1].reshape(micro * 2, hidden, width)
    amount = slot_in.shape[0]
    returned = lax.all_to_all(
        lax.all_to_all(
            shortened(
                (
                    slot_in.reshape(amount, outer, inner, slab_in, hidden),
                    slot_out.reshape(amount, outer, inner, slab_out, width),
                )
            ),
            "gx",
            split_axis=1,
            concat_axis=1,
            tiled=True,
        ),
        "gy",
        split_axis=2,
        concat_axis=2,
        tiled=True,
    )
    onehot = (
        needs.reshape(micro * 2, outer, inner)[None] == expert_ids[:, None, None, None]
    ).astype(jnp.float32)
    added = tuple(
        (jnp.einsum("esab,sabrc->erc", onehot, piece, precision=HIGH) for piece in returned)
    )
    shard_in = shard_in + added[0]
    shard_out = shard_out + added[1]
    dense_shards = (
        lax.psum_scatter(dense_acc[0], ("gx", "gy"), scatter_dimension=0, tiled=True),
        lax.psum_scatter(dense_acc[1], ("gx", "gy"), scatter_dimension=0, tiled=True),
        lax.psum_scatter(dense_acc[2], ("gx", "gy"), scatter_dimension=0, tiled=True),
        lax.psum_scatter(dense_acc[3], ("gx", "gy"), scatter_dimension=0, tiled=True),
        lax.psum_scatter(dense_acc[4], ("gx", "gy"), scatter_dimension=0, tiled=True),
        lax.psum_scatter(dense_acc[5], ("gx", "gy"), scatter_dimension=0, tiled=True),
        lax.psum_scatter(dense_acc[6], ("gx", "gy"), scatter_dimension=0, tiled=True),
    )
    return (
        mixed_all,
        grad_tokens_all,
        dense_shards[0],
        dense_shards[1],
        dense_shards[2],
        shard_in,
        shard_out,
        dense_shards[3],
        dense_shards[4],
        dense_shards[5],
        dense_shards[6],
    )


def solution(mesh):
    placed = (
        P(("gx", "gy"), None, None),
        P(("gx", "gy"), None),
        P(),
        P(),
        P(("gx", "gy"), None),
        P(("gx", "gy"), None),
        P(("gx", "gy"), None),
        P(None, ("gx", "gy"), None),
        P(None, ("gx", "gy"), None),
        P(("gx", "gy")),
        P(("gx", "gy")),
        P(("gx", "gy")),
        P(("gx", "gy")),
        P(("gx", "gy"), None, None),
    )
    return jax.shard_map(
        shards,
        mesh=mesh,
        in_specs=placed,
        out_specs=(
            P(("gx", "gy"), None, None),
            P(("gx", "gy"), None, None),
            P(("gx", "gy"), None),
            P(("gx", "gy"), None),
            P(("gx", "gy"), None),
            P(None, ("gx", "gy"), None),
            P(None, ("gx", "gy"), None),
            P(("gx", "gy")),
            P(("gx", "gy")),
            P(("gx", "gy")),
            P(("gx", "gy")),
        ),
        check_vma=False,
    )
```

profile of v0, /device:TPU:8, one launch (start us, length us, event | category | flops | bytes accessed | tf_op | source)
XLA Modules:
  0.0 2342.1 jit_solution(4184883084381475686)
XLA Ops:
  11.5 40.7 %all-reduce.9 = (bf16[512]{0:T(512)(128)(2,1)S(1)}, bf16[512]{0:T(512)(128)(2,1)S(1)}, bf16[512]{0:T(512)(128)(2,1)S(1)}, bf16[512]{0:T(512)(128)(2,1)S(1)}) all-reduce(bf16[512]{0:T(512)(128)(2,1)S(1)} %dynamic-update-slice, bf16[512]{0:T(512)(128)(2,1)S(1)} %dynamic-update-slice.1, ...), channel_id=1, replica_groups=mesh['gx'=4,'gy'=8] {'gx','gy'}, use_global_device_ids=true, to_apply=%add | all-reduce | flops 2048 | bytes 8192
  55.8 37.0 %all_gather.27 = bf16[512,32]{1,0:T(8,128)(2,1)} all-gather(bf16[16,32]{1,0:T(8,128)(2,1)} %param.24), channel_id=1, replica_groups=mesh['gx'=4,'gy'=8] {'gx','gy'}, dimensions={0}, use_global_device_ids=true | all-gather | bytes 33792 | tf_op jit(solution)/shard_map/all_gather | solution.py:70
  95.0 41.1 %all_gather.24 = bf16[512,512]{1,0:T(8,128)(2,1)} all-gather(bf16[16,512]{1,0:T(8,128)(2,1)} %param.23), channel_id=1, replica_groups=mesh['gx'=4,'gy'=8] {'gx','gy'}, dimensions={0}, use_global_device_ids=true | all-gather | bytes 540672 | tf_op jit(solution)/shard_map/all_gather | solution.py:69
  139.3 640.8 %while.62 = (s32[]{:T(128)}, bf16[2,216,512]{2,1,0:T(8,128)(2,1)}, bf16[2,216,512]{2,1,0:T(8,128)(2,1)}, bf16[2,216,1536]{2,1,0:T(8,128)(2,1)}, f32[2,8,216,1]{2...) while((s32[]{:T(128)}, bf16[2,216,512]{2,1,0:T(8,128)(2,1)}, ...), condition=%wide.region_10.11_spmd.clone, body=%wide.region_0.10_spmd.clone.sunk | while | flops 2392236800 | bytes 207222192 | solution.py:166
  168.7 83.1 %all-to-all-done.2 = bf16[2,4,8,16,2048]{4,3,2,0,1:T(8,128)(2,1)} async-done(((bf16[2,4,8,16,2048]{4,3,2,0,1:T(8,128)(2,1)}), bf16[2,4,8,16,2048]{4,3,2,0,1:T(8,128)(2,1)}, u32[]{:S(2)}, u32[]{:S(2)}) %all-to-all-start.2) | async-done | bytes 4194336 | tf_op jit(solution)/shard_map/while/body/eval_jaxpr/all_to_all | solution.py:132
  264.8 85.1 %all-to-all-done = bf16[2,4,8,64,512]{4,3,2,0,1:T(8,128)(2,1)} async-done(((bf16[2,4,8,64,512]{4,3,2,0,1:T(8,128)(2,1)}), bf16[2,4,8,64,512]{4,3,2,0,1:T(8,128)(2,1)}, u32[]{:S(2)}, u32[]{:S(2)}) %all-to-all-start) | async-done | bytes 4194336 | tf_op jit(solution)/shard_map/while/body/eval_jaxpr/all_to_all | solution.py:132
  364.8 38.8 %all-to-all-done.3 = bf16[2,4,8,16,2048]{4,3,1,0,2:T(8,128)(2,1)} async-done(((bf16[2,4,8,16,2048]{4,3,1,0,2:T(8,128)(2,1)}), bf16[2,4,8,16,2048]{4,3,1,0,2:T(8,128)(2,1)}, u32[]{:S(2)}, u32[]{:S(2)}) %all-to-all-start.3) | async-done | bytes 4194336 | tf_op jit(solution)/shard_map/while/body/eval_jaxpr/all_to_all | solution.py:131
  423.9 33.4 %all-to-all-done.1 = bf16[2,4,8,64,512]{4,3,1,0,2:T(8,128)(2,1)} async-done(((bf16[2,4,8,64,512]{4,3,1,0,2:T(8,128)(2,1)}), bf16[2,4,8,64,512]{4,3,1,0,2:T(8,128)(2,1)}, u32[]{:S(2)}, u32[]{:S(2)}) %all-to-all-start.1) | async-done | bytes 4194336 | tf_op jit(solution)/shard_map/while/body/eval_jaxpr/all_to_all | solution.py:131
  489.0 79.7 %all-to-all-done.2 = bf16[2,4,8,16,2048]{4,3,2,0,1:T(8,128)(2,1)} async-done(((bf16[2,4,8,16,2048]{4,3,2,0,1:T(8,128)(2,1)}), bf16[2,4,8,16,2048]{4,3,2,0,1:T(8,128)(2,1)}, u32[]{:S(2)}, u32[]{:S(2)}) %all-to-all-start.2) | async-done | bytes 4194336 | tf_op jit(solution)/shard_map/while/body/eval_jaxpr/all_to_all | solution.py:132
  581.6 84.6 %all-to-all-done = bf16[2,4,8,64,512]{4,3,2,0,1:T(8,128)(2,1)} async-done(((bf16[2,4,8,64,512]{4,3,2,0,1:T(8,128)(2,1)}), bf16[2,4,8,64,512]{4,3,2,0,1:T(8,128)(2,1)}, u32[]{:S(2)}, u32[]{:S(2)}) %all-to-all-start) | async-done | bytes 4194336 | tf_op jit(solution)/shard_map/while/body/eval_jaxpr/all_to_all | solution.py:132
  681.7 38.9 %all-to-all-done.3 = bf16[2,4,8,16,2048]{4,3,1,0,2:T(8,128)(2,1)} async-done(((bf16[2,4,8,16,2048]{4,3,1,0,2:T(8,128)(2,1)}), bf16[2,4,8,16,2048]{4,3,1,0,2:T(8,128)(2,1)}, u32[]{:S(2)}, u32[]{:S(2)}) %all-to-all-start.3) | async-done | bytes 4194336 | tf_op jit(solution)/shard_map/while/body/eval_jaxpr/all_to_all | solution.py:131
  780.9 687.4 %while.63 = (s32[]{:T(128)}, f32[512,1536]{1,0:T(8,128)}, f32[512,512]{1,0:T(8,128)}, f32[512,32]{0,1:T(8,128)}, f32[512]{0:T(512)}, /*index=5*/f32[512]{0:T(512...) while((s32[]{:T(128)}, f32[512,1536]{1,0:T(8,128)}, ...), condition=%wide.region_28.29_spmd.clone, body=%wide.region_11.28_spmd.clone.sunk | while | flops 4889857024 | bytes 293456960 | solution.py:291
  807.1 79.6 %all-to-all-done.4 = bf16[2,4,8,64,512]{4,3,2,0,1:T(8,128)(2,1)} async-done(((bf16[2,4,8,64,512]{4,3,2,0,1:T(8,128)(2,1)}), bf16[2,4,8,64,512]{4,3,2,0,1:T(8,128)(2,1)}, u32[]{:S(2)}, u32[]{:S(2)}) %all-to-all-start.4) | async-done | bytes 4194336 | tf_op jit(solution)/shard_map/while/body/eval_jaxpr/all_to_all | solution.py:198
  899.7 84.7 %all-to-all-done.6 = bf16[2,4,8,16,2048]{4,3,2,0,1:T(8,128)(2,1)} async-done(((bf16[2,4,8,16,2048]{4,3,2,0,1:T(8,128)(2,1)}), bf16[2,4,8,16,2048]{4,3,2,0,1:T(8,128)(2,1)}, u32[]{:S(2)}, u32[]{:S(2)}) %all-to-all-start.6) | async-done | bytes 4194336 | tf_op jit(solution)/shard_map/while/body/eval_jaxpr/all_to_all | solution.py:198
  999.1 39.6 %all-to-all-done.5 = bf16[2,4,8,64,512]{4,3,1,0,2:T(8,128)(2,1)} async-done(((bf16[2,4,8,64,512]{4,3,1,0,2:T(8,128)(2,1)}), bf16[2,4,8,64,512]{4,3,1,0,2:T(8,128)(2,1)}, u32[]{:S(2)}, u32[]{:S(2)}) %all-to-all-start.5) | async-done | bytes 4194336 | tf_op jit(solution)/shard_map/while/body/eval_jaxpr/all_to_all | solution.py:197
  1149.5 79.6 %all-to-all-done.4 = bf16[2,4,8,64,512]{4,3,2,0,1:T(8,128)(2,1)} async-done(((bf16[2,4,8,64,512]{4,3,2,0,1:T(8,128)(2,1)}), bf16[2,4,8,64,512]{4,3,2,0,1:T(8,128)(2,1)}, u32[]{:S(2)}, u32[]{:S(2)}) %all-to-all-start.4) | async-done | bytes 4194336 | tf_op jit(solution)/shard_map/while/body/eval_jaxpr/all_to_all | solution.py:198
  1242.1 84.7 %all-to-all-done.6 = bf16[2,4,8,16,2048]{4,3,2,0,1:T(8,128)(2,1)} async-done(((bf16[2,4,8,16,2048]{4,3,2,0,1:T(8,128)(2,1)}), bf16[2,4,8,16,2048]{4,3,2,0,1:T(8,128)(2,1)}, u32[]{:S(2)}, u32[]{:S(2)}) %all-to-all-start.6) | async-done | bytes 4194336 | tf_op jit(solution)/shard_map/while/body/eval_jaxpr/all_to_all | solution.py:198
  1341.5 39.6 %all-to-all-done.5 = bf16[2,4,8,64,512]{4,3,1,0,2:T(8,128)(2,1)} async-done(((bf16[2,4,8,64,512]{4,3,1,0,2:T(8,128)(2,1)}), bf16[2,4,8,64,512]{4,3,1,0,2:T(8,128)(2,1)}, u32[]{:S(2)}, u32[]{:S(2)}) %all-to-all-start.5) | async-done | bytes 4194336 | tf_op jit(solution)/shard_map/while/body/eval_jaxpr/all_to_all | solution.py:197
  1500.1 165.7 %all-to-all-done.8 = bf16[4,4,8,16,2048]{4,2,0,3,1:T(8,128)(2,1)} async-done(((bf16[4,4,8,16,2048]{4,2,0,3,1:T(8,128)(2,1)}), bf16[4,4,8,16,2048]{4,2,0,3,1:T(8,128)(2,1)}, u32[]{:S(2)}, u32[]{:S(2)}) %all-to-all-start.8) | async-done | bytes 8388640 | tf_op jit(solution)/shard_map/all_to_all | solution.py:300
  1686.9 167.0 %all-to-all-done.10 = bf16[4,4,8,64,512]{4,2,0,3,1:T(8,128)(2,1)} async-done(((bf16[4,4,8,64,512]{4,2,0,3,1:T(8,128)(2,1)}), bf16[4,4,8,64,512]{4,2,0,3,1:T(8,128)(2,1)}, u32[]{:S(2)}, u32[]{:S(2)}) %all-to-all-start.10) | async-done | bytes 8388640 | tf_op jit(solution)/shard_map/all_to_all | solution.py:300
  1868.6 84.7 %all-to-all-done.9 = bf16[4,4,8,16,2048]{4,0,1,3,2:T(4,128)(2,1)} async-done(((bf16[4,4,8,16,2048]{4,0,1,3,2:T(4,128)(2,1)}), bf16[4,4,8,16,2048]{4,0,1,3,2:T(4,128)(2,1)}, u32[]{:S(2)}, u32[]{:S(2)}) %all-to-all-start.9) | async-done | bytes 8388640 | tf_op jit(solution)/shard_map/all_to_all | solution.py:299
  1961.3 125.8 %all-reduce.8 = (f32[512]{0:T(512)S(1)}, f32[512]{0:T(512)S(1)}, f32[512]{0:T(512)S(1)}, f32[512]{0:T(512)S(1)}) all-reduce(f32[512]{0:T(512)S(1)} %copy-done.40, f32[512]{0:T(512)S(1)} %copy-done.43, f32[512]{0:T(512)S(1)} %copy-done.46, f32[512]{0:T(512)S(1)} %copy-done.49), channel_id=5, replica_groups=mesh['gx'=4,'gy'=8] {'gx','gy'}, use_global_device_ids=true, to_apply=%region_32.33.clone | all-reduce | flops 2048 | bytes 16384
  2115.7 97.7 %reduce-scatter.6.cloned.1.call-done = f32[16,512]{1,0:T(8,128)} async-done(((f32[512,512]{1,0:T(8,128)}), f32[16,512]{1,0:T(8,128)}) %reduce-scatter.6.cloned.1.call-update) | async-done | bytes 32784 | tf_op jit(solution)/shard_map/reduce_scatter | solution.py:327
  2213.5 121.9 %reduce-scatter.4.cloned.1.call-done = f32[16,1536]{1,0:T(8,128)} async-done(((f32[512,1536]{1,0:T(8,128)}), f32[16,1536]{1,0:T(8,128)}) %reduce-scatter.4.cloned.1.call-update) | async-done | bytes 98320 | tf_op jit(solution)/shard_map/reduce_scatter | solution.py:326
  (509 shorter events, 592.7 us)
Async XLA Ops:
  7.2 128.9 %all-gather.2.cloned.1.call-start = ((), (), s32[]{:S(2)}) async-start(), calls=%async_computation.15 | async-start | bytes 1622016 | tf_op jit(solution)/shard_map/all_gather | solution.py:68
  149.4 102.5 %all-to-all-start.2 = ((bf16[2,4,8,16,2048]{4,3,2,0,1:T(8,128)(2,1)}), bf16[2,4,8,16,2048]{4,3,2,0,1:T(8,128)(2,1)}, u32[]{:S(2)}, u32[]{:S(2)}) async-start(bf16[2,4,8,16,2048]{4,3,2,0,1:T(8,128)(2,1)} %copy.235), calls=%async_computation.2 | async-start | bytes 8388608 | tf_op jit(solution)/shard_map/while/body/eval_jaxpr/all_to_all | solution.py:132
  251.8 98.1 %all-to-all-start = ((bf16[2,4,8,64,512]{4,3,2,0,1:T(8,128)(2,1)}), bf16[2,4,8,64,512]{4,3,2,0,1:T(8,128)(2,1)}, u32[]{:S(2)}, u32[]{:S(2)}) async-start(bf16[2,4,8,64,512]{4,3,2,0,1:T(8,128)(2,1)} %copy.232), calls=%async_computation | async-start | bytes 8388608 | tf_op jit(solution)/shard_map/while/body/eval_jaxpr/all_to_all | solution.py:132
  349.9 53.7 %all-to-all-start.3 = ((bf16[2,4,8,16,2048]{4,3,1,0,2:T(8,128)(2,1)}), bf16[2,4,8,16,2048]{4,3,1,0,2:T(8,128)(2,1)}, u32[]{:S(2)}, u32[]{:S(2)}) async-start(bf16[2,4,8,16,2048]{4,3,1,0,2:T(8,128)(2,1)} %copy.236), calls=%async_computation.3 | async-start | bytes 8388608 | tf_op jit(solution)/shard_map/while/body/eval_jaxpr/all_to_all | solution.py:131
  403.6 53.7 %all-to-all-start.1 = ((bf16[2,4,8,64,512]{4,3,1,0,2:T(8,128)(2,1)}), bf16[2,4,8,64,512]{4,3,1,0,2:T(8,128)(2,1)}, u32[]{:S(2)}, u32[]{:S(2)}) async-start(bf16[2,4,8,64,512]{4,3,1,0,2:T(8,128)(2,1)} %copy.233), calls=%async_computation.1 | async-start | bytes 8388608 | tf_op jit(solution)/shard_map/while/body/eval_jaxpr/all_to_all | solution.py:131
  473.2 95.5 %all-to-all-start.2 = ((bf16[2,4,8,16,2048]{4,3,2,0,1:T(8,128)(2,1)}), bf16[2,4,8,16,2048]{4,3,2,0,1:T(8,128)(2,1)}, u32[]{:S(2)}, u32[]{:S(2)}) async-start(bf16[2,4,8,16,2048]{4,3,2,0,1:T(8,128)(2,1)} %copy.235), calls=%async_computation.2 | async-start | bytes 8388608 | tf_op jit(solution)/shard_map/while/body/eval_jaxpr/all_to_all | solution.py:132
  568.7 97.6 %all-to-all-start = ((bf16[2,4,8,64,512]{4,3,2,0,1:T(8,128)(2,1)}), bf16[2,4,8,64,512]{4,3,2,0,1:T(8,128)(2,1)}, u32[]{:S(2)}, u32[]{:S(2)}) async-start(bf16[2,4,8,64,512]{4,3,2,0,1:T(8,128)(2,1)} %copy.232), calls=%async_computation | async-start | bytes 8388608 | tf_op jit(solution)/shard_map/while/body/eval_jaxpr/all_to_all | solution.py:132
  666.2 54.4 %all-to-all-start.3 = ((bf16[2,4,8,16,2048]{4,3,1,0,2:T(8,128)(2,1)}), bf16[2,4,8,16,2048]{4,3,1,0,2:T(8,128)(2,1)}, u32[]{:S(2)}, u32[]{:S(2)}) async-start(bf16[2,4,8,16,2048]{4,3,1,0,2:T(8,128)(2,1)} %copy.236), calls=%async_computation.3 | async-start | bytes 8388608 | tf_op jit(solution)/shard_map/while/body/eval_jaxpr/all_to_all | solution.py:131
  720.6 53.7 %all-to-all-start.1 = ((bf16[2,4,8,64,512]{4,3,1,0,2:T(8,128)(2,1)}), bf16[2,4,8,64,512]{4,3,1,0,2:T(8,128)(2,1)}, u32[]{:S(2)}, u32[]{:S(2)}) async-start(bf16[2,4,8,64,512]{4,3,1,0,2:T(8,128)(2,1)} %copy.233), calls=%async_computation.1 | async-start | bytes 8388608 | tf_op jit(solution)/shard_map/while/body/eval_jaxpr/all_to_all | solution.py:131
  791.2 95.5 %all-to-all-start.4 = ((bf16[2,4,8,64,512]{4,3,2,0,1:T(8,128)(2,1)}), bf16[2,4,8,64,512]{4,3,2,0,1:T(8,128)(2,1)}, u32[]{:S(2)}, u32[]{:S(2)}) async-start(bf16[2,4,8,64,512]{4,3,2,0,1:T(8,128)(2,1)} %copy.242), calls=%async_computation.4 | async-start | bytes 8388608 | tf_op jit(solution)/shard_map/while/body/eval_jaxpr/all_to_all | solution.py:198
  886.8 97.5 %all-to-all-start.6 = ((bf16[2,4,8,16,2048]{4,3,2,0,1:T(8,128)(2,1)}), bf16[2,4,8,16,2048]{4,3,2,0,1:T(8,128)(2,1)}, u32[]{:S(2)}, u32[]{:S(2)}) async-start(bf16[2,4,8,16,2048]{4,3,2,0,1:T(8,128)(2,1)} %copy.245), calls=%async_computation.6 | async-start | bytes 8388608 | tf_op jit(solution)/shard_map/while/body/eval_jaxpr/all_to_all | solution.py:198
  984.3 54.4 %all-to-all-start.5 = ((bf16[2,4,8,64,512]{4,3,1,0,2:T(8,128)(2,1)}), bf16[2,4,8,64,512]{4,3,1,0,2:T(8,128)(2,1)}, u32[]{:S(2)}, u32[]{:S(2)}) async-start(bf16[2,4,8,64,512]{4,3,1,0,2:T(8,128)(2,1)} %copy.243), calls=%async_computation.5 | async-start | bytes 8388608 | tf_op jit(solution)/shard_map/while/body/eval_jaxpr/all_to_all | solution.py:197
  1038.7 53.7 %all-to-all-start.7 = ((bf16[2,4,8,16,2048]{4,3,1,0,2:T(8,128)(2,1)}), bf16[2,4,8,16,2048]{4,3,1,0,2:T(8,128)(2,1)}, u32[]{:S(2)}, u32[]{:S(2)}) async-start(bf16[2,4,8,16,2048]{4,3,1,0,2:T(8,128)(2,1)} %copy.246), calls=%async_computation.7 | async-start | bytes 8388608 | tf_op jit(solution)/shard_map/while/body/eval_jaxpr/all_to_all | solution.py:197
  1133.6 95.5 %all-to-all-start.4 = ((bf16[2,4,8,64,512]{4,3,2,0,1:T(8,128)(2,1)}), bf16[2,4,8,64,512]{4,3,2,0,1:T(8,128)(2,1)}, u32[]{:S(2)}, u32[]{:S(2)}) async-start(bf16[2,4,8,64,512]{4,3,2,0,1:T(8,128)(2,1)} %copy.242), calls=%async_computation.4 | async-start | bytes 8388608 | tf_op jit(solution)/shard_map/while/body/eval_jaxpr/all_to_all | solution.py:198
  1229.2 97.5 %all-to-all-start.6 = ((bf16[2,4,8,16,2048]{4,3,2,0,1:T(8,128)(2,1)}), bf16[2,4,8,16,2048]{4,3,2,0,1:T(8,128)(2,1)}, u32[]{:S(2)}, u32[]{:S(2)}) async-start(bf16[2,4,8,16,2048]{4,3,2,0,1:T(8,128)(2,1)} %copy.245), calls=%async_computation.6 | async-start | bytes 8388608 | tf_op jit(solution)/shard_map/while/body/eval_jaxpr/all_to_all | solution.py:198
  1326.7 54.4 %all-to-all-start.5 = ((bf16[2,4,8,64,512]{4,3,1,0,2:T(8,128)(2,1)}), bf16[2,4,8,64,512]{4,3,1,0,2:T(8,128)(2,1)}, u32[]{:S(2)}, u32[]{:S(2)}) async-start(bf16[2,4,8,64,512]{4,3,1,0,2:T(8,128)(2,1)} %copy.243), calls=%async_computation.5 | async-start | bytes 8388608 | tf_op jit(solution)/shard_map/while/body/eval_jaxpr/all_to_all | solution.py:197
  1381.1 53.7 %all-to-all-start.7 = ((bf16[2,4,8,16,2048]{4,3,1,0,2:T(8,128)(2,1)}), bf16[2,4,8,16,2048]{4,3,1,0,2:T(8,128)(2,1)}, u32[]{:S(2)}, u32[]{:S(2)}) async-start(bf16[2,4,8,16,2048]{4,3,1,0,2:T(8,128)(2,1)} %copy.246), calls=%async_computation.7 | async-start | bytes 8388608 | tf_op jit(solution)/shard_map/while/body/eval_jaxpr/all_to_all | solution.py:197
  1479.7 186.0 %all-to-all-start.8 = ((bf16[4,4,8,16,2048]{4,2,0,3,1:T(8,128)(2,1)}), bf16[4,4,8,16,2048]{4,2,0,3,1:T(8,128)(2,1)}, u32[]{:S(2)}, u32[]{:S(2)}) async-start(bf16[4,4,8,16,2048]{4,2,0,3,1:T(8,128)(2,1)} %copy.184), calls=%async_computation.11 | async-start | bytes 16777216 | tf_op jit(solution)/shard_map/all_to_all | solution.py:300
  1665.7 188.2 %all-to-all-start.10 = ((bf16[4,4,8,64,512]{4,2,0,3,1:T(8,128)(2,1)}), bf16[4,4,8,64,512]{4,2,0,3,1:T(8,128)(2,1)}, u32[]{:S(2)}, u32[]{:S(2)}) async-start(bf16[4,4,8,64,512]{4,2,0,3,1:T(8,128)(2,1)} %copy.187), calls=%async_computation.13 | async-start | bytes 16777216 | tf_op jit(solution)/shard_map/all_to_all | solution.py:300
  1854.0 99.3 %all-to-all-start.9 = ((bf16[4,4,8,16,2048]{4,0,1,3,2:T(4,128)(2,1)}), bf16[4,4,8,16,2048]{4,0,1,3,2:T(4,128)(2,1)}, u32[]{:S(2)}, u32[]{:S(2)}) async-start(bf16[4,4,8,16,2048]{4,0,1,3,2:T(4,128)(2,1)} %copy.185), calls=%async_computation.12 | async-start | bytes 16777216 | tf_op jit(solution)/shard_map/all_to_all | solution.py:299
  1953.3 149.2 %all-to-all-start.11 = ((bf16[4,4,8,64,512]{4,0,1,3,2:T(4,128)(2,1)}), bf16[4,4,8,64,512]{4,0,1,3,2:T(4,128)(2,1)}, u32[]{:S(2)}, u32[]{:S(2)}) async-start(bf16[4,4,8,64,512]{4,0,1,3,2:T(4,128)(2,1)} %copy.188), calls=%async_computation.14 | async-start | bytes 16777216 | tf_op jit(solution)/shard_map/all_to_all | solution.py:299
  1958.3 157.4 %reduce-scatter.8.cloned.1.call-start = ((), (), s32[]{:S(2)}) async-start(), calls=%async_computation.18 | async-start | bytes 270336 | tf_op jit(solution)/shard_map/reduce_scatter | solution.py:328
  1959.3 254.2 %reduce-scatter.6.cloned.1.call-start = ((), (), s32[]{:S(2)}) async-start(), calls=%async_computation.17 | async-start | bytes 1081344 | tf_op jit(solution)/shard_map/reduce_scatter | solution.py:327
  1960.0 375.3 %reduce-scatter.4.cloned.1.call-start = ((), (), s32[]{:S(2)}) async-start(), calls=%async_computation.16 | async-start | bytes 3244032 | tf_op jit(solution)/shard_map/reduce_scatter | solution.py:326
  (103 other events, 1297.3 us)
Sparse Core Ops, SparseCore 0:
  10.9 55.1 all-gather.1
  1962.0 117.6 reduce-scatter.7
  2082.6 130.7 reduce-scatter.5
  2219.3 115.9 reduce-scatter.3
where the time goes:
time: 2350 us; the launch traced here: 2340 us
  waiting for transfers between devices  1590 us (68%)
  blocking collectives  245 us (10%)
  local copies, waits for them, and re-layouts  233 us (10%)
  starting transfers between devices  136 us (6%)
  matrix products  91 us (4%)
  other arithmetic  34.1 us (1%)
    all_to_all x2, waiting for transfers between devices, shards(): lax.all_to_all(shortened((slot_in.reshape(amount, outer, inner, slab_in,...  333 us
    all_to_all x4, waiting for transfers between devices, forward_step(): lax.all_to_all(shortened(slabs(need)), 'gx', split_axis=1, concat_axis=1,...  333 us
    all_to_all x4, waiting for transfers between devices, backward_step(): lax.all_to_all(shortened(slabs(need)), 'gx', split_axis=1, concat_axis=1,...  329 us
    unnamed x2, blocking collectives  167 us
    all_to_all x4, waiting for transfers between devices, forward_step(): lax.all_to_all(lax.all_to_all(shortened(slabs(need)), 'gx', split_axis=1,...  145 us
    all_to_all x4, waiting for transfers between devices, backward_step(): lax.all_to_all(lax.all_to_all(shortened(slabs(need)), 'gx', split_axis=1,...  143 us
    reduce_scatter x1, waiting for transfers between devices, shards(): lax.psum_scatter(dense_acc[0], ('gx', 'gy'), scatter_dimension=0, tiled=T...  122 us
    reduce_scatter x1, waiting for transfers between devices, shards(): lax.psum_scatter(dense_acc[1], ('gx', 'gy'), scatter_dimension=0, tiled=T...  97.7 us
  transfers between devices with their start and end apart: 24, of which 21 were waited for; matrix products, arithmetic and copies ran while one was open for 10% of the time, Pallas kernels for 0%

commit v1 on v0

--- a/solution.py
+++ b/solution.py
@@ -1,11 +1,17 @@
+import functools
 import math
 
 import jax
 import jax.numpy as jnp
 from jax import lax
+from jax.experimental import pallas as pl
+from jax.experimental.pallas import tpu as pltpu
 from jax.sharding import PartitionSpec as P
 
 HEADS = 8
+HEAD = 64
+PACK = 216
+GAIN_ONE = 32
 
 
 EPS = 1e-05
@@ -39,7 +45,7 @@
     )
 
 
-def shards(
+def shards_any(
     tokens,
     segment_ids,
     pack_task,
@@ -346,7 +352,890 @@
     )
 
 
+MESH = pl.DeviceIdType.MESH
+ROWS = 224
+SIDE = 128
+ROOT2PI = math.sqrt(2.0 / math.pi)
+
+
+def dot(left, right):
+    return jnp.dot(left, right, preferred_element_type=jnp.float32)
+
+
+class Place:
+    def __init__(self):
+        self.z = lax.axis_index("gx")
+        g = lax.axis_index("gy")
+        self.core = g % 2
+        across_x = g + 2 - 4 * ((g // 2) % 2)
+        across_y = g + 4 - 8 * (g // 4)
+        across_both = across_x + 4 - 8 * (across_x // 4)
+        self.at = (g, across_x, across_y, across_both)
+        self.sibling = (self.z, g + 1 - 2 * self.core)
+
+    def plane(self, k):
+        return (self.z + k) % 4
+
+    def device(self, rel, k):
+        return (self.plane(k), self.at[rel])
+
+    def chip(self, rel, k):
+        return self.plane(k) * 4 + self.at[rel] // 2
+
+    def index(self, rel, k):
+        return self.plane(k) * 8 + self.at[rel]
+
+    def greet(self):
+        barrier = pltpu.get_barrier_semaphore()
+        others = [(rel, k) for rel in range(4) for k in range(4) if (rel, k) != (0, 0)]
+        for rel, k in others:
+            pl.semaphore_signal(
+                barrier, inc=1, device_id=self.device(rel, k), device_id_type=MESH
+            )
+        pl.semaphore_signal(barrier, inc=1, device_id=self.sibling, device_id_type=MESH)
+        pl.semaphore_wait(barrier, len(others) + 1)
+
+
+def send(started, src, dst, send_sem, recv_sem, device):
+    copy = pltpu.make_async_remote_copy(
+        src_ref=src,
+        dst_ref=dst,
+        send_sem=send_sem,
+        recv_sem=recv_sem,
+        device_id=device,
+        device_id_type=MESH,
+    )
+    copy.start()
+    started.append(copy)
+
+
+def arrived(ref, sem):
+    pltpu.make_async_copy(ref, ref, sem).wait()
+
+
+def back(k):
+    return (4 - k) % 4
+
+
+class Spread:
+    def __init__(self, place, here, there, packs, half, sems):
+        self.place, self.here, self.there = place, here, there
+        self.packs, self.half, self.started = packs, half, []
+        self.send_sem, self.recv_sem = sems
+
+    def go(self, kind, k_sem, k_there, rel, k, p, src, rel_there, device):
+        send(
+            self.started,
+            src,
+            self.there(rel_there, k_there, p, rel, k),
+            self.send_sem.at[kind, k_sem * self.packs + p],
+            self.recv_sem.at[kind, k_there * self.packs + p],
+            device,
+        )
+
+    def wait(self, kind, rel, k, p):
+        arrived(self.here(rel, k, p), self.recv_sem.at[kind, k * self.packs + p])
+
+    def own(self, p, src, planes=True):
+        if planes:
+            for k in (1, 2, 3):
+                self.go(0, k, back(k), 0, 0, p, src, 0, self.place.device(0, k))
+        self.go(1, 0, 0, 0, 0, p, src, 1, self.place.device(1, 0))
+        self.go(2, 0, 0, 0, 0, p, src, 2, self.place.device(2, 0))
+
+    def plane(self, k, p):
+        if k:
+            self.wait(0, 0, k, p)
+            src = self.here(0, k, p)
+            self.go(1, k, k, 0, k, p, src, 1, self.place.device(1, 0))
+            self.go(2, k, k, 0, k, p, src, 2, self.place.device(2, 0))
+
+    def corner(self, k, p):
+        self.wait(1, 1, k, p)
+        self.wait(2, 2, k, p)
+        if self.half(k, p) == 0:
+            self.go(3, k, k, 1, k, p, self.here(1, k, p), 3, self.place.device(2, 0))
+        else:
+            self.go(3, k, k, 2, k, p, self.here(2, k, p), 3, self.place.device(1, 0))
+
+    def last(self, k, p):
+        self.wait(3, 3, k, p)
+
+    def finish(self):
+        for copy in self.started:
+            copy.wait_send()
+
+
+def norm_parts(values):
+    center = values - jnp.mean(values, -1, keepdims=True)
+    spread = jnp.mean(center * center, -1, keepdims=True)
+    rise = lax.rsqrt(spread + EPS)
+    return center * rise, rise
+
+
+def real_rows():
+    return lax.broadcasted_iota(jnp.int32, (ROWS, 1), 0) < PACK
+
+
+def head_lanes(h):
+    lane = lax.broadcasted_iota(jnp.int32, (1, SIDE), 1)
+    inside = (lane >= h * HEAD) & (lane < (h + 1) * HEAD)
+    return inside.astype(jnp.bfloat16)
+
+
+def softmax_rows(queries, keys, same):
+    scores = contract_cols(queries, keys) * (1.0 / math.sqrt(HEAD))
+    scores = jnp.where(same, scores, MASK_FILL)
+    raised = jnp.exp(scores - jnp.max(scores, -1, keepdims=True))
+    return raised * (1.0 / jnp.sum(raised, -1, keepdims=True))
+
+
+def pick(logits, expert):
+    lane = lax.broadcasted_iota(jnp.int32, logits.shape, 1)
+    return jnp.sum(jnp.where(lane == expert, logits, 0.0), -1, keepdims=True)
+
+
+def two_gates(logits, first, second):
+    gap = pick(logits, second) - pick(logits, first)
+    return 1.0 / (1.0 + jnp.exp(gap)), 1.0 / (1.0 + jnp.exp(-gap))
+
+
+def front_kernel(
+    tok, seg_col, seg_row, own_dense, cot, w_in, w_out,
+    routed_all, cot_all, w_in_all, w_out_all, dense_out, proj, heads, middle,
+    dense, routed, turned,
+    cot_send, cot_recv, routed_send, routed_recv, dense_send, dense_recv,
+    core_send, core_recv, in_send, in_recv, pair_send, pair_recv, local_sem,
+):
+    place = Place()
+    width = tok.shape[2]
+    place.greet()
+
+    def block_here(ref):
+        return lambda rel, k, p: ref.at[rel, k * 2 + p]
+
+    def block_there(ref):
+        return lambda rel_there, k_there, p, rel, k: ref.at[rel_there, k_there * 2 + p]
+
+    dense_tree = Spread(
+        place,
+        lambda rel, k, p: dense.at[place.index(rel, k)],
+        lambda rel_there, k_there, p, rel, k: dense.at[place.index(rel, k)],
+        1,
+        lambda k, p: k % 2,
+        (dense_send, dense_recv),
+    )
+    core_started = []
+
+    def to_core(rel, k):
+        slot = dense.at[place.index(rel, k)]
+        send(
+            core_started, slot, slot, core_send.at[rel, k], core_recv.at[rel, k], place.sibling
+        )
+
+    dense[place.index(0, 0)] = own_dense[...]
+    dense_tree.own(0, dense.at[place.index(0, 0)])
+    to_core(0, 0)
+    for k in (1, 2, 3):
+        dense_tree.plane(k, 0)
+        to_core(0, k)
+    for k in range(4):
+        dense_tree.corner(k, 0)
+        to_core(1, k)
+        to_core(2, k)
+
+    local = []
+
+    def local_copy(src, dst):
+        copy = pltpu.make_async_copy(src, dst, local_sem.at[len(local)])
+        copy.start()
+        local.append(copy)
+
+    cot_tree = Spread(
+        place, block_here(cot_all), block_there(cot_all), 2, lambda k, p: p, (cot_send, cot_recv)
+    )
+    for p in range(2):
+        cot_tree.own(p, cot.at[p])
+        local_copy(cot.at[p], cot_all.at[0, p])
+    for k in range(4):
+        dense_tree.last(k, 0)
+        to_core(3, k)
+    in_started = []
+    for rel in (3, 1, 2, 0):
+        for k in (2, 1, 3, 0):
+            columns = pl.ds(pl.multiple_of(place.chip(rel, k) * SIDE, SIDE), SIDE)
+            src = w_in.at[:, :, columns]
+            dst = w_in_all.at[place.chip(0, 0), place.core]
+            if (rel, k) == (0, 0):
+                local_copy(src, dst)
+            else:
+                send(
+                    in_started, src, dst, in_send.at[rel, k], in_recv.at[rel, back(k)],
+                    place.device(rel, k),
+                )
+    pair_started = []
+    local_copy(w_out, w_out_all.at[place.core])
+    send(
+        pair_started, w_out, w_out_all.at[place.core], pair_send.at[0], pair_recv.at[0],
+        place.sibling,
+    )
+    for k in range(4):
+        for rel in range(4):
+            slot = dense.at[place.plane(k) * 8 + place.at[rel] + 1 - 2 * place.core]
+            arrived(slot, core_recv.at[rel, k])
+    local_copy(dense, dense_out)
+
+    small = dense[:, :, 4 * width : 4 * width + SIDE].reshape(width, SIDE)
+    turned[...] = jnp.transpose(small.astype(jnp.float32))
+    gain_one, bias_one = turned[GAIN_ONE : GAIN_ONE + 1, :], turned[GAIN_ONE + 1 : GAIN_ONE + 2, :]
+    gain_two, bias_two = turned[GAIN_ONE + 2 : GAIN_ONE + 3, :], turned[GAIN_ONE + 3 : GAIN_ONE + 4, :]
+
+    routed_tree = Spread(
+        place,
+        block_here(routed_all),
+        block_there(routed_all),
+        2,
+        lambda k, p: p,
+        (routed_send, routed_recv),
+    )
+
+    for p in range(2):
+        block = tok[p].astype(jnp.float32)
+        unit, unused = norm_parts(block)
+        normed = (unit * gain_one + bias_one).astype(jnp.bfloat16)
+        w_qkv = dense[:, :, : 3 * width].reshape(width, 3 * width)
+        proj[p] = dot(normed, w_qkv).astype(jnp.bfloat16)
+        same = seg_col[p] == seg_row[p]
+
+        def pair_of_heads(j, carry, p=p, same=same):
+            at = pl.multiple_of(j * SIDE, SIDE)
+            queries = proj[p, :, pl.ds(at, SIDE)]
+            keys = proj[p, :, pl.ds(at + width, SIDE)]
+            values = proj[p, :, pl.ds(at + 2 * width, SIDE)]
+            out = jnp.zeros((ROWS, SIDE), jnp.float32)
+            for h in range(2):
+                lanes = head_lanes(h)
+                probs = softmax_rows(queries * lanes, keys, same).astype(jnp.bfloat16)
+                out = out + dot(probs, values * lanes)
+            heads[p, :, pl.ds(at, SIDE)] = out.astype(jnp.bfloat16)
+            return carry
+
+        lax.fori_loop(0, width // SIDE, pair_of_heads, 0)
+        w_attn = dense[:, :, 3 * width : 4 * width].reshape(width, width)
+        mid = block + dot(heads[p], w_attn)
+        middle[p] = mid
+        unit, unused = norm_parts(mid)
+        routed[p] = jnp.where(real_rows(), unit * gain_two + bias_two, 0.0).astype(jnp.bfloat16)
+        routed_tree.own(p, routed.at[p])
+        local_copy(routed.at[p], routed_all.at[0, p])
+
+    for k in (1, 2, 3):
+        for p in range(2):
+            cot_tree.plane(k, p)
+    for k in range(4):
+        for p in range(2):
+            cot_tree.corner(k, p)
+    for k in (1, 2, 3):
+        for p in range(2):
+            routed_tree.plane(k, p)
+    for rel in range(4):
+        for k in range(4):
+            if (rel, k) != (0, 0):
+                arrived(w_in_all.at[place.chip(rel, k), place.core], in_recv.at[rel, k])
+    local[2 + 0].wait()
+    mine = w_in_all.at[:, place.core]
+    send(pair_started, mine, mine, pair_send.at[1], pair_recv.at[1], place.sibling)
+    for k in range(4):
+        for p in range(2):
+            routed_tree.corner(k, p)
+    for k in range(4):
+        for p in range(2):
+            cot_tree.last(k, p)
+            routed_tree.last(k, p)
+    other = 1 - place.core
+    arrived(w_out_all.at[other], pair_recv.at[0])
+    arrived(w_in_all.at[:, other], pair_recv.at[1])
+    for copy in local[:2] + local[3:]:
+        copy.wait()
+    for tree in (dense_tree, cot_tree, routed_tree):
+        tree.finish()
+    for copy in core_started + in_started + pair_started:
+        copy.wait_send()
+
+
+def expert_kernel(
+    pairs, core, routed, cot, w_in_all, w_out_all, dense,
+    mixed, grad, d_in, d_out_own, d_out_far,
+    acc_in, acc_out, gate_row,
+):
+    step = pl.program_id(0)
+    width, slab = routed.shape[3], 2 * SIDE
+    experts = acc_in.shape[0]
+
+    @pl.when(step == 0)
+    def clear():
+        def one(e, carry):
+            acc_in[e] = jnp.zeros(acc_in.shape[1:], jnp.float32)
+            acc_out[e] = jnp.zeros(acc_out.shape[1:], jnp.float32)
+            return carry
+
+        lax.fori_loop(0, experts, one, 0)
+        gate_row[...] = jnp.zeros_like(gate_row)
+
+    first, second = pairs[2 * step], pairs[2 * step + 1]
+    rows, cots = routed[0, 0], cot[0, 0]
+    w_in = jnp.concatenate(
+        [w_in_all[:, :, e].reshape(width, SIDE) for e in (first, second)], axis=1
+    )
+    w_out = jnp.concatenate(
+        [w_out_all[:, e].reshape(SIDE, width) for e in (first, second)], axis=0
+    )
+    route = dense[:, :, 4 * width : 4 * width + SIDE].reshape(width, SIDE)
+    gate_a, gate_b = two_gates(dot(rows, route), first, second)
+    lane = lax.broadcasted_iota(jnp.int32, (1, slab), 1)
+    gates = jnp.where(lane < SIDE, gate_a, gate_b)
+    hidden = dot(rows, w_in)
+    back_act = contract_cols(cots, w_out)
+    square = hidden * hidden
+    bend = jnp.tanh(ROOT2PI * hidden * (1.0 + 0.044715 * square))
+    half = 0.5 * (1.0 + bend)
+    act = (hidden * half).astype(jnp.bfloat16).astype(jnp.float32)
+    slope = half + 0.5 * hidden * (1.0 - bend * bend) * (ROOT2PI * (1.0 + 0.134145 * square))
+    gated = (gates * act).astype(jnp.bfloat16)
+    grad_pre = (gates * back_act * slope).astype(jnp.bfloat16)
+    product = (act * back_act).astype(jnp.bfloat16)
+    sign = jnp.where(lane < SIDE, 1.0, -1.0)
+    signs = jnp.broadcast_to(sign, (8, slab)).astype(jnp.bfloat16)
+    gate_row[:, :ROWS] = contract_cols(signs, product)
+    mixed[0, 0] = dot(gated, w_out).astype(jnp.bfloat16)
+    grads = contract_cols(grad_pre, w_in)
+    grad[0, 0] = jnp.concatenate([grads[:PACK], gate_row[...]], axis=0).astype(jnp.bfloat16)
+    new_in = contract_rows(rows, grad_pre)
+    acc_in[first] += new_in[:, :SIDE]
+    acc_in[second] += new_in[:, SIDE:]
+    new_out = contract_rows(gated, cots)
+    acc_out[first] += new_out[:SIDE]
+    acc_out[second] += new_out[SIDE:]
+
+    @pl.when(step == pl.num_programs(0) - 1)
+    def emit():
+        own = pl.multiple_of(core[0] * HEAD, HEAD)
+        far = pl.multiple_of((1 - core[0]) * HEAD, HEAD)
+
+        def one(e, carry):
+            total = acc_in[e].astype(jnp.bfloat16).reshape(16, 2, 16, SIDE)
+            d_in[0, :, e] = total[:, 0]
+            d_in[1, :, e] = total[:, 1]
+            d_out_own[e] = acc_out[e, pl.ds(own, HEAD)]
+            d_out_far[e] = acc_out[e, pl.ds(far, HEAD)].astype(jnp.bfloat16)
+            return carry
+
+        lax.fori_loop(0, experts, one, 0)
+
+
+class Collect:
+    def __init__(self, place, part, corner, from_x, from_y, from_z, packs, half, sems):
+        self.place, self.part = place, part
+        self.corner, self.from_x, self.from_y, self.from_z = corner, from_x, from_y, from_z
+        self.packs, self.half, self.started = packs, half, []
+        self.send_sem, self.recv_sem = sems
+
+    def go(self, kind, src, dst, at_send, at_recv, device):
+        send(
+            self.started, src, dst, self.send_sem.at[kind, at_send],
+            self.recv_sem.at[kind, at_recv], device,
+        )
+
+    def opposite(self, k, p):
+        at = k * self.packs + p
+        towards = 2 if self.half(k, p) == 0 else 1
+        self.go(3, self.part(3, k, p), self.corner.at[at], at, at, self.place.device(towards, 0))
+
+    def straight(self, k, p):
+        at = k * self.packs + p
+        if self.half(k, p) == 0:
+            self.go(2, self.part(2, k, p), self.from_y.at[at], at, at, self.place.device(2, 0))
+        else:
+            self.go(1, self.part(1, k, p), self.from_x.at[at], at, at, self.place.device(1, 0))
+
+    def helped(self, k, p, mine):
+        at = k * self.packs + p
+        ref = self.corner.at[at]
+        arrived(ref, self.recv_sem.at[3, at])
+        total = ref[...].astype(jnp.float32) + mine().astype(jnp.float32)
+        ref[...] = total.astype(jnp.bfloat16)
+        if self.half(k, p) == 0:
+            self.go(1, ref, self.from_x.at[at], at, at, self.place.device(1, 0))
+        else:
+            self.go(2, ref, self.from_y.at[at], at, at, self.place.device(2, 0))
+
+    def plane(self, k, p, mine):
+        at = k * self.packs + p
+        arrived(self.from_x.at[at], self.recv_sem.at[1, at])
+        arrived(self.from_y.at[at], self.recv_sem.at[2, at])
+        total = self.from_x[at].astype(jnp.float32) + self.from_y[at].astype(jnp.float32)
+        total = total + mine().astype(jnp.float32)
+        if k:
+            self.from_x[at] = total.astype(jnp.bfloat16)
+            there = back(k) * self.packs + p
+            self.go(
+                0, self.from_x.at[at], self.from_z.at[there], at, there, self.place.device(0, k)
+            )
+            return None
+        for other in (1, 2, 3):
+            at = other * self.packs + p
+            arrived(self.from_z.at[at], self.recv_sem.at[0, at])
+            total = total + self.from_z[at].astype(jnp.float32)
+        return total
+
+    def finish(self):
+        for copy in self.started:
+            copy.wait_send()
+
+
+def tail_kernel(
+    pairs, tok, cot, seg_col, seg_row, proj, heads, middle, dense, grad_part, mixed_part, d_in,
+    d_out_far,
+    mixed, d_tok, d_dense, d_in_all, d_out_all,
+    g_own, g_corner, g_x, g_y, g_z, m_own, m_corner, m_x, m_y, m_z,
+    total_grad, grad_mid, grad_heads, grad_qkv, acc, small_rows, turned,
+    in_far, in_mine, far_dense, got_dense, part_dense, s_corner, s_x, s_y, s_z,
+    g_send, g_recv, m_send, m_recv, s_send, s_recv, in_send, in_recv,
+    pair_send, pair_recv, load_sem,
+):
+    place = Place()
+    width = tok.shape[2]
+    place.greet()
+
+    def by_pack(k, p):
+        return p
+
+    def part_of(ref):
+        return lambda rel, k, p: ref.at[rel, k * 2 + p]
+
+    grads = Collect(
+        place, part_of(grad_part), g_corner, g_x, g_y, g_z, 2, by_pack, (g_send, g_recv)
+    )
+    mixes = Collect(
+        place, part_of(mixed_part), m_corner, m_x, m_y, m_z, 2, by_pack, (m_send, m_recv)
+    )
+    order = [(k, p) for k in (2, 1, 3, 0) for p in range(2)]
+    for k, p in order:
+        grads.opposite(k, p)
+    for k, p in order:
+        grads.straight(k, p)
+
+    loads = []
+
+    def load(src, dst):
+        copy = pltpu.make_async_copy(src, dst, load_sem.at[len(loads)])
+        copy.start()
+        loads.append(copy)
+        return copy
+
+    def load_parts(ref, own):
+        waits = {}
+        for k, p in order:
+            at = k * 2 + p
+            waits["helped", k, p] = load(ref.at[1 + p, at], own.at[1, at])
+        for k, p in order:
+            at = k * 2 + p
+            waits["plane", k, p] = load(ref.at[0, at], own.at[0, at])
+        return waits
+
+    g_waits = load_parts(grad_part, g_own)
+    pair_started = []
+    send(
+        pair_started, d_in.at[1 - place.core], in_far, pair_send.at[0], pair_recv.at[0],
+        place.sibling,
+    )
+    send(
+        pair_started, d_out_far, d_out_all, pair_send.at[1], pair_recv.at[1], place.sibling
+    )
+    in_load = load(d_in.at[place.core], in_mine)
+    m_waits = load_parts(mixed_part, m_own)
+
+    def mine(waits, own, kind, k, p):
+        def get():
+            waits[kind, k, p].wait()
+            return own[0 if kind == "plane" else 1, k * 2 + p]
+
+        return get
+
+    in_load.wait()
+    arrived(in_far, pair_recv.at[0])
+
+    def add_pair(i, carry):
+        total = in_mine[i].astype(jnp.float32) + in_far[i].astype(jnp.float32)
+        in_mine[i] = total.astype(jnp.bfloat16)
+        return carry
+
+    lax.fori_loop(0, in_mine.shape[0], add_pair, 0)
+
+    for k, p in order:
+        grads.helped(k, p, mine(g_waits, g_own, "helped", k, p))
+    for k, p in order:
+        mixes.opposite(k, p)
+    for k, p in order:
+        mixes.straight(k, p)
+    for k, p in order:
+        if k:
+            grads.plane(k, p, mine(g_waits, g_own, "plane", k, p))
+    in_started = []
+    columns = pl.ds(pl.multiple_of(place.chip(0, 0) * SIDE, SIDE), SIDE)
+    for rel in (3, 1, 2, 0):
+        for k in (2, 1, 3, 0):
+            src = in_mine.at[place.chip(rel, k)]
+            dst = d_in_all.at[:, :, columns]
+            if (rel, k) == (0, 0):
+                in_local = load(src, dst)
+            else:
+                send(
+                    in_started, src, dst, in_send.at[rel, k], in_recv.at[rel, back(k)],
+                    place.device(rel, k),
+                )
+    for p in range(2):
+        total_grad[p] = grads.plane(0, p, mine(g_waits, g_own, "plane", 0, p))
+
+    small = dense[:, :, 4 * width : 4 * width + SIDE].reshape(width, SIDE)
+    turned[...] = jnp.transpose(small.astype(jnp.float32))
+    small_rows[...] = jnp.zeros_like(small_rows)
+    gain_one, bias_one = turned[GAIN_ONE : GAIN_ONE + 1, :], turned[GAIN_ONE + 1 : GAIN_ONE + 2, :]
+    gain_two, bias_two = turned[GAIN_ONE + 2 : GAIN_ONE + 3, :], turned[GAIN_ONE + 3 : GAIN_ONE + 4, :]
+
+    def add_to(p, columns, value):
+        if p == 0:
+            acc[:, columns] = value
+        else:
+            acc[:, columns] += value
+
+    def add_row(at, value):
+        small_rows[at : at + 1, :] += jnp.sum(value, 0, keepdims=True)
+
+    for p in range(2):
+        first, second = pairs[2 * p], pairs[2 * p + 1]
+        got = total_grad[p]
+        tall = jnp.concatenate(
+            [got[PACK:, : 2 * SIDE], jnp.zeros((SIDE - 8, 2 * SIDE), jnp.float32)], axis=0
+        )
+        gap_grad = jnp.transpose(tall)[:ROWS, 0:1]
+        got = jnp.where(real_rows(), got, 0.0)
+        mid = middle[p]
+        unit, rise = norm_parts(mid)
+        routed = jnp.where(real_rows(), unit * gain_two + bias_two, 0.0).astype(jnp.bfloat16)
+        route = dense[:, :, 4 * width : 4 * width + SIDE].reshape(width, SIDE)
+        gate_a, gate_b = two_gates(dot(routed, route), first, second)
+        grad_a = gate_a * gate_b * gap_grad
+        lane = lax.broadcasted_iota(jnp.int32, (ROWS, SIDE), 1)
+        grad_logits = jnp.where(lane == first, grad_a, jnp.where(lane == second, -grad_a, 0.0))
+        grad_logits = jnp.where(real_rows(), grad_logits, 0.0).astype(jnp.bfloat16)
+        add_to(p, pl.ds(4 * width, SIDE), contract_rows(routed, grad_logits))
+        got = got + contract_cols(grad_logits, route)
+        add_row(2, got * unit)
+        add_row(3, got)
+        u = got * gain_two
+        grad_middle = cot[p].astype(jnp.float32) + rise * (
+            u - jnp.mean(u, -1, keepdims=True) - unit * jnp.mean(u * unit, -1, keepdims=True)
+        )
+        grad_mid[...] = grad_middle
+        attended = grad_middle.astype(jnp.bfloat16)
+        add_to(p, pl.ds(3 * width, width), contract_rows(heads[p], attended))
+        w_attn = dense[:, :, 3 * width : 4 * width].reshape(width, width)
+        grad_heads[...] = contract_cols(attended, w_attn).astype(jnp.bfloat16)
+        same = seg_col[p] == seg_row[p]
+
+        def pair_of_heads(j, carry, p=p, same=same):
+            at = pl.multiple_of(j * SIDE, SIDE)
+            queries = proj[p, :, pl.ds(at, SIDE)]
+            keys = proj[p, :, pl.ds(at + width, SIDE)]
+            values = proj[p, :, pl.ds(at + 2 * width, SIDE)]
+            out_grad = grad_heads[:, pl.ds(at, SIDE)]
+            zero = jnp.zeros((ROWS, SIDE), jnp.float32)
+            grad_q, grad_k, grad_v = zero, zero, zero
+            for h in range(2):
+                lanes = head_lanes(h)
+                probs = softmax_rows(queries * lanes, keys, same)
+                mine_grad = out_grad * lanes
+                grad_v = grad_v + contract_rows(probs.astype(jnp.bfloat16), mine_grad)
+                grad_probs = contract_cols(mine_grad, values)
+                row_dot = jnp.sum(probs * grad_probs, -1, keepdims=True)
+                grad_scores = (probs * (grad_probs - row_dot)).astype(jnp.bfloat16)
+                grad_q = grad_q + dot(grad_scores, keys * lanes)
+                grad_k = grad_k + contract_rows(grad_scores, queries * lanes)
+            scale = 1.0 / math.sqrt(HEAD)
+            grad_qkv[:, pl.ds(at, SIDE)] = (grad_q * scale).astype(jnp.bfloat16)
+            grad_qkv[:, pl.ds(at + width, SIDE)] = (grad_k * scale).astype(jnp.bfloat16)
+            grad_qkv[:, pl.ds(at + 2 * width, SIDE)] = grad_v.astype(jnp.bfloat16)
+            return carry
+
+        lax.fori_loop(0, width // SIDE, pair_of_heads, 0)
+        for k, q in order[4 * p : 4 * p + 4]:
+            mixes.helped(k, q, mine(m_waits, m_own, "helped", k, q))
+        unit, rise = norm_parts(tok[p].astype(jnp.float32))
+        normed = (unit * gain_one + bias_one).astype(jnp.bfloat16)
+        add_to(p, pl.ds(0, 3 * width), contract_rows(normed, grad_qkv[...]))
+        w_qkv = dense[:, :, : 3 * width].reshape(width, 3 * width)
+        grad_normed = contract_cols(grad_qkv[...], w_qkv)
+        add_row(0, grad_normed * unit)
+        add_row(1, grad_normed)
+        u = grad_normed * gain_one
+        d_tok[p] = (
+            grad_mid[...]
+            + rise
+            * (u - jnp.mean(u, -1, keepdims=True) - unit * jnp.mean(u * unit, -1, keepdims=True))
+        ).astype(jnp.bfloat16)
+
+    tall = jnp.concatenate(
+        [
+            jnp.zeros((GAIN_ONE, width), jnp.float32),
+            small_rows[...],
+            jnp.zeros((SIDE - GAIN_ONE - 8, width), jnp.float32),
+        ],
+        axis=0,
+    )
+    acc[:, 4 * width :] += jnp.transpose(tall)
+    columns_all = acc.shape[1]
+
+    def cut(i, carry):
+        own_rows = pl.ds(pl.multiple_of(i * 32 + place.core * 16, 16), 16)
+        far_rows = pl.ds(pl.multiple_of(i * 32 + 16 - place.core * 16, 16), 16)
+        far_dense[i] = acc[far_rows, :].astype(jnp.bfloat16)
+        part_dense[i] = acc[own_rows, :]
+        return carry
+
+    lax.fori_loop(0, 16, cut, 0)
+    send(
+        pair_started, far_dense, got_dense, pair_send.at[2], pair_recv.at[2], place.sibling
+    )
+    arrived(got_dense, pair_recv.at[2])
+
+    def join(i, carry):
+        far_dense_sum = part_dense[i] + got_dense[i].astype(jnp.float32)
+        got_dense[i] = far_dense_sum.astype(jnp.bfloat16)
+        return carry
+
+    lax.fori_loop(0, 16, join, 0)
+
+    def dense_part(rel, k, p):
+        return got_dense.at[place.chip(rel, k)]
+
+    sums = Collect(
+        place, dense_part, s_corner, s_x, s_y, s_z, 1, lambda k, p: k % 2, (s_send, s_recv)
+    )
+    for k in (2, 1, 3, 0):
+        sums.opposite(k, 0)
+    for k in (2, 1, 3, 0):
+        sums.straight(k, 0)
+    for k in (2, 1, 3, 0):
+        sums.helped(k, 0, lambda k=k: got_dense[place.chip(1 + k % 2, k)])
+    for k in (2, 1, 3):
+        sums.plane(k, 0, lambda k=k: got_dense[place.chip(0, k)])
+    d_dense[...] = sums.plane(0, 0, lambda: got_dense[place.chip(0, 0)])
+
+    for k, p in order:
+        if k:
+            mixes.plane(k, p, mine(m_waits, m_own, "plane", k, p))
+    for p in range(2):
+        summed = mixes.plane(0, p, mine(m_waits, m_own, "plane", 0, p))
+        mixed[p] = (middle[p] + summed).astype(jnp.bfloat16)
+
+    for rel in range(4):
+        for k in range(4):
+            if (rel, k) != (0, 0):
+                place_columns = pl.ds(pl.multiple_of(place.chip(rel, k) * SIDE, SIDE), SIDE)
+                arrived(d_in_all.at[:, :, place_columns], in_recv.at[rel, k])
+    in_local.wait()
+    arrived(d_out_all, pair_recv.at[1])
+    for tree in (grads, mixes, sums):
+        tree.finish()
+    for copy in pair_started + in_started:
+        copy.wait_send()
+
+
+def shards_fast(
+    tokens,
+    segment_ids,
+    pack_task,
+    task_experts,
+    w_qkv,
+    w_attn_out,
+    w_router,
+    w_expert_in,
+    w_expert_out,
+    norm1_gain,
+    norm1_bias,
+    norm2_gain,
+    norm2_bias,
+    cotangent,
+):
+    packs, length, width = tokens.shape
+    experts, slab_in, hidden = w_expert_in.shape
+    slab_out = w_expert_out.shape[1]
+    dense_width = 4 * width + SIDE
+    any_space = pl.BlockSpec(memory_space=pl.ANY)
+    vmem = pl.BlockSpec(memory_space=pltpu.VMEM)
+    smem = pl.BlockSpec(memory_space=pltpu.SMEM)
+    low = jnp.bfloat16
+    flat = jax.ShapeDtypeStruct
+    dma = pltpu.SemaphoreType.DMA
+
+    def tall(array, fill=0):
+        return jnp.pad(
+            array,
+            ((0, 0), (0, ROWS - length)) + ((0, 0),) * (array.ndim - 2),
+            constant_values=fill,
+        )
+
+    tok, cot = tall(tokens), tall(cotangent)
+    segments = tall(segment_ids, -1)
+    seg_col, seg_row = segments[:, :, None], segments[:, None, :]
+    norms = jnp.stack([norm1_gain, norm1_bias, norm2_gain, norm2_bias], axis=1)
+    small = jnp.concatenate([w_router, norms], axis=1)
+    small = jnp.pad(small, ((0, 0), (0, SIDE - small.shape[1])))
+    own_dense = jnp.concatenate([w_qkv, w_attn_out, small], axis=1)
+
+    pack_pairs = task_experts[pack_task]
+    z, g = lax.axis_index("gx"), lax.axis_index("gy")
+    core = g % 2
+    slot_devices = []
+    for rel in range(4):
+        at = g + (2 - 4 * ((g // 2) % 2)) * (rel % 2) + (4 - 8 * (g // 4)) * (rel // 2)
+        for k in range(4):
+            slot_devices.append(((z + k) % 4) * 8 + at)
+    slots = jnp.stack(slot_devices)
+    slot_pairs = pack_pairs.reshape(32, packs * 2)[slots].reshape(-1)
+
+    blocks = flat((4, 4 * packs, ROWS, width), low)
+    (
+        routed_all, cot_all, w_in_all, w_out_all, dense, proj, heads, middle,
+    ) = pl.pallas_call(
+        front_kernel,
+        out_shape=(
+            blocks,
+            blocks,
+            flat((16, 2, experts, slab_in, SIDE), low),
+            flat((2, experts, slab_out, width), low),
+            flat((32, slab_in, dense_width), low),
+            flat((packs, ROWS, 3 * width), low),
+            flat((packs, ROWS, width), low),
+            flat((packs, ROWS, width), jnp.float32),
+        ),
+        in_specs=[vmem] * 4 + [any_space] * 3,
+        out_specs=(any_space,) * 5 + (vmem,) * 3,
+        scratch_shapes=[
+            pltpu.VMEM((32, slab_in, dense_width), low),
+            pltpu.VMEM((packs, ROWS, width), low),
+            pltpu.VMEM((SIDE, width), jnp.float32),
+            dma((4, 8)), dma((4, 8)), dma((4, 8)), dma((4, 8)), dma((4, 4)), dma((4, 4)),
+            dma((4, 4)), dma((4, 4)), dma((4, 4)), dma((4, 4)), dma((2,)), dma((2,)), dma((8,)),
+        ],
+        compiler_params=pltpu.CompilerParams(
+            collective_id=0, has_side_effects=True, vmem_limit_bytes=40 << 20
+        ),
+        name="front",
+    )(tok, seg_col, seg_row, own_dense, cot, w_expert_in, w_expert_out)
+
+    steps = 4 * 4 * packs
+    one_block = pl.BlockSpec(
+        (1, 1, ROWS, width), lambda i, *unused: (i // (4 * packs), i % (4 * packs), 0, 0)
+    )
+    mixed_part, grad_part, d_in, d_out_own, d_out_far = pl.pallas_call(
+        expert_kernel,
+        grid_spec=pltpu.PrefetchScalarGridSpec(
+            num_scalar_prefetch=2,
+            grid=(steps,),
+            in_specs=[one_block, one_block, vmem, vmem, vmem],
+            out_specs=[one_block, one_block, vmem, vmem, vmem],
+            scratch_shapes=[
+                pltpu.VMEM((experts, width, SIDE), jnp.float32),
+                pltpu.VMEM((experts, SIDE, width), jnp.float32),
+                pltpu.VMEM((8, width), jnp.float32),
+            ],
+        ),
+        out_shape=(
+            blocks,
+            blocks,
+            flat((2, 16, experts, slab_in, SIDE), low),
+            flat((experts, slab_out, width), jnp.float32),
+            flat((experts, slab_out, width), low),
+        ),
+        compiler_params=pltpu.CompilerParams(vmem_limit_bytes=56 << 20),
+        name="experts",
+    )(slot_pairs, core[None], routed_all, cot_all, w_in_all, w_out_all, dense)
+
+    parts = pltpu.VMEM((4 * packs, ROWS, width), low)
+    slices = pltpu.VMEM((4, slab_in, dense_width), low)
+    sliced = pltpu.VMEM((16, slab_in, dense_width), low)
+    mixed, d_tok, d_dense, d_in_all, d_out_all = pl.pallas_call(
+        tail_kernel,
+        out_shape=(
+            flat((packs, ROWS, width), low),
+            flat((packs, ROWS, width), low),
+            flat((slab_in, dense_width), jnp.float32),
+            flat((experts, slab_in, hidden), low),
+            flat((experts, slab_out, width), low),
+        ),
+        in_specs=[smem] + [vmem] * 8 + [any_space] * 4,
+        out_specs=(vmem,) * 3 + (any_space,) * 2,
+        scratch_shapes=[
+            pltpu.VMEM((2, 4 * packs, ROWS, width), low), parts, parts, parts, parts,
+            pltpu.VMEM((2, 4 * packs, ROWS, width), low), parts, parts, parts, parts,
+            pltpu.VMEM((packs, ROWS, width), jnp.float32),
+            pltpu.VMEM((ROWS, width), jnp.float32),
+            pltpu.VMEM((ROWS, width), low),
+            pltpu.VMEM((ROWS, 3 * width), low),
+            pltpu.VMEM((width, dense_width), jnp.float32),
+            pltpu.VMEM((8, width), jnp.float32),
+            pltpu.VMEM((SIDE, width), jnp.float32),
+            pltpu.VMEM((16, experts, slab_in, SIDE), low),
+            pltpu.VMEM((16, experts, slab_in, SIDE), low),
+            sliced, sliced,
+            pltpu.VMEM((16, slab_in, dense_width), jnp.float32),
+            slices, slices, slices, slices,
+            dma((4, 8)), dma((4, 8)), dma((4, 8)), dma((4, 8)), dma((4, 4)), dma((4, 4)),
+            dma((4, 4)), dma((4, 4)), dma((3,)), dma((3,)), dma((40,)),
+        ],
+        compiler_params=pltpu.CompilerParams(
+            collective_id=1, has_side_effects=True, vmem_limit_bytes=60 << 20
+        ),
+        name="tail",
+    )(
+        slot_pairs[: 2 * packs], tok, cot, seg_col, seg_row, proj, heads, middle, dense,
+        grad_part, mixed_part, d_in, d_out_far,
+    )
+    norm_at = 4 * width + GAIN_ONE
+    return (
+        mixed[:, :length],
+        d_tok[:, :length],
+        d_dense[:, : 3 * width],
+        d_dense[:, 3 * width : 4 * width],
+        d_dense[:, 4 * width : 4 * width + experts],
+        d_in_all.astype(jnp.float32),
+        d_out_own + d_out_all.astype(jnp.float32),
+        d_dense[:, norm_at],
+        d_dense[:, norm_at + 1],
+        d_dense[:, norm_at + 2],
+        d_dense[:, norm_at + 3],
+    )
+
+
 def solution(mesh):
+    outer, inner = mesh.shape["gx"], mesh.shape["gy"]
+
+    def shards(*arrays):
+        packs, length, width = arrays[0].shape
+        experts, slab_in, hidden = arrays[7].shape
+        fits = (
+            (outer, inner) == (4, 8)
+            and packs == 2
+            and length == PACK
+            and experts == GAIN_ONE
+            and width == HEADS * HEAD
+            and slab_in == 16
+            and hidden == 16 * SIDE
+        )
+        return (shards_fast if fits else shards_any)(*arrays)
+
     placed = (
         P(("gx", "gy"), None, None),
         P(("gx", "gy"), None),

time: 2350 us -> 468 us (0.20)
  waiting for transfers between devices: 1590 us -> 0 us
  Pallas kernels: 0 us -> 433 us
  blocking collectives: 245 us -> 0 us
  local copies, waits for them, and re-layouts: 233 us -> 22.1 us
  starting transfers between devices: 136 us -> 0 us
  matrix products: 91 us -> 0 us
  other arithmetic: 34.1 us -> 10.1 us
    all_to_all x20 -> x0, waiting for transfers between devices: 1370 us -> none  [the longest x2 333 us: shards(): lax.all_to_all(shortened((slot_in.reshape(amount, outer, inner, slab_in,...]
    pallas_call x0 -> x3, Pallas kernels: none -> 433 us  [the longest x1 201 us: shards_fast(): pl.pallas_call(tail_kernel, out_shape=(flat((packs, ROWS, width), low), f...]
    reduce_scatter x3 -> x0, waiting for transfers between devices: 220 us -> none  [the longest x1 122 us: shards(): lax.psum_scatter(dense_acc[0], ('gx', 'gy'), scatter_dimension=0, tiled=T...]
    unnamed x2 -> x0, blocking collectives: 167 us -> none
    all_to_all x20 -> x0, starting transfers between devices: 136 us -> none  [the longest x4 36.6 us: forward_step(): lax.all_to_all(shortened(slabs(need)), 'gx', split_axis=1, concat_axis=1,...]
    dot_general x46 -> x0, matrix products: 91 us -> none  [the longest x2 17.4 us: shards(): jnp.einsum('esab,sabrc->erc', onehot, piece, precision=HIGH)]
    all_to_all x18 -> x0, local copies, waits for them, and re-layouts: 81.1 us -> none  [the longest x2 21.7 us: shards(): lax.all_to_all(shortened((slot_in.reshape(amount, outer, inner, slab_in,...]
    all_gather x2 -> x0, blocking collectives: 78.1 us -> none  [the longest x1 41.1 us: shards(): lax.all_gather(w_attn_out, ('gx', 'gy'), axis=0, tiled=True)]
  transfers between devices with their start and end apart: 24 -> 0, of which waited for: 21 -> 0; matrix products, arithmetic and copies ran while one was open for 10% -> 0% of each run, Pallas kernels for 0% -> 0%
where the time goes in v1:
time: 468 us; the launch traced here: 467 us
  Pallas kernels  433 us (93%)
  local copies, waits for them, and re-layouts  22.1 us (5%)
  other arithmetic  10.1 us (2%)
    pallas_call x1, Pallas kernels, shards_fast(): pl.pallas_call(tail_kernel, out_shape=(flat((packs, ROWS, width), low), f...  201 us
    pallas_call x1, Pallas kernels, shards_fast(): pl.pallas_call(front_kernel, out_shape=(blocks, blocks, flat((16, 2, expe...  187 us
    pallas_call x1, Pallas kernels, shards_fast(): pl.pallas_call(expert_kernel, grid_spec=pltpu.PrefetchScalarGridSpec(num_...  45.5 us

profile of v1, /device:TPU:8, one launch (start us, length us, event | category | flops | bytes accessed | tf_op | source)
XLA Modules:
  0.0 466.6 jit_solution(13733749342026975907)
XLA Ops:
  0.9 0.8 compare_select_fusion.1
  1.7 0.7 copy.33
  2.4 0.7 copy.34
  3.2 0.7 copy.35
  3.9 0.7 copy.36
  4.7 0.8 concatenate.25
  6.1 0.8 copy.32
  9.2 0.8 fusion.1.own_dense
  10.2 1.1 pad.15.tok
  11.4 1.2 pad.16.cot
  12.6 1.6 copy-done.5
  14.2 186.6 %front.1 = (bf16[4,8,224,512]{3,2,1,0:T(8,128)(2,1)}, bf16[4,8,224,512]{3,2,1,0:T(8,128)(2,1)}, bf16[16,2,32,16,128]{4,3,2,1,0:T(8,128)(2,1)S(1)}, bf16[2,32,64,...) custom-call(bf16[2,224,512]{2,1,0:T(8,128)(2,1)S(1)} %pad.15.tok, ...), custom_call_target="tpu_custom_call" | custom-call | tf_op jit(solution)/shard_map/front/pallas_call | solution.py:1111
  200.8 1.3 copy-done
  202.1 2.0 copy-done.1
  204.2 1.1 copy-done.7
  205.2 1.0 copy-done.8
  206.2 0.8 copy-done.9
  207.0 45.5 %experts.1 = (bf16[4,8,224,512]{3,2,1,0:T(8,128)(2,1)}, bf16[4,8,224,512]{3,2,1,0:T(8,128)(2,1)}, bf16[2,16,32,16,128]{4,3,2,1,0:T(8,128)(2,1)}, f32[32,64,512]{2,1,0:T(8,128)}, bf16[32,64,512]{2,1,0:T(8,128)(2,1)}) custom-call(s32[64]{0:T(128)} %reshape.647.pairs, s32[1]{0:T(128)} %bitcast.23.core, bf16[4,8,224,512]{3,2,1,0:T(8,128)(2,1)} %get-tuple-element.33.routed, ...), custom_call_target="tpu_custom_call" | custom-call | tf_op jit(solution)/shard_map/experts/pallas_call | solution.py:1142
  252.5 201.3 %tail.1 = (bf16[2,224,512]{2,1,0:T(8,128)(2,1)}, bf16[2,224,512]{2,1,0:T(8,128)(2,1)}, f32[16,2176]{1,0:T(8,128)}, bf16[32,16,2048]{2,1,0:T(8,128)(2,1)}, bf16[32,64,512]{2,1,0:T(8,128)(2,1)}) custom-call(s32[4]{0:T(128)} %slice_bitcast_fusion.pairs, bf16[2,224,512]{2,1,0:T(8,128)(2,1)} %copy-done.2, bf16[2,224,512]{2,1,0:T(8,128)(2,1)} %copy-done.3, ...), custom_call_target="tpu_custom_call" | custom-call | tf_op jit(solution)/shard_map/tail/pallas_call | solution.py:1169
  453.9 6.0 %convert_add_fusion = f32[32,64,512]{2,1,0:T(8,128)} fusion(f32[32,64,512]{2,1,0:T(8,128)} %get-tuple-element.45, bf16[32,64,512]{2,1,0:T(8,128)(2,1)} %get-tuple-element.46), kind=kLoop, calls=%fused_computation.2 | loop fusion | flops 2097152 | bytes 10485760 | tf_op jit(solution)/shard_map/add | solution.py:1214
  459.9 0.8 slice.35
  460.7 0.7 slice_reduce_fusion
  463.3 0.8 slice.36
  464.1 2.5 convert_element_type.11
  (39 shorter events, 5.2 us)
Async XLA Ops:
  0.6 11.9 %copy-start.4 = (bf16[32,16,2048]{2,1,0:T(8,128)(2,1)S(1)}, bf16[32,16,2048]{2,1,0:T(8,128)(2,1)}, u32[]{:S(2)}) copy-start(bf16[32,16,2048]{2,1,0:T(8,128)(2,1)} %w_in.1) | copy-start | bytes 6291460
  6.1 246.4 %copy-start.10 = (s32[2,1,224]{2,1,0:T(1,128)}, s32[2,1,224]{2,1,0:T(1,128)S(1)}, u32[]{:S(2)}) copy-start(s32[2,1,224]{2,1,0:T(1,128)S(1)} %broadcast_in_dim.15.seg_row) | copy-start | bytes 5380
  10.2 242.3 %copy-start.6 = (s32[2,224,1]{2,1,0:T(8,128)}, s32[2,224,1]{2,1,0:T(8,128)S(1)}, u32[]{:S(2)}) copy-start(s32[2,224,1]{2,1,0:T(8,128)S(1)} %copy.38.seg_col) | copy-start | bytes 5380
  11.3 241.2 %copy-start.2 = (bf16[2,224,512]{2,1,0:T(8,128)(2,1)}, bf16[2,224,512]{2,1,0:T(8,128)(2,1)S(1)}, u32[]{:S(2)}) copy-start(bf16[2,224,512]{2,1,0:T(8,128)(2,1)S(1)} %pad.15.tok) | copy-start | bytes 1376260
  12.6 1.6 copy-start.5
  14.2 238.3 %copy-start.3 = (bf16[2,224,512]{2,1,0:T(8,128)(2,1)}, bf16[2,224,512]{2,1,0:T(8,128)(2,1)S(1)}, u32[]{:S(2)}) copy-start(bf16[2,224,512]{2,1,0:T(8,128)(2,1)S(1)} %pad.16.cot) | copy-start | bytes 1376260
  200.8 1.4 copy-start
  202.1 2.0 copy-start.1
  204.2 1.1 copy-start.7
  205.2 1.0 copy-start.8
  206.2 0.8 copy-start.9
  453.9 6.0 %copy-start.13 = (bf16[2,224,512]{2,1,0:T(8,128)(2,1)S(1)}, bf16[2,224,512]{2,1,0:T(8,128)(2,1)}, u32[]{:S(2)}) copy-start(bf16[2,224,512]{2,1,0:T(8,128)(2,1)} %get-tuple-element.41) | copy-start | bytes 1376260
  453.9 6.8 %copy-start.14 = (f32[16,2176]{1,0:T(8,128)S(1)}, f32[16,2176]{1,0:T(8,128)}, u32[]{:S(2)}) copy-start(f32[16,2176]{1,0:T(8,128)} %get-tuple-element.43) | copy-start | bytes 417796
  453.9 9.4 %copy-start.12 = (bf16[2,224,512]{2,1,0:T(8,128)(2,1)S(1)}, bf16[2,224,512]{2,1,0:T(8,128)(2,1)}, u32[]{:S(2)}) copy-start(bf16[2,224,512]{2,1,0:T(8,128)(2,1)} %get-tuple-element.42) | copy-start | bytes 1376260
  453.9 10.2 %copy-start.11 = (bf16[32,16,2048]{2,1,0:T(8,128)(2,1)S(1)}, bf16[32,16,2048]{2,1,0:T(8,128)(2,1)}, u32[]{:S(2)}) copy-start(bf16[32,16,2048]{2,1,0:T(8,128)(2,1)} %get-tuple-element.44) | copy-start | bytes 6291460

commit v2 on v1

--- a/solution.py
+++ b/solution.py
@@ -358,6 +358,39 @@
 ROOT2PI = math.sqrt(2.0 / math.pi)
 
 
+(
+    DOWN, DPLANE, DCORNER, DLAST, DWAIT, ATT, WIN, WO, WINWAIT, WSIBWAIT, WAVE, COWN,
+    CPLANE, CCORNER, RPLANE, RCORNER, GFIRST, MFIRST, GHELP, MHELP, GPLANE, MPLANE, PAIR, ADDPAIR, DENSE,
+) = range(25)
+
+FRONT_STEPS = (
+    (WIN, 2, 1), (COWN, 0), (DOWN,), (WO,), (WIN, 2, 0), (WIN, 3, 1), (COWN, 1), (DPLANE, 2), (WIN, 3, 2),
+    (DPLANE, 3), (WIN, 1, 3), (DCORNER, 2), (DCORNER, 0), (DPLANE, 1), (CPLANE, 1, 1), (WIN, 2, 2),
+    (WIN, 1, 2), (DLAST, 2), (DCORNER, 1), (CPLANE, 1, 0), (DCORNER, 3), (WIN, 1, 1), (CPLANE, 2, 1),
+    (CCORNER, 1, 0), (DLAST, 1), (DLAST, 3), (CPLANE, 2, 0), (DLAST, 0), (CPLANE, 3, 1), (WIN, 0, 1),
+    (DWAIT,), (ATT, 0), (WIN, 0, 3), (ATT, 1), (RPLANE, 1, 0), (WIN, 2, 3), (WIN, 1, 0), (WIN, 0, 2),
+    (CCORNER, 0, 0), (WIN, 3, 3), (WIN, 3, 0), (RPLANE, 1, 1), (RPLANE, 2, 0), (CCORNER, 2, 0),
+    (CCORNER, 2, 1), (WINWAIT,), (CCORNER, 0, 1), (RCORNER, 0, 1), (RCORNER, 1, 0), (WSIBWAIT,),
+    (CCORNER, 1, 1), (RCORNER, 0, 0), (WAVE, 0, 1), (RCORNER, 2, 0), (RCORNER, 1, 1), (CPLANE, 3, 0),
+    (WAVE, 1, 0), (RPLANE, 2, 1), (RPLANE, 3, 0), (CCORNER, 3, 0), (WAVE, 1, 1), (RPLANE, 3, 1), (WAVE, 2, 0),
+    (RCORNER, 3, 0), (RCORNER, 2, 1), (WAVE, 0, 0), (CCORNER, 3, 1), (WAVE, 2, 1), (RCORNER, 3, 1),
+    (WAVE, 3, 0), (WAVE, 3, 1),
+)
+TAIL_STEPS = (
+    (GFIRST, 0, 0), (GFIRST, 0, 1), (GHELP, 0, 0), (PAIR,), (GFIRST, 1, 0), (GHELP, 1, 0), (GFIRST, 2, 1),
+    (ADDPAIR,), (GHELP, 0, 1), (WIN, 0, 2), (GPLANE, 1, 0), (GFIRST, 2, 0), (GPLANE, 0, 0), (GFIRST, 1, 1),
+    (MFIRST, 0, 0), (WIN, 0, 1), (WIN, 2, 0), (MHELP, 0, 0), (GHELP, 2, 0), (WIN, 3, 1), (WIN, 0, 0),
+    (GHELP, 1, 1), (WIN, 1, 1), (GHELP, 2, 1), (GPLANE, 0, 1), (MFIRST, 0, 1), (GFIRST, 3, 0), (WIN, 3, 0),
+    (WIN, 2, 1), (GPLANE, 2, 0), (GPLANE, 1, 1), (GPLANE, 2, 1), (GFIRST, 3, 1), (GHELP, 3, 0), (MHELP, 0, 1),
+    (MFIRST, 1, 0), (WIN, 3, 2), (WIN, 2, 2), (WIN, 1, 2), (GHELP, 3, 1), (MHELP, 1, 0), (MPLANE, 0, 0),
+    (GPLANE, 3, 0), (MFIRST, 1, 1), (GPLANE, 3, 1), (MFIRST, 2, 1), (MFIRST, 2, 0), (ATT, 0), (MHELP, 1, 1),
+    (ATT, 1), (ATT, 2), (ATT, 3), (ATT, 4), (MFIRST, 3, 0), (MHELP, 2, 0), (MPLANE, 1, 0), (MPLANE, 1, 1),
+    (MPLANE, 0, 1), (WIN, 1, 0), (MFIRST, 3, 1), (ATT, 5), (MHELP, 2, 1), (DENSE,), (MPLANE, 2, 0),
+    (MHELP, 3, 0), (MHELP, 3, 1), (WIN, 3, 3), (MPLANE, 2, 1), (WIN, 1, 3), (WIN, 2, 3), (MPLANE, 3, 0),
+    (MPLANE, 3, 1),
+)
+
+
 def dot(left, right):
     return jnp.dot(left, right, preferred_element_type=jnp.float32)
 
@@ -371,11 +404,16 @@
         across_y = g + 4 - 8 * (g // 4)
         across_both = across_x + 4 - 8 * (across_x // 4)
         self.at = (g, across_x, across_y, across_both)
+        self.step_x, self.step_y = across_x - g, across_y - g
         self.sibling = (self.z, g + 1 - 2 * self.core)
 
     def plane(self, k):
         return (self.z + k) % 4
 
+    def nearest(self, j):
+        z = self.z
+        return (0, 1 + 2 * (z // 2), 2 + z - 3 * (z // 2), 3 - z + z // 2)[j]
+
     def device(self, rel, k):
         return (self.plane(k), self.at[rel])
 
@@ -384,6 +422,11 @@
 
     def index(self, rel, k):
         return self.plane(k) * 8 + self.at[rel]
+
+    def pair(self, pack_task, task_experts, rel, k, p):
+        at = self.at[0] + self.step_x * (rel % 2) + self.step_y * (rel // 2)
+        task = pack_task[(self.plane(k) * 8 + at) * 2 + p]
+        return task_experts[task, 0], task_experts[task, 1]
 
     def greet(self):
         barrier = pltpu.get_barrier_semaphore()
@@ -418,52 +461,71 @@
 
 
 class Spread:
-    def __init__(self, place, here, there, packs, half, sems):
+    def __init__(self, place, here, there, packs, half, chained, sems):
         self.place, self.here, self.there = place, here, there
-        self.packs, self.half, self.started = packs, half, []
+        self.packs, self.half, self.chained, self.started = packs, half, chained, []
         self.send_sem, self.recv_sem = sems
 
-    def go(self, kind, k_sem, k_there, rel, k, p, src, rel_there, device):
-        send(
-            self.started,
-            src,
-            self.there(rel_there, k_there, p, rel, k),
-            self.send_sem.at[kind, k_sem * self.packs + p],
-            self.recv_sem.at[kind, k_there * self.packs + p],
-            device,
-        )
+    def go(self, kind, at_send, k_there, rel, k, p, src, rel_there, device, only_if=None):
+        copy = pltpu.make_async_remote_copy(
+            src_ref=src,
+            dst_ref=self.there(rel_there, k_there, p, rel, k),
+            send_sem=self.send_sem.at[kind, at_send * self.packs + p],
+            recv_sem=self.recv_sem.at[kind % 4, k_there * self.packs + p],
+            device_id=device,
+            device_id_type=MESH,
+        )
+        if only_if is None:
+            copy.start()
+        else:
+            pl.when(only_if)(copy.start)
+        self.started.append((copy, only_if))
 
     def wait(self, kind, rel, k, p):
         arrived(self.here(rel, k, p), self.recv_sem.at[kind, k * self.packs + p])
 
-    def own(self, p, src, planes=True):
-        if planes:
+    def own(self, p, src):
+        place = self.place
+        if self.chained:
+            self.go(0, 0, 3, 0, 0, p, src, 0, place.device(0, 1), place.z < 3)
+            self.go(4, 0, 1, 0, 0, p, src, 0, place.device(0, 3), place.z > 0)
+        else:
             for k in (1, 2, 3):
-                self.go(0, k, back(k), 0, 0, p, src, 0, self.place.device(0, k))
-        self.go(1, 0, 0, 0, 0, p, src, 1, self.place.device(1, 0))
-        self.go(2, 0, 0, 0, 0, p, src, 2, self.place.device(2, 0))
-
-    def plane(self, k, p):
-        if k:
-            self.wait(0, 0, k, p)
-            src = self.here(0, k, p)
-            self.go(1, k, k, 0, k, p, src, 1, self.place.device(1, 0))
-            self.go(2, k, k, 0, k, p, src, 2, self.place.device(2, 0))
-
-    def corner(self, k, p):
-        self.wait(1, 1, k, p)
-        self.wait(2, 2, k, p)
-        if self.half(k, p) == 0:
-            self.go(3, k, k, 1, k, p, self.here(1, k, p), 3, self.place.device(2, 0))
-        else:
-            self.go(3, k, k, 2, k, p, self.here(2, k, p), 3, self.place.device(1, 0))
-
-    def last(self, k, p):
+                self.go(0, k, back(k), 0, 0, p, src, 0, place.device(0, k))
+        self.go(1, 0, 0, 0, 0, p, src, 1, place.device(1, 0))
+        self.go(2, 0, 0, 0, 0, p, src, 2, place.device(2, 0))
+
+    def plane(self, j, p):
+        place = self.place
+        k = place.nearest(j)
+        self.wait(0, 0, k, p)
+        src = self.here(0, k, p)
+        if self.chained:
+            step = 2 * ((place.z - place.plane(k) + 3) // 4) - 1
+            goes = (place.z + step >= 0) & (place.z + step <= 3)
+            on = (place.plane(step + 4), place.at[0])
+            self.go(0, k, (k - step + 4) % 4, 0, k, p, src, 0, on, goes)
+        self.go(1, k, k, 0, k, p, src, 1, place.device(1, 0))
+        self.go(2, k, k, 0, k, p, src, 2, place.device(2, 0))
+
+    def corner(self, j, p):
+        k = self.place.nearest(j)
+        rel = 1 + self.half(j, p)
+        self.wait(rel, rel, k, p)
+        self.go(3, k, k, rel, k, p, self.here(rel, k, p), 3, self.place.device(3 - rel, 0))
+
+    def last(self, j, p):
+        k = self.place.nearest(j)
+        rel = 2 - self.half(j, p)
+        self.wait(rel, rel, k, p)
         self.wait(3, 3, k, p)
 
     def finish(self):
-        for copy in self.started:
-            copy.wait_send()
+        for copy, only_if in self.started:
+            if only_if is None:
+                copy.wait_send()
+            else:
+                pl.when(only_if)(copy.wait_send)
 
 
 def norm_parts(values):
@@ -500,32 +562,66 @@
     return 1.0 / (1.0 + jnp.exp(gap)), 1.0 / (1.0 + jnp.exp(-gap))
 
 
+def lengthened(ref, p):
+    rows = ref[p].astype(jnp.float32)
+    return jnp.concatenate([rows, jnp.zeros((ROWS - PACK, rows.shape[1]), jnp.float32)], axis=0)
+
+
+def same_documents(segments, flat_ids, tall_ids):
+    flat_ids[...] = jnp.full(flat_ids.shape, -1.0, jnp.float32)
+    flat_ids[: segments.shape[0], :PACK] = segments[...].astype(jnp.float32)
+    tall_ids[...] = jnp.transpose(flat_ids[...])
+
+
+def same_document(flat_ids, tall_ids, p):
+    return tall_ids[:ROWS, p : p + 1] == flat_ids[p : p + 1, :ROWS]
+
+
 def front_kernel(
-    tok, seg_col, seg_row, own_dense, cot, w_in, w_out,
-    routed_all, cot_all, w_in_all, w_out_all, dense_out, proj, heads, middle,
-    dense, routed, turned,
+    pack_task, task_experts, tok, segments, w_qkv_own, w_attn_own, route_own,
+    gain_one_own, bias_one_own, gain_two_own, bias_two_own, cot_own, w_in, w_out,
+    in_terms, out_terms, mixed_out, grad_out, dense_out, proj, heads, middle,
+    dense, routed_all, cot_all, w_in_all, w_out_all, in_stage, out_stage, mixed_all, grad_all,
+    turned, square, flat_ids, tall_ids, gate_row,
     cot_send, cot_recv, routed_send, routed_recv, dense_send, dense_recv,
-    core_send, core_recv, in_send, in_recv, pair_send, pair_recv, local_sem,
+    core_send, core_recv, in_send, in_recv, pair_send, pair_recv, local_sem, out_sem,
 ):
     place = Place()
-    width = tok.shape[2]
-    place.greet()
+    width, experts = tok.shape[2], route_own.shape[1]
+    other = 1 - place.core
 
     def block_here(ref):
         return lambda rel, k, p: ref.at[rel, k * 2 + p]
 
     def block_there(ref):
         return lambda rel_there, k_there, p, rel, k: ref.at[rel_there, k_there * 2 + p]
+
+    own = place.index(0, 0)
+    dense[own, :, : 3 * width] = w_qkv_own[...]
+    dense[own, :, 3 * width : 4 * width] = w_attn_own[...]
+    square[...] = jnp.zeros_like(square)
+    for i, ref in enumerate((gain_one_own, bias_one_own, gain_two_own, bias_two_own)):
+        square[GAIN_ONE + i : GAIN_ONE + i + 1, : ref.shape[0]] = (
+            ref[...].astype(jnp.float32).reshape(1, ref.shape[0])
+        )
+    columns = jnp.transpose(square[...])[: gain_one_own.shape[0]]
+    square[: gain_one_own.shape[0], :] = columns
+    square[: gain_one_own.shape[0], :experts] = route_own[...].astype(jnp.float32)
+    dense[own, :, 4 * width :] = square[: gain_one_own.shape[0], :].astype(jnp.bfloat16)
+    for p in range(2):
+        cot_all[0, p] = lengthened(cot_own, p).astype(jnp.bfloat16)
+    place.greet()
 
     dense_tree = Spread(
         place,
         lambda rel, k, p: dense.at[place.index(rel, k)],
         lambda rel_there, k_there, p, rel, k: dense.at[place.index(rel, k)],
         1,
-        lambda k, p: k % 2,
+        lambda j, p: j % 2,
+        False,
         (dense_send, dense_recv),
     )
-    core_started = []
+    core_started, in_started, pair_started, local, outs = [], [], [], [], []
 
     def to_core(rel, k):
         slot = dense.at[place.index(rel, k)]
@@ -533,81 +629,61 @@
             core_started, slot, slot, core_send.at[rel, k], core_recv.at[rel, k], place.sibling
         )
 
-    dense[place.index(0, 0)] = own_dense[...]
-    dense_tree.own(0, dense.at[place.index(0, 0)])
-    to_core(0, 0)
-    for k in (1, 2, 3):
-        dense_tree.plane(k, 0)
-        to_core(0, k)
-    for k in range(4):
-        dense_tree.corner(k, 0)
-        to_core(1, k)
-        to_core(2, k)
-
-    local = []
+    def tree(ref, sems):
+        return Spread(place, block_here(ref), block_there(ref), 2, lambda j, p: p, True, sems)
+
+    cot_tree = tree(cot_all, (cot_send, cot_recv))
+    routed_tree = tree(routed_all, (routed_send, routed_recv))
 
     def local_copy(src, dst):
         copy = pltpu.make_async_copy(src, dst, local_sem.at[len(local)])
         copy.start()
         local.append(copy)
 
-    cot_tree = Spread(
-        place, block_here(cot_all), block_there(cot_all), 2, lambda k, p: p, (cot_send, cot_recv)
-    )
-    for p in range(2):
-        cot_tree.own(p, cot.at[p])
-        local_copy(cot.at[p], cot_all.at[0, p])
-    for k in range(4):
-        dense_tree.last(k, 0)
+    def down():
+        dense_tree.own(0, dense.at[own])
+        to_core(0, 0)
+        local_copy(w_in.at[:, :, pl.ds(pl.multiple_of(place.chip(0, 0) * SIDE, SIDE), SIDE)],
+                   w_in_all.at[place.chip(0, 0), place.core])
+        same_documents(segments, flat_ids, tall_ids)
+        gate_row[...] = jnp.zeros_like(gate_row)
+
+    def dplane(j):
+        dense_tree.plane(j, 0)
+        to_core(0, place.nearest(j))
+
+    def dcorner(j):
+        k = place.nearest(j)
+        dense_tree.corner(j, 0)
+        other_side = 2 - j % 2
+        dense_tree.wait(other_side, other_side, k, 0)
+        to_core(1, k)
+        to_core(2, k)
+
+    def dlast(j):
+        k = place.nearest(j)
+        dense_tree.wait(3, 3, k, 0)
         to_core(3, k)
-    in_started = []
-    for rel in (3, 1, 2, 0):
-        for k in (2, 1, 3, 0):
-            columns = pl.ds(pl.multiple_of(place.chip(rel, k) * SIDE, SIDE), SIDE)
-            src = w_in.at[:, :, columns]
-            dst = w_in_all.at[place.chip(0, 0), place.core]
-            if (rel, k) == (0, 0):
-                local_copy(src, dst)
-            else:
-                send(
-                    in_started, src, dst, in_send.at[rel, k], in_recv.at[rel, back(k)],
-                    place.device(rel, k),
-                )
-    pair_started = []
-    local_copy(w_out, w_out_all.at[place.core])
-    send(
-        pair_started, w_out, w_out_all.at[place.core], pair_send.at[0], pair_recv.at[0],
-        place.sibling,
-    )
-    for k in range(4):
-        for rel in range(4):
-            slot = dense.at[place.plane(k) * 8 + place.at[rel] + 1 - 2 * place.core]
-            arrived(slot, core_recv.at[rel, k])
-    local_copy(dense, dense_out)
-
-    small = dense[:, :, 4 * width : 4 * width + SIDE].reshape(width, SIDE)
-    turned[...] = jnp.transpose(small.astype(jnp.float32))
-    gain_one, bias_one = turned[GAIN_ONE : GAIN_ONE + 1, :], turned[GAIN_ONE + 1 : GAIN_ONE + 2, :]
-    gain_two, bias_two = turned[GAIN_ONE + 2 : GAIN_ONE + 3, :], turned[GAIN_ONE + 3 : GAIN_ONE + 4, :]
-
-    routed_tree = Spread(
-        place,
-        block_here(routed_all),
-        block_there(routed_all),
-        2,
-        lambda k, p: p,
-        (routed_send, routed_recv),
-    )
-
-    for p in range(2):
-        block = tok[p].astype(jnp.float32)
+
+    def dwait():
+        for k in range(4):
+            for rel in range(4):
+                slot = dense.at[place.plane(k) * 8 + place.at[rel] + 1 - 2 * place.core]
+                arrived(slot, core_recv.at[rel, k])
+        local_copy(dense, dense_out)
+        small = dense[:, :, 4 * width : 4 * width + SIDE].reshape(width, SIDE)
+        turned[...] = jnp.transpose(small.astype(jnp.float32))
+
+    def att(p):
+        row = [turned[GAIN_ONE + i : GAIN_ONE + i + 1, :] for i in range(4)]
+        block = lengthened(tok, p)
         unit, unused = norm_parts(block)
-        normed = (unit * gain_one + bias_one).astype(jnp.bfloat16)
+        normed = (unit * row[0] + row[1]).astype(jnp.bfloat16)
         w_qkv = dense[:, :, : 3 * width].reshape(width, 3 * width)
         proj[p] = dot(normed, w_qkv).astype(jnp.bfloat16)
-        same = seg_col[p] == seg_row[p]
-
-        def pair_of_heads(j, carry, p=p, same=same):
+        same = same_document(flat_ids, tall_ids, p)
+
+        def pair_of_heads(j, carry):
             at = pl.multiple_of(j * SIDE, SIDE)
             queries = proj[p, :, pl.ds(at, SIDE)]
             keys = proj[p, :, pl.ds(at + width, SIDE)]
@@ -625,71 +701,95 @@
         mid = block + dot(heads[p], w_attn)
         middle[p] = mid
         unit, unused = norm_parts(mid)
-        routed[p] = jnp.where(real_rows(), unit * gain_two + bias_two, 0.0).astype(jnp.bfloat16)
-        routed_tree.own(p, routed.at[p])
-        local_copy(routed.at[p], routed_all.at[0, p])
-
-    for k in (1, 2, 3):
-        for p in range(2):
-            cot_tree.plane(k, p)
-    for k in range(4):
-        for p in range(2):
-            cot_tree.corner(k, p)
-    for k in (1, 2, 3):
-        for p in range(2):
-            routed_tree.plane(k, p)
-    for rel in range(4):
-        for k in range(4):
-            if (rel, k) != (0, 0):
-                arrived(w_in_all.at[place.chip(rel, k), place.core], in_recv.at[rel, k])
-    local[2 + 0].wait()
-    mine = w_in_all.at[:, place.core]
-    send(pair_started, mine, mine, pair_send.at[1], pair_recv.at[1], place.sibling)
-    for k in range(4):
-        for p in range(2):
-            routed_tree.corner(k, p)
-    for k in range(4):
-        for p in range(2):
-            cot_tree.last(k, p)
-            routed_tree.last(k, p)
-    other = 1 - place.core
-    arrived(w_out_all.at[other], pair_recv.at[0])
-    arrived(w_in_all.at[:, other], pair_recv.at[1])
-    for copy in local[:2] + local[3:]:
-        copy.wait()
-    for tree in (dense_tree, cot_tree, routed_tree):
-        tree.finish()
+        routed_all[0, p] = jnp.where(real_rows(), unit * row[2] + row[3], 0.0).astype(jnp.bfloat16)
+        routed_tree.own(p, routed_all.at[0, p])
+
+    def win(rel, j):
+        k = place.nearest(j)
+        columns = pl.ds(pl.multiple_of(place.chip(rel, k) * SIDE, SIDE), SIDE)
+        send(
+            in_started, w_in.at[:, :, columns], w_in_all.at[place.chip(0, 0), place.core],
+            in_send.at[rel, k], in_recv.at[rel, (4 - k) % 4], place.device(rel, k),
+        )
+
+    def wo():
+        local_copy(w_out, w_out_all.at[place.core])
+        send(
+            pair_started, w_out, w_out_all.at[place.core], pair_send.at[0], pair_recv.at[0],
+            place.sibling,
+        )
+
+    def winwait():
+        for rel in range(4):
+            for k in range(4):
+                if (rel, k) != (0, 0):
+                    arrived(w_in_all.at[place.chip(rel, k), place.core], in_recv.at[rel, k])
+        local[0].wait()
+        mine = w_in_all.at[:, place.core]
+        send(pair_started, mine, mine, pair_send.at[1], pair_recv.at[1], place.sibling)
+
+    def wsibwait():
+        for copy in local[1:]:
+            copy.wait()
+        arrived(w_out_all.at[other], pair_recv.at[0])
+        arrived(w_in_all.at[:, other], pair_recv.at[1])
+
+    def put(src, dst):
+        copy = pltpu.make_async_copy(src, dst, out_sem.at[len(outs)])
+        copy.start()
+        outs.append(copy)
+
+    def wave(j, p):
+        at = place.nearest(j) * 2 + p
+        cot_tree.last(j, p)
+        routed_tree.last(j, p)
+        count = len(outs) // 4
+        stage = count % 2
+        if count >= 2:
+            outs[4 * count - 8].wait()
+            outs[4 * count - 7].wait()
+
+        def one_block(rel, carry):
+            pair = place.pair(pack_task, task_experts, rel, place.nearest(j), p)
+            rows, cots = routed_all[rel, at], cot_all[rel, at]
+            gated, grad_pre, mixed, grad = expert_block(
+                pair, rows, cots, w_in_all, w_out_all, dense, gate_row
+            )
+            mixed_all[rel, at] = mixed
+            grad_all[rel, at] = grad
+            in_stage[stage, rel] = contract_rows(rows, grad_pre).astype(jnp.bfloat16)
+            out_stage[stage, rel] = contract_rows(gated, cots).astype(jnp.bfloat16)
+            return carry
+
+        lax.fori_loop(0, 4, one_block, 0)
+        put(in_stage.at[stage], in_terms.at[:, at])
+        put(out_stage.at[stage], out_terms.at[:, at])
+        put(grad_all.at[:, at], grad_out.at[:, at])
+        put(mixed_all.at[:, at], mixed_out.at[:, at])
+
+    steps = {
+        DOWN: down, DPLANE: dplane, DCORNER: dcorner, DLAST: dlast, DWAIT: dwait,
+        ATT: att, WIN: win, WO: wo, WINWAIT: winwait, WSIBWAIT: wsibwait, WAVE: wave,
+        COWN: lambda p: cot_tree.own(p, cot_all.at[0, p]),
+        CPLANE: cot_tree.plane, CCORNER: cot_tree.corner,
+        RPLANE: routed_tree.plane, RCORNER: routed_tree.corner,
+    }
+    for name, *where in FRONT_STEPS:
+        steps[name](*where)
+    for i, copy in enumerate(outs):
+        if i % 4 >= 2 or i >= len(outs) - 8:
+            copy.wait()
+    for each in (dense_tree, cot_tree, routed_tree):
+        each.finish()
     for copy in core_started + in_started + pair_started:
         copy.wait_send()
 
 
-def expert_kernel(
-    pairs, core, routed, cot, w_in_all, w_out_all, dense,
-    mixed, grad, d_in, d_out_own, d_out_far,
-    acc_in, acc_out, gate_row,
-):
-    step = pl.program_id(0)
-    width, slab = routed.shape[3], 2 * SIDE
-    experts = acc_in.shape[0]
-
-    @pl.when(step == 0)
-    def clear():
-        def one(e, carry):
-            acc_in[e] = jnp.zeros(acc_in.shape[1:], jnp.float32)
-            acc_out[e] = jnp.zeros(acc_out.shape[1:], jnp.float32)
-            return carry
-
-        lax.fori_loop(0, experts, one, 0)
-        gate_row[...] = jnp.zeros_like(gate_row)
-
-    first, second = pairs[2 * step], pairs[2 * step + 1]
-    rows, cots = routed[0, 0], cot[0, 0]
-    w_in = jnp.concatenate(
-        [w_in_all[:, :, e].reshape(width, SIDE) for e in (first, second)], axis=1
-    )
-    w_out = jnp.concatenate(
-        [w_out_all[:, e].reshape(SIDE, width) for e in (first, second)], axis=0
-    )
+def expert_block(pair, rows, cots, w_in_all, w_out_all, dense, gate_row):
+    width, slab = rows.shape[1], 2 * SIDE
+    first, second = pair
+    w_in = jnp.concatenate([w_in_all[:, :, e].reshape(width, SIDE) for e in pair], axis=1)
+    w_out = jnp.concatenate([w_out_all[:, e].reshape(SIDE, width) for e in pair], axis=0)
     route = dense[:, :, 4 * width : 4 * width + SIDE].reshape(width, SIDE)
     gate_a, gate_b = two_gates(dot(rows, route), first, second)
     lane = lax.broadcasted_iota(jnp.int32, (1, slab), 1)
@@ -704,33 +804,82 @@
     gated = (gates * act).astype(jnp.bfloat16)
     grad_pre = (gates * back_act * slope).astype(jnp.bfloat16)
     product = (act * back_act).astype(jnp.bfloat16)
-    sign = jnp.where(lane < SIDE, 1.0, -1.0)
-    signs = jnp.broadcast_to(sign, (8, slab)).astype(jnp.bfloat16)
+    signs = jnp.broadcast_to(jnp.where(lane < SIDE, 1.0, -1.0), (8, slab)).astype(jnp.bfloat16)
     gate_row[:, :ROWS] = contract_cols(signs, product)
-    mixed[0, 0] = dot(gated, w_out).astype(jnp.bfloat16)
+    mixed = dot(gated, w_out).astype(jnp.bfloat16)
     grads = contract_cols(grad_pre, w_in)
-    grad[0, 0] = jnp.concatenate([grads[:PACK], gate_row[...]], axis=0).astype(jnp.bfloat16)
-    new_in = contract_rows(rows, grad_pre)
-    acc_in[first] += new_in[:, :SIDE]
-    acc_in[second] += new_in[:, SIDE:]
-    new_out = contract_rows(gated, cots)
-    acc_out[first] += new_out[:SIDE]
-    acc_out[second] += new_out[SIDE:]
-
-    @pl.when(step == pl.num_programs(0) - 1)
-    def emit():
-        own = pl.multiple_of(core[0] * HEAD, HEAD)
-        far = pl.multiple_of((1 - core[0]) * HEAD, HEAD)
-
-        def one(e, carry):
-            total = acc_in[e].astype(jnp.bfloat16).reshape(16, 2, 16, SIDE)
-            d_in[0, :, e] = total[:, 0]
-            d_in[1, :, e] = total[:, 1]
-            d_out_own[e] = acc_out[e, pl.ds(own, HEAD)]
-            d_out_far[e] = acc_out[e, pl.ds(far, HEAD)].astype(jnp.bfloat16)
+    grad = jnp.concatenate([grads[:PACK], gate_row[...]], axis=0).astype(jnp.bfloat16)
+    return gated, grad_pre, mixed, grad
+
+
+def sum_kernel(
+    pack_task, task_experts, where, in_terms, out_terms, d_in, d_out_own, d_out_far, heads, nexts,
+    total_in, total_out,
+):
+    group = d_out_own.shape[0]
+    experts = group * pl.num_programs(0)
+    slots = in_terms.shape[0] * in_terms.shape[1]
+
+    @pl.when(pl.program_id(0) == 0)
+    def list_uses():
+        def clear(e, carry):
+            heads[e] = -1
             return carry
 
-        lax.fori_loop(0, experts, one, 0)
+        lax.fori_loop(0, experts, clear, 0)
+        g = where[1]
+        step_x, step_y = 2 - 4 * ((g // 2) % 2), 4 - 8 * (g // 4)
+
+        def one(slot, carry):
+            rel, k, p = slot // 8, (slot // 2) % 4, slot % 2
+            at = g + step_x * (rel % 2) + step_y * (rel // 2)
+            task = pack_task[(((where[0] + k) % 4) * 8 + at) * 2 + p]
+            for i in range(2):
+                e = task_experts[task, i]
+                nexts[slot * 2 + i] = heads[e]
+                heads[e] = slot * 2 + i
+            return carry
+
+        lax.fori_loop(0, slots, one, 0)
+
+    def terms(use):
+        slot = use // 2
+        rel, at, half = slot // 8, slot % 8, pl.multiple_of((use % 2) * SIDE, SIDE)
+        return (
+            in_terms[rel, at, :, pl.ds(half, SIDE)].astype(jnp.float32),
+            out_terms[rel, at, pl.ds(half, SIDE), :].astype(jnp.float32),
+        )
+
+    def add_terms(use):
+        new_in, new_out = terms(use)
+        total_in[...] += new_in
+        total_out[...] += new_out
+        return nexts[use]
+
+    own = pl.ds(pl.multiple_of(where[2] * HEAD, HEAD), HEAD)
+    far = pl.ds(pl.multiple_of((1 - where[2]) * HEAD, HEAD), HEAD)
+
+    def one_expert(i, carry):
+        head = heads[pl.program_id(0) * group + i]
+
+        @pl.when(head < 0)
+        def unused():
+            total_in[...] = jnp.zeros_like(total_in)
+            total_out[...] = jnp.zeros_like(total_out)
+
+        @pl.when(head >= 0)
+        def used():
+            total_in[...], total_out[...] = terms(head)
+            lax.while_loop(lambda use: use >= 0, add_terms, nexts[head])
+
+        low = total_in[...].astype(jnp.bfloat16).reshape(16, 2, 16, SIDE)
+        d_in[0, :, i] = low[:, 0]
+        d_in[1, :, i] = low[:, 1]
+        d_out_own[i] = total_out[own, :]
+        d_out_far[i] = total_out[far, :].astype(jnp.bfloat16)
+        return carry
+
+    lax.fori_loop(0, group, one_expert, 0)
 
 
 class Collect:
@@ -794,11 +943,11 @@
 
 
 def tail_kernel(
-    pairs, tok, cot, seg_col, seg_row, proj, heads, middle, dense, grad_part, mixed_part, d_in,
-    d_out_far,
+    pack_task, task_experts, tok, cot, segments, proj, heads, middle, dense, grad_part, mixed_part,
+    d_in, d_out_far,
     mixed, d_tok, d_dense, d_in_all, d_out_all,
     g_own, g_corner, g_x, g_y, g_z, m_own, m_corner, m_x, m_y, m_z,
-    total_grad, grad_mid, grad_heads, grad_qkv, acc, small_rows, turned,
+    total_grad, grad_mid, grad_heads, grad_qkv, acc, small_rows, turned, flat_ids, tall_ids,
     in_far, in_mine, far_dense, got_dense, part_dense, s_corner, s_x, s_y, s_z,
     g_send, g_recv, m_send, m_recv, s_send, s_recv, in_send, in_recv,
     pair_send, pair_recv, load_sem,
@@ -819,12 +968,8 @@
     mixes = Collect(
         place, part_of(mixed_part), m_corner, m_x, m_y, m_z, 2, by_pack, (m_send, m_recv)
     )
-    order = [(k, p) for k in (2, 1, 3, 0) for p in range(2)]
-    for k, p in order:
-        grads.opposite(k, p)
-    for k, p in order:
-        grads.straight(k, p)
-
+    planes = (2, 1, 3, 0)
+    order = [(k, p) for k in planes for p in range(2)]
     loads = []
 
     def load(src, dst):
@@ -844,16 +989,9 @@
         return waits
 
     g_waits = load_parts(grad_part, g_own)
-    pair_started = []
-    send(
-        pair_started, d_in.at[1 - place.core], in_far, pair_send.at[0], pair_recv.at[0],
-        place.sibling,
-    )
-    send(
-        pair_started, d_out_far, d_out_all, pair_send.at[1], pair_recv.at[1], place.sibling
-    )
     in_load = load(d_in.at[place.core], in_mine)
     m_waits = load_parts(mixed_part, m_own)
+    pair_started, in_started, kept = [], [], {}
 
     def mine(waits, own, kind, k, p):
         def get():
@@ -862,46 +1000,57 @@
 
         return get
 
-    in_load.wait()
-    arrived(in_far, pair_recv.at[0])
-
-    def add_pair(i, carry):
-        total = in_mine[i].astype(jnp.float32) + in_far[i].astype(jnp.float32)
-        in_mine[i] = total.astype(jnp.bfloat16)
-        return carry
-
-    lax.fori_loop(0, in_mine.shape[0], add_pair, 0)
-
-    for k, p in order:
-        grads.helped(k, p, mine(g_waits, g_own, "helped", k, p))
-    for k, p in order:
-        mixes.opposite(k, p)
-    for k, p in order:
-        mixes.straight(k, p)
-    for k, p in order:
-        if k:
-            grads.plane(k, p, mine(g_waits, g_own, "plane", k, p))
-    in_started = []
-    columns = pl.ds(pl.multiple_of(place.chip(0, 0) * SIDE, SIDE), SIDE)
-    for rel in (3, 1, 2, 0):
-        for k in (2, 1, 3, 0):
-            src = in_mine.at[place.chip(rel, k)]
-            dst = d_in_all.at[:, :, columns]
-            if (rel, k) == (0, 0):
-                in_local = load(src, dst)
-            else:
-                send(
-                    in_started, src, dst, in_send.at[rel, k], in_recv.at[rel, back(k)],
-                    place.device(rel, k),
-                )
-    for p in range(2):
-        total_grad[p] = grads.plane(0, p, mine(g_waits, g_own, "plane", 0, p))
-
+    same_documents(segments, flat_ids, tall_ids)
     small = dense[:, :, 4 * width : 4 * width + SIDE].reshape(width, SIDE)
     turned[...] = jnp.transpose(small.astype(jnp.float32))
     small_rows[...] = jnp.zeros_like(small_rows)
-    gain_one, bias_one = turned[GAIN_ONE : GAIN_ONE + 1, :], turned[GAIN_ONE + 1 : GAIN_ONE + 2, :]
-    gain_two, bias_two = turned[GAIN_ONE + 2 : GAIN_ONE + 3, :], turned[GAIN_ONE + 3 : GAIN_ONE + 4, :]
+    gain_one, bias_one, gain_two, bias_two = (
+        turned[GAIN_ONE + i : GAIN_ONE + i + 1, :] for i in range(4)
+    )
+
+    def pair():
+        send(
+            pair_started, d_in.at[1 - place.core], in_far, pair_send.at[0], pair_recv.at[0],
+            place.sibling,
+        )
+        send(
+            pair_started, d_out_far, d_out_all, pair_send.at[1], pair_recv.at[1], place.sibling
+        )
+
+    def addpair():
+        in_load.wait()
+        arrived(in_far, pair_recv.at[0])
+
+        def one(i, carry):
+            total = in_mine[i].astype(jnp.float32) + in_far[i].astype(jnp.float32)
+            in_mine[i] = total.astype(jnp.bfloat16)
+            return carry
+
+        lax.fori_loop(0, in_mine.shape[0], one, 0)
+        columns = pl.ds(pl.multiple_of(place.chip(0, 0) * SIDE, SIDE), SIDE)
+        kept["local"] = load(in_mine.at[place.chip(0, 0)], d_in_all.at[:, :, columns])
+
+    def win(rel, j):
+        k = planes[j]
+        columns = pl.ds(pl.multiple_of(place.chip(0, 0) * SIDE, SIDE), SIDE)
+        send(
+            in_started, in_mine.at[place.chip(rel, k)], d_in_all.at[:, :, columns],
+            in_send.at[rel, k], in_recv.at[rel, back(k)], place.device(rel, k),
+        )
+
+    def plane_of(tree, waits, own_parts, keep):
+        def run(j, p):
+            got = tree.plane(planes[j], p, mine(waits, own_parts, "plane", planes[j], p))
+            if got is not None:
+                keep(p, got)
+
+        return run
+
+    def keep_grad(p, got):
+        total_grad[p] = got
+
+    def keep_mixed(p, got):
+        mixed[p] = (middle[p] + got).astype(jnp.bfloat16)
 
     def add_to(p, columns, value):
         if p == 0:
@@ -912,8 +1061,12 @@
     def add_row(at, value):
         small_rows[at : at + 1, :] += jnp.sum(value, 0, keepdims=True)
 
-    for p in range(2):
-        first, second = pairs[2 * p], pairs[2 * p + 1]
+    def att(part):
+        p = part // 3
+        (att_routed, att_heads, att_normed)[part % 3](p)
+
+    def att_routed(p):
+        first, second = place.pair(pack_task, task_experts, 0, 0, p)
         got = total_grad[p]
         tall = jnp.concatenate(
             [got[PACK:, : 2 * SIDE], jnp.zeros((SIDE - 8, 2 * SIDE), jnp.float32)], axis=0
@@ -934,7 +1087,7 @@
         add_row(2, got * unit)
         add_row(3, got)
         u = got * gain_two
-        grad_middle = cot[p].astype(jnp.float32) + rise * (
+        grad_middle = lengthened(cot, p) + rise * (
             u - jnp.mean(u, -1, keepdims=True) - unit * jnp.mean(u * unit, -1, keepdims=True)
         )
         grad_mid[...] = grad_middle
@@ -942,9 +1095,11 @@
         add_to(p, pl.ds(3 * width, width), contract_rows(heads[p], attended))
         w_attn = dense[:, :, 3 * width : 4 * width].reshape(width, width)
         grad_heads[...] = contract_cols(attended, w_attn).astype(jnp.bfloat16)
-        same = seg_col[p] == seg_row[p]
-
-        def pair_of_heads(j, carry, p=p, same=same):
+
+    def att_heads(p):
+        same = same_document(flat_ids, tall_ids, p)
+
+        def pair_of_heads(j, carry):
             at = pl.multiple_of(j * SIDE, SIDE)
             queries = proj[p, :, pl.ds(at, SIDE)]
             keys = proj[p, :, pl.ds(at + width, SIDE)]
@@ -969,9 +1124,9 @@
             return carry
 
         lax.fori_loop(0, width // SIDE, pair_of_heads, 0)
-        for k, q in order[4 * p : 4 * p + 4]:
-            mixes.helped(k, q, mine(m_waits, m_own, "helped", k, q))
-        unit, rise = norm_parts(tok[p].astype(jnp.float32))
+
+    def att_normed(p):
+        unit, rise = norm_parts(lengthened(tok, p))
         normed = (unit * gain_one + bias_one).astype(jnp.bfloat16)
         add_to(p, pl.ds(0, 3 * width), contract_rows(normed, grad_qkv[...]))
         w_qkv = dense[:, :, : 3 * width].reshape(width, 3 * width)
@@ -985,71 +1140,103 @@
             * (u - jnp.mean(u, -1, keepdims=True) - unit * jnp.mean(u * unit, -1, keepdims=True))
         ).astype(jnp.bfloat16)
 
-    tall = jnp.concatenate(
-        [
-            jnp.zeros((GAIN_ONE, width), jnp.float32),
-            small_rows[...],
-            jnp.zeros((SIDE - GAIN_ONE - 8, width), jnp.float32),
-        ],
-        axis=0,
-    )
-    acc[:, 4 * width :] += jnp.transpose(tall)
-    columns_all = acc.shape[1]
-
-    def cut(i, carry):
-        own_rows = pl.ds(pl.multiple_of(i * 32 + place.core * 16, 16), 16)
-        far_rows = pl.ds(pl.multiple_of(i * 32 + 16 - place.core * 16, 16), 16)
-        far_dense[i] = acc[far_rows, :].astype(jnp.bfloat16)
-        part_dense[i] = acc[own_rows, :]
-        return carry
-
-    lax.fori_loop(0, 16, cut, 0)
-    send(
-        pair_started, far_dense, got_dense, pair_send.at[2], pair_recv.at[2], place.sibling
-    )
-    arrived(got_dense, pair_recv.at[2])
-
-    def join(i, carry):
-        far_dense_sum = part_dense[i] + got_dense[i].astype(jnp.float32)
-        got_dense[i] = far_dense_sum.astype(jnp.bfloat16)
-        return carry
-
-    lax.fori_loop(0, 16, join, 0)
-
     def dense_part(rel, k, p):
         return got_dense.at[place.chip(rel, k)]
 
     sums = Collect(
         place, dense_part, s_corner, s_x, s_y, s_z, 1, lambda k, p: k % 2, (s_send, s_recv)
     )
-    for k in (2, 1, 3, 0):
-        sums.opposite(k, 0)
-    for k in (2, 1, 3, 0):
-        sums.straight(k, 0)
-    for k in (2, 1, 3, 0):
-        sums.helped(k, 0, lambda k=k: got_dense[place.chip(1 + k % 2, k)])
-    for k in (2, 1, 3):
-        sums.plane(k, 0, lambda k=k: got_dense[place.chip(0, k)])
-    d_dense[...] = sums.plane(0, 0, lambda: got_dense[place.chip(0, 0)])
-
-    for k, p in order:
-        if k:
-            mixes.plane(k, p, mine(m_waits, m_own, "plane", k, p))
-    for p in range(2):
-        summed = mixes.plane(0, p, mine(m_waits, m_own, "plane", 0, p))
-        mixed[p] = (middle[p] + summed).astype(jnp.bfloat16)
+    def dense_step():
+        tall = jnp.concatenate(
+            [
+                jnp.zeros((GAIN_ONE, width), jnp.float32),
+                small_rows[...],
+                jnp.zeros((SIDE - GAIN_ONE - 8, width), jnp.float32),
+            ],
+            axis=0,
+        )
+        acc[:, 4 * width :] += jnp.transpose(tall)
+        columns_all = acc.shape[1]
+
+        def cut(i, carry):
+            own_rows = pl.ds(pl.multiple_of(i * 32 + place.core * 16, 16), 16)
+            far_rows = pl.ds(pl.multiple_of(i * 32 + 16 - place.core * 16, 16), 16)
+            far_dense[i] = acc[far_rows, :].astype(jnp.bfloat16)
+            part_dense[i] = acc[own_rows, :]
+            return carry
+
+        lax.fori_loop(0, 16, cut, 0)
+        send(
+            pair_started, far_dense, got_dense, pair_send.at[2], pair_recv.at[2], place.sibling
+        )
+        arrived(got_dense, pair_recv.at[2])
+
+        def join(i, carry):
+            far_dense_sum = part_dense[i] + got_dense[i].astype(jnp.float32)
+            got_dense[i] = far_dense_sum.astype(jnp.bfloat16)
+            return carry
+
+        lax.fori_loop(0, 16, join, 0)
+
+        for k in (2, 1, 3, 0):
+            sums.opposite(k, 0)
+        for k in (2, 1, 3, 0):
+            sums.straight(k, 0)
+        for k in (2, 1, 3, 0):
+            sums.helped(k, 0, lambda k=k: got_dense[place.chip(1 + k % 2, k)])
+        for k in (2, 1, 3):
+            sums.plane(k, 0, lambda k=k: got_dense[place.chip(0, k)])
+        d_dense[...] = sums.plane(0, 0, lambda: got_dense[place.chip(0, 0)])
+
+    steps = {
+        GFIRST: lambda j, p: (grads.opposite(planes[j], p), grads.straight(planes[j], p)),
+        MFIRST: lambda j, p: (mixes.opposite(planes[j], p), mixes.straight(planes[j], p)),
+        GHELP: lambda j, p: grads.helped(
+            planes[j], p, mine(g_waits, g_own, "helped", planes[j], p)
+        ),
+        MHELP: lambda j, p: mixes.helped(
+            planes[j], p, mine(m_waits, m_own, "helped", planes[j], p)
+        ),
+        GPLANE: plane_of(grads, g_waits, g_own, keep_grad),
+        MPLANE: plane_of(mixes, m_waits, m_own, keep_mixed),
+        PAIR: pair, ADDPAIR: addpair, WIN: win, ATT: att, DENSE: dense_step,
+    }
+    for name, *where in TAIL_STEPS:
+        steps[name](*where)
 
     for rel in range(4):
         for k in range(4):
             if (rel, k) != (0, 0):
                 place_columns = pl.ds(pl.multiple_of(place.chip(rel, k) * SIDE, SIDE), SIDE)
                 arrived(d_in_all.at[:, :, place_columns], in_recv.at[rel, k])
-    in_local.wait()
+    kept["local"].wait()
     arrived(d_out_all, pair_recv.at[1])
     for tree in (grads, mixes, sums):
         tree.finish()
     for copy in pair_started + in_started:
         copy.wait_send()
+
+
+def last_kernel(
+    mixed_tall, d_tok_tall, d_dense, d_in_low, d_out_own, d_out_far,
+    mixed, d_tok, d_qkv, d_attn, d_route, d_in, d_out, gain_one, bias_one, gain_two, bias_two,
+):
+    width, experts = mixed.shape[2], d_route.shape[1]
+
+    @pl.when(pl.program_id(0) == 0)
+    def small():
+        for p in range(mixed.shape[0]):
+            mixed[p] = mixed_tall[p, :PACK]
+            d_tok[p] = d_tok_tall[p, :PACK]
+        d_qkv[...] = d_dense[:, : 3 * width]
+        d_attn[...] = d_dense[:, 3 * width : 4 * width]
+        d_route[...] = d_dense[:, 4 * width : 4 * width + experts]
+        rows = jnp.transpose(d_dense[:, 4 * width :])
+        for i, ref in enumerate((gain_one, bias_one, gain_two, bias_two)):
+            ref[...] = rows[GAIN_ONE + i]
+
+    d_in[...] = d_in_low[...].astype(jnp.float32)
+    d_out[...] = d_out_own[...] + d_out_far[...].astype(jnp.float32)
 
 
 def shards_fast(
@@ -1075,122 +1262,116 @@
     any_space = pl.BlockSpec(memory_space=pl.ANY)
     vmem = pl.BlockSpec(memory_space=pltpu.VMEM)
     smem = pl.BlockSpec(memory_space=pltpu.SMEM)
-    low = jnp.bfloat16
+    low, full = jnp.bfloat16, jnp.float32
     flat = jax.ShapeDtypeStruct
     dma = pltpu.SemaphoreType.DMA
 
-    def tall(array, fill=0):
-        return jnp.pad(
-            array,
-            ((0, 0), (0, ROWS - length)) + ((0, 0),) * (array.ndim - 2),
-            constant_values=fill,
-        )
-
-    tok, cot = tall(tokens), tall(cotangent)
-    segments = tall(segment_ids, -1)
-    seg_col, seg_row = segments[:, :, None], segments[:, None, :]
-    norms = jnp.stack([norm1_gain, norm1_bias, norm2_gain, norm2_bias], axis=1)
-    small = jnp.concatenate([w_router, norms], axis=1)
-    small = jnp.pad(small, ((0, 0), (0, SIDE - small.shape[1])))
-    own_dense = jnp.concatenate([w_qkv, w_attn_out, small], axis=1)
-
-    pack_pairs = task_experts[pack_task]
     z, g = lax.axis_index("gx"), lax.axis_index("gy")
-    core = g % 2
-    slot_devices = []
-    for rel in range(4):
-        at = g + (2 - 4 * ((g // 2) % 2)) * (rel % 2) + (4 - 8 * (g // 4)) * (rel // 2)
-        for k in range(4):
-            slot_devices.append(((z + k) % 4) * 8 + at)
-    slots = jnp.stack(slot_devices)
-    slot_pairs = pack_pairs.reshape(32, packs * 2)[slots].reshape(-1)
+    where = jnp.stack([z, g, g % 2])
 
     blocks = flat((4, 4 * packs, ROWS, width), low)
-    (
-        routed_all, cot_all, w_in_all, w_out_all, dense, proj, heads, middle,
-    ) = pl.pallas_call(
+    in_sums = flat((4, 4 * packs, width, 2 * SIDE), low)
+    out_sums = flat((4, 4 * packs, 2 * SIDE, width), low)
+
+    def held(shape):
+        return pltpu.VMEM(shape.shape, shape.dtype)
+
+    in_terms, out_terms, mixed_part, grad_part, dense, proj, heads, middle = pl.pallas_call(
         front_kernel,
         out_shape=(
-            blocks,
-            blocks,
-            flat((16, 2, experts, slab_in, SIDE), low),
-            flat((2, experts, slab_out, width), low),
+            in_sums, out_sums, blocks, blocks,
             flat((32, slab_in, dense_width), low),
             flat((packs, ROWS, 3 * width), low),
             flat((packs, ROWS, width), low),
-            flat((packs, ROWS, width), jnp.float32),
+            flat((packs, ROWS, width), full),
         ),
-        in_specs=[vmem] * 4 + [any_space] * 3,
+        in_specs=[smem] * 2 + [vmem] * 10 + [any_space] * 2,
         out_specs=(any_space,) * 5 + (vmem,) * 3,
         scratch_shapes=[
             pltpu.VMEM((32, slab_in, dense_width), low),
-            pltpu.VMEM((packs, ROWS, width), low),
-            pltpu.VMEM((SIDE, width), jnp.float32),
-            dma((4, 8)), dma((4, 8)), dma((4, 8)), dma((4, 8)), dma((4, 4)), dma((4, 4)),
-            dma((4, 4)), dma((4, 4)), dma((4, 4)), dma((4, 4)), dma((2,)), dma((2,)), dma((8,)),
+            held(blocks), held(blocks),
+            pltpu.VMEM((16, 2, experts, slab_in, SIDE), low),
+            pltpu.VMEM((2, experts, slab_out, width), low),
+            pltpu.VMEM((2, 4, width, 2 * SIDE), low),
+            pltpu.VMEM((2, 4, 2 * SIDE, width), low),
+            held(blocks), held(blocks),
+            pltpu.VMEM((SIDE, width), full),
+            pltpu.VMEM((SIDE, SIDE), full),
+            pltpu.VMEM((8, 2 * SIDE), full),
+            pltpu.VMEM((2 * SIDE, 8), full),
+            pltpu.VMEM((8, width), full),
+            dma((5, 8)), dma((4, 8)), dma((5, 8)), dma((4, 8)), dma((5, 4)), dma((4, 4)),
+            dma((4, 4)), dma((4, 4)), dma((4, 4)), dma((4, 4)), dma((2,)), dma((2,)), dma((3,)),
+            dma((32,)),
         ],
         compiler_params=pltpu.CompilerParams(
-            collective_id=0, has_side_effects=True, vmem_limit_bytes=40 << 20
+            collective_id=0, has_side_effects=True, vmem_limit_bytes=60 << 20
         ),
         name="front",
-    )(tok, seg_col, seg_row, own_dense, cot, w_expert_in, w_expert_out)
-
-    steps = 4 * 4 * packs
-    one_block = pl.BlockSpec(
-        (1, 1, ROWS, width), lambda i, *unused: (i // (4 * packs), i % (4 * packs), 0, 0)
-    )
-    mixed_part, grad_part, d_in, d_out_own, d_out_far = pl.pallas_call(
-        expert_kernel,
+    )(
+        pack_task, task_experts, tokens, segment_ids, w_qkv, w_attn_out, w_router,
+        norm1_gain, norm1_bias, norm2_gain, norm2_bias, cotangent, w_expert_in, w_expert_out,
+    )
+
+    def by_expert(rows):
+        return pl.BlockSpec((experts // 8, rows, width), lambda e, *unused: (e, 0, 0))
+
+    d_in, d_out_own, d_out_far = pl.pallas_call(
+        sum_kernel,
         grid_spec=pltpu.PrefetchScalarGridSpec(
-            num_scalar_prefetch=2,
-            grid=(steps,),
-            in_specs=[one_block, one_block, vmem, vmem, vmem],
-            out_specs=[one_block, one_block, vmem, vmem, vmem],
+            num_scalar_prefetch=3,
+            grid=(8,),
+            in_specs=[vmem] * 2,
+            out_specs=[
+                pl.BlockSpec((2, 16, experts // 8, slab_in, SIDE), lambda e, *unused: (0, 0, e, 0, 0)),
+                by_expert(slab_out), by_expert(slab_out),
+            ],
             scratch_shapes=[
-                pltpu.VMEM((experts, width, SIDE), jnp.float32),
-                pltpu.VMEM((experts, SIDE, width), jnp.float32),
-                pltpu.VMEM((8, width), jnp.float32),
+                pltpu.SMEM((experts,), jnp.int32),
+                pltpu.SMEM((32 * packs,), jnp.int32),
+                pltpu.VMEM((width, SIDE), full),
+                pltpu.VMEM((SIDE, width), full),
             ],
         ),
         out_shape=(
-            blocks,
-            blocks,
             flat((2, 16, experts, slab_in, SIDE), low),
-            flat((experts, slab_out, width), jnp.float32),
+            flat((experts, slab_out, width), full),
             flat((experts, slab_out, width), low),
         ),
-        compiler_params=pltpu.CompilerParams(vmem_limit_bytes=56 << 20),
-        name="experts",
-    )(slot_pairs, core[None], routed_all, cot_all, w_in_all, w_out_all, dense)
+        compiler_params=pltpu.CompilerParams(vmem_limit_bytes=60 << 20),
+        name="sums",
+    )(pack_task, task_experts, where, in_terms, out_terms)
 
     parts = pltpu.VMEM((4 * packs, ROWS, width), low)
     slices = pltpu.VMEM((4, slab_in, dense_width), low)
     sliced = pltpu.VMEM((16, slab_in, dense_width), low)
-    mixed, d_tok, d_dense, d_in_all, d_out_all = pl.pallas_call(
+    mixed_tall, d_tok_tall, d_dense, d_in_all, d_out_all = pl.pallas_call(
         tail_kernel,
         out_shape=(
             flat((packs, ROWS, width), low),
             flat((packs, ROWS, width), low),
-            flat((slab_in, dense_width), jnp.float32),
+            flat((slab_in, dense_width), full),
             flat((experts, slab_in, hidden), low),
             flat((experts, slab_out, width), low),
         ),
-        in_specs=[smem] + [vmem] * 8 + [any_space] * 4,
+        in_specs=[smem] * 2 + [vmem] * 7 + [any_space] * 4,
         out_specs=(vmem,) * 3 + (any_space,) * 2,
         scratch_shapes=[
             pltpu.VMEM((2, 4 * packs, ROWS, width), low), parts, parts, parts, parts,
             pltpu.VMEM((2, 4 * packs, ROWS, width), low), parts, parts, parts, parts,
-            pltpu.VMEM((packs, ROWS, width), jnp.float32),
-            pltpu.VMEM((ROWS, width), jnp.float32),
+            pltpu.VMEM((packs, ROWS, width), full),
+            pltpu.VMEM((ROWS, width), full),
             pltpu.VMEM((ROWS, width), low),
             pltpu.VMEM((ROWS, 3 * width), low),
-            pltpu.VMEM((width, dense_width), jnp.float32),
-            pltpu.VMEM((8, width), jnp.float32),
-            pltpu.VMEM((SIDE, width), jnp.float32),
+            pltpu.VMEM((width, dense_width), full),
+            pltpu.VMEM((8, width), full),
+            pltpu.VMEM((SIDE, width), full),
+            pltpu.VMEM((8, 2 * SIDE), full),
+            pltpu.VMEM((2 * SIDE, 8), full),
             pltpu.VMEM((16, experts, slab_in, SIDE), low),
             pltpu.VMEM((16, experts, slab_in, SIDE), low),
             sliced, sliced,
-            pltpu.VMEM((16, slab_in, dense_width), jnp.float32),
+            pltpu.VMEM((16, slab_in, dense_width), full),
             slices, slices, slices, slices,
             dma((4, 8)), dma((4, 8)), dma((4, 8)), dma((4, 8)), dma((4, 4)), dma((4, 4)),
             dma((4, 4)), dma((4, 4)), dma((3,)), dma((3,)), dma((40,)),
@@ -1200,23 +1381,39 @@
         ),
         name="tail",
     )(
-        slot_pairs[: 2 * packs], tok, cot, seg_col, seg_row, proj, heads, middle, dense,
+        pack_task, task_experts, tokens, cotangent, segment_ids, proj, heads, middle, dense,
         grad_part, mixed_part, d_in, d_out_far,
     )
-    norm_at = 4 * width + GAIN_ONE
-    return (
-        mixed[:, :length],
-        d_tok[:, :length],
-        d_dense[:, : 3 * width],
-        d_dense[:, 3 * width : 4 * width],
-        d_dense[:, 4 * width : 4 * width + experts],
-        d_in_all.astype(jnp.float32),
-        d_out_own + d_out_all.astype(jnp.float32),
-        d_dense[:, norm_at],
-        d_dense[:, norm_at + 1],
-        d_dense[:, norm_at + 2],
-        d_dense[:, norm_at + 3],
-    )
+
+    group = experts // 2
+
+    def some(rows, columns):
+        return pl.BlockSpec((group, rows, columns), lambda i: (i, 0, 0))
+
+    def whole(*shape):
+        return pl.BlockSpec(shape, lambda i: (0,) * len(shape))
+
+    return pl.pallas_call(
+        last_kernel,
+        grid=(2,),
+        in_specs=[
+            whole(packs, ROWS, width), whole(packs, ROWS, width), whole(slab_in, dense_width),
+            some(slab_in, hidden), some(slab_out, width), some(slab_out, width),
+        ],
+        out_specs=(
+            whole(packs, length, width), whole(packs, length, width),
+            whole(slab_in, 3 * width), whole(slab_in, width), whole(slab_in, experts),
+            some(slab_in, hidden), some(slab_out, width),
+        ) + (whole(slab_in),) * 4,
+        out_shape=(
+            flat((packs, length, width), low), flat((packs, length, width), low),
+            flat((slab_in, 3 * width), full), flat((slab_in, width), full),
+            flat((slab_in, experts), full),
+            flat((experts, slab_in, hidden), full), flat((experts, slab_out, width), full),
+        ) + (flat((slab_in,), full),) * 4,
+        compiler_params=pltpu.CompilerParams(vmem_limit_bytes=60 << 20),
+        name="last",
+    )(mixed_tall, d_tok_tall, d_dense, d_in_all, d_out_own, d_out_all)
 
 
 def solution(mesh):

time: 468 us -> 376 us (0.80)
  Pallas kernels: 433 us -> 374 us
  local copies, waits for them, and re-layouts: 22.1 us -> 1.36 us
  other arithmetic: 10.1 us -> 0.59 us
    pallas_call x2 -> x3, Pallas kernels: 232 us -> 197 us  [the longest x1 175 us: shards_fast(): pl.pallas_call(front_kernel, out_shape=(in_sums, out_sums, blocks, blocks...]
    pallas_call x1, Pallas kernels: 201 us -> 177 us  [shards_fast(): pl.pallas_call(tail_kernel, out_shape=(flat((packs, ROWS, width), low), f...]
    unnamed x31 -> x1, local copies, waits for them, and re-layouts: 8.58 us -> 1.36 us
    add x1 -> x0, other arithmetic: 5.96 us -> none  [shards_fast(): d_out_own + d_out_all.astype(jnp.float32)]
    slice x7 -> x0, local copies, waits for them, and re-layouts: 4.69 us -> none  [the longest x1 0.79 us: shards_fast(): d_tok[:, :length]]
where the time goes in v2:
time: 376 us
  Pallas kernels  374 us (99%)
    pallas_call x1, Pallas kernels, shards_fast(): pl.pallas_call(tail_kernel, out_shape=(flat((packs, ROWS, width), low), f...  177 us
    pallas_call x1, Pallas kernels, shards_fast(): pl.pallas_call(front_kernel, out_shape=(in_sums, out_sums, blocks, blocks...  175 us
    pallas_call x1, Pallas kernels, shards_fast(): pl.pallas_call(sum_kernel, grid_spec=pltpu.PrefetchScalarGridSpec(num_sca...  14.4 us

profile of v2, /device:TPU:8, one launch (start us, length us, event | category | flops | bytes accessed | tf_op | source)
XLA Modules:
  0.0 376.3 jit_solution(14714433767129484162)
XLA Ops:
  0.7 0.6 pad_add_fusion.where
  1.2 1.4 copy.27.task_experts
  2.6 175.2 %front.1 = (bf16[4,8,512,256]{3,2,1,0:T(8,128)(2,1)}, bf16[4,8,256,512]{3,2,1,0:T(8,128)(2,1)}, bf16[4,8,224,512]{3,2,1,0:T(8,128)(2,1)}, bf16[4,8,224,512]{3,2,...) custom-call(s32[64]{0:T(128)} %pack_task.5, ...), custom_call_target="tpu_custom_call" | custom-call | tf_op jit(solution)/shard_map/front/pallas_call | solution.py:1279
  177.8 14.4 %sums.1 = (bf16[2,16,32,16,128]{4,3,2,1,0:T(8,128)(2,1)}, f32[32,64,512]{2,1,0:T(8,128)}, bf16[32,64,512]{2,1,0:T(8,128)(2,1)}) custom-call(s32[64]{0:T(128)} %pack_task.5, s32[24,2]{1,0:T(8,128)} %copy.27.task_experts, s32[3]{0:T(128)} %pad_add_fusion.where, bf16[4,8,512,256]{3,2,1,0:T(8,128)(2,1)} %get-tuple-element.33.in_terms, ...), custom_call_target="tpu_custom_call" | custom-call | tf_op jit(solution)/shard_map/sums/pallas_call | solution.py:1319
  192.2 177.0 %tail.1 = (bf16[2,224,512]{2,1,0:T(8,128)(2,1)}, bf16[2,224,512]{2,1,0:T(8,128)(2,1)}, f32[16,2176]{1,0:T(8,128)}, bf16[32,16,2048]{2,1,0:T(8,128)(2,1)}, bf16[32,64,512]{2,1,0:T(8,128)(2,1)}) custom-call(s32[64]{0:T(128)} %pack_task.5, s32[24,2]{1,0:T(8,128)} %copy.27.task_experts, bf16[2,216,512]{2,1,0:T(8,128)(2,1)} %tok.3, bf16[2,216,512]{2,1,0:T(8,128)(2,1)} %cot.1, ...), custom_call_target="tpu_custom_call" | custom-call | tf_op jit(solution)/shard_map/tail/pallas_call | solution.py:1348
  369.2 7.1 %last.1 = (bf16[2,216,512]{2,1,0:T(8,128)(2,1)}, bf16[2,216,512]{2,1,0:T(8,128)(2,1)}, f32[16,1536]{1,0:T(8,128)}, f32[16,512]{1,0:T(8,128)}, f32[16,32]{1,0:T(8...) custom-call(bf16[2,224,512]{2,1,0:T(8,128)(2,1)} %get-tuple-element., ...), custom_call_target="tpu_custom_call" | custom-call | tf_op jit(solution)/shard_map/last/pallas_call | solution.py:1396

commit v3 on v2

--- a/solution.py
+++ b/solution.py
@@ -360,34 +360,37 @@
 
 (
     DOWN, DPLANE, DCORNER, DLAST, DWAIT, ATT, WIN, WO, WINWAIT, WSIBWAIT, WAVE, COWN,
-    CPLANE, CCORNER, RPLANE, RCORNER, GFIRST, MFIRST, GHELP, MHELP, GPLANE, MPLANE, PAIR, ADDPAIR, DENSE,
-) = range(25)
+    CPLANE, CCORNER, CNEAR, CMZ, RPLANE, RCORNER, GFIRST, MFIRST, GHELP, MHELP, GPLANE, MPLANE, PAIR, ADDPAIR, DENSE,
+) = range(27)
+
+SIDE_PACKS = (0, 1)
+
+EARLY = ((0, 3), (1, 3))
 
 FRONT_STEPS = (
-    (WIN, 2, 1), (COWN, 0), (DOWN,), (WO,), (WIN, 2, 0), (WIN, 3, 1), (COWN, 1), (DPLANE, 2), (WIN, 3, 2),
-    (DPLANE, 3), (WIN, 1, 3), (DCORNER, 2), (DCORNER, 0), (DPLANE, 1), (CPLANE, 1, 1), (WIN, 2, 2),
-    (WIN, 1, 2), (DLAST, 2), (DCORNER, 1), (CPLANE, 1, 0), (DCORNER, 3), (WIN, 1, 1), (CPLANE, 2, 1),
-    (CCORNER, 1, 0), (DLAST, 1), (DLAST, 3), (CPLANE, 2, 0), (DLAST, 0), (CPLANE, 3, 1), (WIN, 0, 1),
-    (DWAIT,), (ATT, 0), (WIN, 0, 3), (ATT, 1), (RPLANE, 1, 0), (WIN, 2, 3), (WIN, 1, 0), (WIN, 0, 2),
-    (CCORNER, 0, 0), (WIN, 3, 3), (WIN, 3, 0), (RPLANE, 1, 1), (RPLANE, 2, 0), (CCORNER, 2, 0),
-    (CCORNER, 2, 1), (WINWAIT,), (CCORNER, 0, 1), (RCORNER, 0, 1), (RCORNER, 1, 0), (WSIBWAIT,),
-    (CCORNER, 1, 1), (RCORNER, 0, 0), (WAVE, 0, 1), (RCORNER, 2, 0), (RCORNER, 1, 1), (CPLANE, 3, 0),
-    (WAVE, 1, 0), (RPLANE, 2, 1), (RPLANE, 3, 0), (CCORNER, 3, 0), (WAVE, 1, 1), (RPLANE, 3, 1), (WAVE, 2, 0),
-    (RCORNER, 3, 0), (RCORNER, 2, 1), (WAVE, 0, 0), (CCORNER, 3, 1), (WAVE, 2, 1), (RCORNER, 3, 1),
-    (WAVE, 3, 0), (WAVE, 3, 1),
+    (DOWN,), (COWN, 0), (WIN, 3, 0), (WIN, 0, 2), (DPLANE, 1), (DPLANE, 2), (DPLANE, 3), (WIN, 1, 3),
+    (COWN, 1), (WIN, 1, 1), (DCORNER, 2), (DCORNER, 0), (DCORNER, 3), (WIN, 3, 2), (CNEAR, 0), (CMZ, 0, 1, 0),
+    (CNEAR, 1), (WIN, 0, 1), (DLAST, 3), (DCORNER, 1), (CMZ, 0, 1, 1), (WIN, 2, 2), (WIN, 2, 0), (WIN, 0, 3),
+    (WO,), (CMZ, 1, 1, 0), (DLAST, 2), (CMZ, 0, 2, 0), (WIN, 1, 0), (DLAST, 0), (DLAST, 1), (WIN, 2, 1),
+    (CMZ, 1, 1, 1), (CMZ, 0, 2, 1), (DWAIT,), (WIN, 1, 2), (ATT, 0), (WIN, 2, 3), (WIN, 3, 1), (ATT, 1),
+    (RPLANE, 1, 0), (CMZ, 1, 2, 1), (WIN, 3, 3), (RPLANE, 1, 1), (RCORNER, 0, 0), (WINWAIT,), (RPLANE, 2, 1),
+    (RPLANE, 2, 0), (CMZ, 1, 2, 0), (WSIBWAIT,), (RCORNER, 1, 1), (RCORNER, 1, 0), (WAVE, 0, 0),
+    (RCORNER, 0, 1), (RCORNER, 2, 1), (RPLANE, 3, 1), (WAVE, 1, 1), (RCORNER, 2, 0), (RPLANE, 3, 0),
+    (WAVE, 1, 0), (CMZ, 1, 3, 0), (WAVE, 2, 1), (CMZ, 0, 3, 0), (RCORNER, 3, 1), (WAVE, 2, 0), (CMZ, 1, 3, 1),
+    (RCORNER, 3, 0), (WAVE, 0, 1), (CMZ, 0, 3, 1), (WAVE, 3, 0), (WAVE, 3, 1),
 )
 TAIL_STEPS = (
-    (GFIRST, 0, 0), (GFIRST, 0, 1), (GHELP, 0, 0), (PAIR,), (GFIRST, 1, 0), (GHELP, 1, 0), (GFIRST, 2, 1),
-    (ADDPAIR,), (GHELP, 0, 1), (WIN, 0, 2), (GPLANE, 1, 0), (GFIRST, 2, 0), (GPLANE, 0, 0), (GFIRST, 1, 1),
-    (MFIRST, 0, 0), (WIN, 0, 1), (WIN, 2, 0), (MHELP, 0, 0), (GHELP, 2, 0), (WIN, 3, 1), (WIN, 0, 0),
-    (GHELP, 1, 1), (WIN, 1, 1), (GHELP, 2, 1), (GPLANE, 0, 1), (MFIRST, 0, 1), (GFIRST, 3, 0), (WIN, 3, 0),
-    (WIN, 2, 1), (GPLANE, 2, 0), (GPLANE, 1, 1), (GPLANE, 2, 1), (GFIRST, 3, 1), (GHELP, 3, 0), (MHELP, 0, 1),
-    (MFIRST, 1, 0), (WIN, 3, 2), (WIN, 2, 2), (WIN, 1, 2), (GHELP, 3, 1), (MHELP, 1, 0), (MPLANE, 0, 0),
-    (GPLANE, 3, 0), (MFIRST, 1, 1), (GPLANE, 3, 1), (MFIRST, 2, 1), (MFIRST, 2, 0), (ATT, 0), (MHELP, 1, 1),
-    (ATT, 1), (ATT, 2), (ATT, 3), (ATT, 4), (MFIRST, 3, 0), (MHELP, 2, 0), (MPLANE, 1, 0), (MPLANE, 1, 1),
-    (MPLANE, 0, 1), (WIN, 1, 0), (MFIRST, 3, 1), (ATT, 5), (MHELP, 2, 1), (DENSE,), (MPLANE, 2, 0),
-    (MHELP, 3, 0), (MHELP, 3, 1), (WIN, 3, 3), (MPLANE, 2, 1), (WIN, 1, 3), (WIN, 2, 3), (MPLANE, 3, 0),
-    (MPLANE, 3, 1),
+    (MHELP, 0, 0), (GFIRST, 0, 0), (PAIR,), (GFIRST, 2, 0), (GFIRST, 0, 1), (ADDPAIR,), (GHELP, 0, 0),
+    (MHELP, 1, 0), (MHELP, 2, 0), (GHELP, 0, 1), (MHELP, 0, 1), (GFIRST, 1, 1), (GFIRST, 1, 0),
+    (GPLANE, 0, 0), (WIN, 0, 1), (GHELP, 2, 0), (GPLANE, 0, 1), (MHELP, 3, 1), (GHELP, 1, 0), (GHELP, 1, 1),
+    (GFIRST, 2, 1), (MFIRST, 0, 0), (GPLANE, 2, 0), (GPLANE, 1, 0), (MFIRST, 0, 1), (WIN, 0, 0),
+    (GHELP, 2, 1), (GPLANE, 1, 1), (MPLANE, 0, 0), (GFIRST, 3, 1), (GFIRST, 3, 0), (MFIRST, 1, 0),
+    (MFIRST, 3, 1), (MPLANE, 0, 1), (GPLANE, 2, 1), (GHELP, 3, 1), (GHELP, 3, 0), (MPLANE, 1, 0),
+    (MFIRST, 1, 1), (WIN, 3, 3), (GPLANE, 3, 1), (MFIRST, 2, 0), (GPLANE, 3, 0), (WIN, 1, 0), (ATT, 0),
+    (MPLANE, 2, 0), (MFIRST, 3, 0), (MFIRST, 2, 1), (MHELP, 3, 0), (MPLANE, 1, 1), (WIN, 2, 2), (WIN, 2, 1),
+    (ATT, 1), (ATT, 2), (WIN, 3, 0), (WIN, 2, 3), (ATT, 3), (WIN, 1, 1), (MHELP, 1, 1), (WIN, 2, 0), (ATT, 4),
+    (ATT, 5), (MPLANE, 3, 0), (MPLANE, 2, 1), (WIN, 3, 2), (WIN, 1, 3), (DENSE,), (MHELP, 2, 1), (WIN, 1, 2),
+    (WIN, 0, 2), (WIN, 3, 1), (MPLANE, 3, 1),
 )
 
 
@@ -528,6 +531,63 @@
                 pl.when(only_if)(copy.wait_send)
 
 
+class SideSpread(Spread):
+    def side(self, p):
+        return 1 + p
+
+    def along(self, w, rel, k, p, src, first):
+        place = self.place
+        if first:
+            ways = ((2 + w, 3, 1, place.z < 3), (4 + w, 1, 3, place.z > 0))
+        else:
+            step = 2 * ((place.z - place.plane(k) + 3) // 4) - 1
+            goes = (place.z + step >= 0) & (place.z + step <= 3)
+            ways = ((2 + w, (k - step + 4) % 4, step + 4, goes),)
+        for kind, k_there, on, goes in ways:
+            self.go(kind, k, k_there, rel, k, p, src, rel, (place.plane(on), place.at[0]), goes)
+
+    def go(self, kind, at_send, k_there, rel, k, p, src, rel_there, device, only_if=None):
+        copy = pltpu.make_async_remote_copy(
+            src_ref=src,
+            dst_ref=self.there(rel_there, k_there, p, rel, k),
+            send_sem=self.send_sem.at[kind, at_send * self.packs + p],
+            recv_sem=self.recv_sem.at[rel_there, k_there * self.packs + p],
+            device_id=device,
+            device_id_type=MESH,
+        )
+        if only_if is None:
+            copy.start()
+        else:
+            pl.when(only_if)(copy.start)
+        self.started.append((copy, only_if))
+
+    def own(self, p, src):
+        side, other = self.side(p), 3 - self.side(p)
+        self.go(6, 0, 0, 0, 0, p, src, side, self.place.device(side, 0))
+        self.along(0, 0, 0, p, src, True)
+        self.go(0, 0, 0, 0, 0, p, src, other, self.place.device(other, 0))
+
+    def near(self, p):
+        side, other = self.side(p), 3 - self.side(p)
+        self.wait(side, side, 0, p)
+        src = self.here(side, 0, p)
+        self.along(1, side, 0, p, src, True)
+        self.go(1, 0, 0, side, 0, p, src, 3, self.place.device(other, 0))
+
+    def passed(self, w, j, p):
+        side, other = self.side(p), 3 - self.side(p)
+        rel, k = side * w, self.place.nearest(j)
+        self.wait(rel, rel, k, p)
+        src = self.here(rel, k, p)
+        self.along(w, rel, k, p, src, False)
+        self.go(w, k, k, rel, k, p, src, 3 if w else other, self.place.device(other, 0))
+
+    def last(self, j, p):
+        k = self.place.nearest(j)
+        for rel in (3 - self.side(p), 3):
+            self.wait(rel, rel, k, p)
+
+
 def norm_parts(values):
     center = values - jnp.mean(values, -1, keepdims=True)
     spread = jnp.mean(center * center, -1, keepdims=True)
@@ -580,11 +640,11 @@
 def front_kernel(
     pack_task, task_experts, tok, segments, w_qkv_own, w_attn_own, route_own,
     gain_one_own, bias_one_own, gain_two_own, bias_two_own, cot_own, w_in, w_out,
-    in_terms, out_terms, mixed_out, grad_out, dense_out, proj, heads, middle,
+    in_terms, out_terms, mixed_out, grad_out, dense_out, early_y, early_x, proj, heads, middle,
     dense, routed_all, cot_all, w_in_all, w_out_all, in_stage, out_stage, mixed_all, grad_all,
     turned, square, flat_ids, tall_ids, gate_row,
     cot_send, cot_recv, routed_send, routed_recv, dense_send, dense_recv,
-    core_send, core_recv, in_send, in_recv, pair_send, pair_recv, local_sem, out_sem,
+    core_send, core_recv, in_send, in_recv, pair_send, pair_recv, local_sem, out_sem, early_sem,
 ):
     place = Place()
     width, experts = tok.shape[2], route_own.shape[1]
@@ -621,7 +681,7 @@
         False,
         (dense_send, dense_recv),
     )
-    core_started, in_started, pair_started, local, outs = [], [], [], [], []
+    core_started, in_started, pair_started, local, outs, early = [], [], [], [], [], []
 
     def to_core(rel, k):
         slot = dense.at[place.index(rel, k)]
@@ -629,11 +689,13 @@
             core_started, slot, slot, core_send.at[rel, k], core_recv.at[rel, k], place.sibling
         )
 
-    def tree(ref, sems):
-        return Spread(place, block_here(ref), block_there(ref), 2, lambda j, p: p, True, sems)
-
-    cot_tree = tree(cot_all, (cot_send, cot_recv))
-    routed_tree = tree(routed_all, (routed_send, routed_recv))
+    def tree(kind, ref, sems):
+        return kind(place, block_here(ref), block_there(ref), 2, lambda j, p: p, True, sems)
+
+    cot_side = tree(SideSpread, cot_all, (cot_send, cot_recv))
+    cot_plain = tree(Spread, cot_all, (cot_send, cot_recv))
+    cot_trees = [cot_side if p in SIDE_PACKS else cot_plain for p in range(2)]
+    routed_tree = tree(Spread, routed_all, (routed_send, routed_recv))
 
     def local_copy(src, dst):
         copy = pltpu.make_async_copy(src, dst, local_sem.at[len(local)])
@@ -741,8 +803,9 @@
 
     def wave(j, p):
         at = place.nearest(j) * 2 + p
-        cot_tree.last(j, p)
-        routed_tree.last(j, p)
+        k = place.nearest(j)
+        cot_trees[p].last(j, p)
+        routed_tree.wait(2 - p, 2 - p, k, p)
         count = len(outs) // 4
         stage = count % 2
         if count >= 2:
@@ -761,17 +824,29 @@
             out_stage[stage, rel] = contract_rows(gated, cots).astype(jnp.bfloat16)
             return carry
 
-        lax.fori_loop(0, 4, one_block, 0)
+        lax.fori_loop(0, 3, one_block, 0)
+        routed_tree.wait(3, 3, k, p)
+        one_block(3, 0)
         put(in_stage.at[stage], in_terms.at[:, at])
         put(out_stage.at[stage], out_terms.at[:, at])
         put(grad_all.at[:, at], grad_out.at[:, at])
         put(mixed_all.at[:, at], mixed_out.at[:, at])
+        for i, (back_j, rel) in enumerate(EARLY):
+            if back_j == 3 - j:
+                copy = pltpu.make_async_copy(
+                    grad_all.at[2 - p if rel == 1 else rel, at],
+                    (early_y, early_x)[p].at[i],
+                    early_sem.at[p, i],
+                )
+                copy.start()
+                early.append(copy)
 
     steps = {
         DOWN: down, DPLANE: dplane, DCORNER: dcorner, DLAST: dlast, DWAIT: dwait,
         ATT: att, WIN: win, WO: wo, WINWAIT: winwait, WSIBWAIT: wsibwait, WAVE: wave,
-        COWN: lambda p: cot_tree.own(p, cot_all.at[0, p]),
-        CPLANE: cot_tree.plane, CCORNER: cot_tree.corner,
+        COWN: lambda p: cot_trees[p].own(p, cot_all.at[0, p]),
+        CPLANE: cot_plain.plane, CCORNER: cot_plain.corner,
+        CNEAR: cot_side.near, CMZ: cot_side.passed,
         RPLANE: routed_tree.plane, RCORNER: routed_tree.corner,
     }
     for name, *where in FRONT_STEPS:
@@ -779,7 +854,9 @@
     for i, copy in enumerate(outs):
         if i % 4 >= 2 or i >= len(outs) - 8:
             copy.wait()
-    for each in (dense_tree, cot_tree, routed_tree):
+    for copy in early:
+        copy.wait()
+    for each in (dense_tree, cot_side, cot_plain, routed_tree):
         each.finish()
     for copy in core_started + in_started + pair_started:
         copy.wait_send()
@@ -942,34 +1019,176 @@
             copy.wait_send()
 
 
+class Return:
+    def __init__(self, place, part, own, from_z, sems, load):
+        self.place, self.part, self.own, self.from_z = place, part, own, from_z
+        self.send_sem, self.recv_sem, self.z_sem = sems
+        self.started, self.loads = [], {}
+        for kind, j, p in self.needs:
+            rel = self.beside(p) if kind else 0
+            at = self.at(j, p)
+            self.loads[kind, j, p] = load(part.at[rel, at], own.at[kind, at])
+
+    needs = [(kind, j, p) for j in range(4) for p in range(2) for kind in (1, 0)]
+
+    def at(self, j, p):
+        return self.place.nearest(3 - j) * 2 + p
+
+    def beside(self, p):
+        return 1 + p
+
+    def go(self, kind, at, src, dst, recv_sem, device):
+        send(self.started, src, dst, self.send_sem.at[kind, at], recv_sem, device)
+
+    def mine(self, kind, j, p):
+        return self.own[kind, self.at(j, p)].astype(jnp.float32)
+
+    def along(self, kind, send_kind, j, p, ref, total):
+        place = self.place
+        k = place.nearest(3 - j)
+        step = 2 * ((place.plane(k) - place.z + 3) // 4) - 1
+        behind = self.from_z.at[kind, k * 2 + p]
+        more = (place.z - step >= 0) & (place.z - step <= 3)
+
+        @pl.when(more)
+        def add():
+            arrived(behind, self.z_sem.at[kind, k * 2 + p])
+            ref[...] = (total() + behind[...].astype(jnp.float32)).astype(jnp.bfloat16)
+
+        @pl.when(jnp.logical_not(more))
+        def first():
+            ref[...] = total().astype(jnp.bfloat16)
+
+        there = (k - step + 4) % 4
+        slot = (there + (4 - there) // 4 * (2 - 2 * step)) * 2 + p
+        self.go(
+            send_kind, k * 2 + p, ref, self.from_z.at[kind, slot], self.z_sem.at[kind, slot],
+            (place.plane(step + 4), place.at[0]),
+        )
+
+    def owned(self, kind, p, total, out):
+        out[...] = total()
+        for slot, comes in ((p, self.place.z > 0), (8 + p, self.place.z < 3)):
+
+            @pl.when(comes)
+            def add(slot=slot):
+                ref = self.from_z.at[kind, slot]
+                arrived(ref, self.z_sem.at[kind, slot])
+                out[...] += ref[...].astype(jnp.float32)
+
+    def finish(self):
+        for copy in self.started:
+            copy.wait_send()
+
+
+class PlaneFirst(Return):
+    def __init__(self, place, part, own, from_z, sems, load, corner, from_x, from_y, got):
+        self.corner, self.near, self.early = corner, (None, from_x, from_y), {}
+        for i, (j, rel) in enumerate(EARLY):
+            for p in range(2):
+                into = corner if rel == 3 else self.near[2 - p]
+                at = place.nearest(3 - j) * 2 + p
+                self.early[rel == 3, j, p] = load(got[p].at[i], into.at[at])
+        super().__init__(place, part, own, from_z, sems, load)
+
+    def here(self, far, j, p, ref, sem):
+        if (far, j, p) in self.early:
+            self.early[far, j, p].wait()
+        else:
+            arrived(ref, sem)
+
+    def first(self, j, p):
+        at, way = self.at(j, p), 2 - p
+        if (True, j, p) not in self.early:
+            self.go(
+                3, at, self.part.at[3, at], self.corner.at[at], self.recv_sem.at[3, at],
+                self.place.device(way, 0),
+            )
+        if (False, j, p) not in self.early:
+            self.go(
+                way, at, self.part.at[way, at], self.near[way].at[at], self.recv_sem.at[way, at],
+                self.place.device(way, 0),
+            )
+
+    def helped(self, j, p):
+        at, way = self.at(j, p), 1 + p
+        ref = self.corner.at[at]
+        self.loads[1, j, p].wait()
+        self.here(True, j, p, ref, self.recv_sem.at[3, at])
+        ref[...] = (ref[...].astype(jnp.float32) + self.mine(1, j, p)).astype(jnp.bfloat16)
+        self.go(
+            way, at, ref, self.near[way].at[at], self.recv_sem.at[way, at],
+            self.place.device(way, 0),
+        )
+
+    def plane(self, j, p, out):
+        at = self.at(j, p)
+        self.loads[0, j, p].wait()
+        self.here(False, j, p, self.near[2 - p].at[at], self.recv_sem.at[2 - p, at])
+        arrived(self.near[1 + p].at[at], self.recv_sem.at[1 + p, at])
+
+        def total():
+            both = self.near[1][at].astype(jnp.float32) + self.near[2][at].astype(jnp.float32)
+            return both + self.mine(0, j, p)
+
+        if j < 3:
+            self.along(0, 0, j, p, self.near[1].at[at], total)
+        else:
+            self.owned(0, p, total, out)
+
+
+class SideFirst(Return):
+    def __init__(self, place, part, own, from_z, sems, load, near, last, total):
+        super().__init__(place, part, own, from_z, sems, load)
+        self.near, self.last, self.total = near, last, total
+
+    def first(self, j, p):
+        at, way = self.at(j, p), 2 - p
+        for kind, rel in ((1, 3), (0, way)):
+            self.go(
+                kind, at, self.part.at[rel, at], self.near.at[kind, at],
+                self.recv_sem.at[kind, at], self.place.device(way, 0),
+            )
+
+    def plane(self, j, p, out):
+        at, way = self.at(j, p), 1 + p
+        for kind in (1, 0):
+            ref = self.near.at[kind, at]
+            self.loads[kind, j, p].wait()
+            arrived(ref, self.recv_sem.at[kind, at])
+
+            def total(kind=kind, ref=ref):
+                return ref[...].astype(jnp.float32) + self.mine(kind, j, p)
+
+            if j < 3:
+                self.along(kind, 2 + kind, j, p, ref, total)
+            elif kind:
+                self.owned(kind, p, total, self.total)
+                ref[...] = self.total[...].astype(jnp.bfloat16)
+                self.go(
+                    2, at, ref, self.last.at[p], self.recv_sem.at[2, p], self.place.device(way, 0)
+                )
+            else:
+                self.owned(kind, p, total, out)
+        if j == 3:
+            arrived(self.last.at[p], self.recv_sem.at[2, p])
+            out[...] += self.last[p].astype(jnp.float32)
+
+
 def tail_kernel(
     pack_task, task_experts, tok, cot, segments, proj, heads, middle, dense, grad_part, mixed_part,
-    d_in, d_out_far,
+    d_in, d_out_far, got_y, got_x,
     mixed, d_tok, d_dense, d_in_all, d_out_all,
-    g_own, g_corner, g_x, g_y, g_z, m_own, m_corner, m_x, m_y, m_z,
+    g_own, g_corner, g_x, g_y, g_z, m_own, m_near, m_last, m_z, m_total, m_out,
     total_grad, grad_mid, grad_heads, grad_qkv, acc, small_rows, turned, flat_ids, tall_ids,
     in_far, in_mine, far_dense, got_dense, part_dense, s_corner, s_x, s_y, s_z,
-    g_send, g_recv, m_send, m_recv, s_send, s_recv, in_send, in_recv,
+    g_send, g_recv, gz_recv, m_send, m_recv, mz_recv, s_send, s_recv, in_send, in_recv,
     pair_send, pair_recv, load_sem,
 ):
     place = Place()
     width = tok.shape[2]
     place.greet()
 
-    def by_pack(k, p):
-        return p
-
-    def part_of(ref):
-        return lambda rel, k, p: ref.at[rel, k * 2 + p]
-
-    grads = Collect(
-        place, part_of(grad_part), g_corner, g_x, g_y, g_z, 2, by_pack, (g_send, g_recv)
-    )
-    mixes = Collect(
-        place, part_of(mixed_part), m_corner, m_x, m_y, m_z, 2, by_pack, (m_send, m_recv)
-    )
-    planes = (2, 1, 3, 0)
-    order = [(k, p) for k in planes for p in range(2)]
     loads = []
 
     def load(src, dst):
@@ -978,27 +1197,16 @@
         loads.append(copy)
         return copy
 
-    def load_parts(ref, own):
-        waits = {}
-        for k, p in order:
-            at = k * 2 + p
-            waits["helped", k, p] = load(ref.at[1 + p, at], own.at[1, at])
-        for k, p in order:
-            at = k * 2 + p
-            waits["plane", k, p] = load(ref.at[0, at], own.at[0, at])
-        return waits
-
-    g_waits = load_parts(grad_part, g_own)
+    grads = PlaneFirst(
+        place, grad_part, g_own, g_z, (g_send, g_recv, gz_recv), load, g_corner, g_x, g_y,
+        (got_y, got_x),
+    )
     in_load = load(d_in.at[place.core], in_mine)
-    m_waits = load_parts(mixed_part, m_own)
+    mixes = SideFirst(
+        place, mixed_part, m_own, m_z, (m_send, m_recv, mz_recv), load, m_near, m_last, m_total
+    )
     pair_started, in_started, kept = [], [], {}
-
-    def mine(waits, own, kind, k, p):
-        def get():
-            waits[kind, k, p].wait()
-            return own[0 if kind == "plane" else 1, k * 2 + p]
-
-        return get
+    planes = (2, 1, 3, 0)
 
     same_documents(segments, flat_ids, tall_ids)
     small = dense[:, :, 4 * width : 4 * width + SIDE].reshape(width, SIDE)
@@ -1038,19 +1246,10 @@
             in_send.at[rel, k], in_recv.at[rel, back(k)], place.device(rel, k),
         )
 
-    def plane_of(tree, waits, own_parts, keep):
-        def run(j, p):
-            got = tree.plane(planes[j], p, mine(waits, own_parts, "plane", planes[j], p))
-            if got is not None:
-                keep(p, got)
-
-        return run
-
-    def keep_grad(p, got):
-        total_grad[p] = got
-
-    def keep_mixed(p, got):
-        mixed[p] = (middle[p] + got).astype(jnp.bfloat16)
+    def mplane(j, p):
+        mixes.plane(j, p, m_out)
+        if j == 3:
+            mixed[p] = (middle[p] + m_out[...]).astype(jnp.bfloat16)
 
     def add_to(p, columns, value):
         if p == 0:
@@ -1189,16 +1388,9 @@
         d_dense[...] = sums.plane(0, 0, lambda: got_dense[place.chip(0, 0)])
 
     steps = {
-        GFIRST: lambda j, p: (grads.opposite(planes[j], p), grads.straight(planes[j], p)),
-        MFIRST: lambda j, p: (mixes.opposite(planes[j], p), mixes.straight(planes[j], p)),
-        GHELP: lambda j, p: grads.helped(
-            planes[j], p, mine(g_waits, g_own, "helped", planes[j], p)
-        ),
-        MHELP: lambda j, p: mixes.helped(
-            planes[j], p, mine(m_waits, m_own, "helped", planes[j], p)
-        ),
-        GPLANE: plane_of(grads, g_waits, g_own, keep_grad),
-        MPLANE: plane_of(mixes, m_waits, m_own, keep_mixed),
+        GFIRST: grads.first, GHELP: grads.helped,
+        GPLANE: lambda j, p: grads.plane(j, p, total_grad.at[p]),
+        MFIRST: mixes.first, MPLANE: mplane, MHELP: lambda j, p: None,
         PAIR: pair, ADDPAIR: addpair, WIN: win, ATT: att, DENSE: dense_step,
     }
     for name, *where in TAIL_STEPS:
@@ -1276,17 +1468,21 @@
     def held(shape):
         return pltpu.VMEM(shape.shape, shape.dtype)
 
-    in_terms, out_terms, mixed_part, grad_part, dense, proj, heads, middle = pl.pallas_call(
+    early_blocks = flat((len(EARLY), ROWS, width), low)
+    (
+        in_terms, out_terms, mixed_part, grad_part, dense, early_y, early_x, proj, heads, middle,
+    ) = pl.pallas_call(
         front_kernel,
         out_shape=(
             in_sums, out_sums, blocks, blocks,
             flat((32, slab_in, dense_width), low),
+            early_blocks, early_blocks,
             flat((packs, ROWS, 3 * width), low),
             flat((packs, ROWS, width), low),
             flat((packs, ROWS, width), full),
         ),
         in_specs=[smem] * 2 + [vmem] * 10 + [any_space] * 2,
-        out_specs=(any_space,) * 5 + (vmem,) * 3,
+        out_specs=(any_space,) * 7 + (vmem,) * 3,
         scratch_shapes=[
             pltpu.VMEM((32, slab_in, dense_width), low),
             held(blocks), held(blocks),
@@ -1300,9 +1496,9 @@
             pltpu.VMEM((8, 2 * SIDE), full),
             pltpu.VMEM((2 * SIDE, 8), full),
             pltpu.VMEM((8, width), full),
-            dma((5, 8)), dma((4, 8)), dma((5, 8)), dma((4, 8)), dma((5, 4)), dma((4, 4)),
+            dma((7, 8)), dma((4, 8)), dma((5, 8)), dma((4, 8)), dma((5, 4)), dma((4, 4)),
             dma((4, 4)), dma((4, 4)), dma((4, 4)), dma((4, 4)), dma((2,)), dma((2,)), dma((3,)),
-            dma((32,)),
+            dma((32,)), dma((2, len(EARLY))),
         ],
         compiler_params=pltpu.CompilerParams(
             collective_id=0, has_side_effects=True, vmem_limit_bytes=60 << 20
@@ -1312,6 +1508,10 @@
         pack_task, task_experts, tokens, segment_ids, w_qkv, w_attn_out, w_router,
         norm1_gain, norm1_bias, norm2_gain, norm2_bias, cotangent, w_expert_in, w_expert_out,
     )
+
+    across = lax.axis_size("gy")
+    got_y = lax.ppermute(early_y, "gy", [(i, i ^ 4) for i in range(across)])
+    got_x = lax.ppermute(early_x, "gy", [(i, i ^ 2) for i in range(across)])
 
     def by_expert(rows):
         return pl.BlockSpec((experts // 8, rows, width), lambda e, *unused: (e, 0, 0))
@@ -1339,6 +1539,9 @@
             flat((experts, slab_out, width), low),
         ),
         compiler_params=pltpu.CompilerParams(vmem_limit_bytes=60 << 20),
+        cost_estimate=pl.CostEstimate(
+            flops=10**10, bytes_accessed=40 * 10**6, transcendentals=0
+        ),
         name="sums",
     )(pack_task, task_experts, where, in_terms, out_terms)
 
@@ -1354,11 +1557,17 @@
             flat((experts, slab_in, hidden), low),
             flat((experts, slab_out, width), low),
         ),
-        in_specs=[smem] * 2 + [vmem] * 7 + [any_space] * 4,
+        in_specs=[smem] * 2 + [vmem] * 7 + [any_space] * 6,
         out_specs=(vmem,) * 3 + (any_space,) * 2,
         scratch_shapes=[
-            pltpu.VMEM((2, 4 * packs, ROWS, width), low), parts, parts, parts, parts,
-            pltpu.VMEM((2, 4 * packs, ROWS, width), low), parts, parts, parts, parts,
+            pltpu.VMEM((2, 4 * packs, ROWS, width), low), parts, parts, parts,
+            pltpu.VMEM((1, 5 * packs, ROWS, width), low),
+            pltpu.VMEM((2, 4 * packs, ROWS, width), low),
+            pltpu.VMEM((2, 4 * packs, ROWS, width), low),
+            pltpu.VMEM((packs, ROWS, width), low),
+            pltpu.VMEM((2, 5 * packs, ROWS, width), low),
+            pltpu.VMEM((ROWS, width), full),
+            pltpu.VMEM((ROWS, width), full),
             pltpu.VMEM((packs, ROWS, width), full),
             pltpu.VMEM((ROWS, width), full),
             pltpu.VMEM((ROWS, width), low),
@@ -1373,8 +1582,8 @@
             sliced, sliced,
             pltpu.VMEM((16, slab_in, dense_width), full),
             slices, slices, slices, slices,
-            dma((4, 8)), dma((4, 8)), dma((4, 8)), dma((4, 8)), dma((4, 4)), dma((4, 4)),
-            dma((4, 4)), dma((4, 4)), dma((3,)), dma((3,)), dma((40,)),
+            dma((4, 8)), dma((4, 8)), dma((1, 10)), dma((4, 8)), dma((4, 8)), dma((2, 10)),
+            dma((4, 4)), dma((4, 4)), dma((4, 4)), dma((4, 4)), dma((3,)), dma((3,)), dma((48,)),
         ],
         compiler_params=pltpu.CompilerParams(
             collective_id=1, has_side_effects=True, vmem_limit_bytes=60 << 20
@@ -1382,7 +1591,7 @@
         name="tail",
     )(
         pack_task, task_experts, tokens, cotangent, segment_ids, proj, heads, middle, dense,
-        grad_part, mixed_part, d_in, d_out_far,
+        grad_part, mixed_part, d_in, d_out_far, got_y, got_x,
     )
 
     group = experts // 2

time: 376 us -> 352 us (0.936)
  Pallas kernels: 374 us -> 344 us
    pallas_call x1, Pallas kernels: 177 us -> 157 us  [shards_fast(): pl.pallas_call(tail_kernel, out_shape=(flat((packs, ROWS, width), low), f...]
    pallas_call x1, Pallas kernels: 175 us -> 166 us  [shards_fast(): pl.pallas_call(front_kernel, out_shape=(in_sums, out_sums, blocks, blocks...]
  transfers between devices with their start and end apart: 0 -> 2, of which waited for: 0 -> 0; matrix products, arithmetic and copies ran while one was open for 0% -> 0% of each run, Pallas kernels for 0% -> 4%
where the time goes in v3:
time: 352 us; the launch traced here: 350 us
  Pallas kernels  344 us (98%)
    pallas_call x1, Pallas kernels, shards_fast(): pl.pallas_call(front_kernel, out_shape=(in_sums, out_sums, blocks, blocks...  166 us
    pallas_call x1, Pallas kernels, shards_fast(): pl.pallas_call(tail_kernel, out_shape=(flat((packs, ROWS, width), low), f...  157 us
    pallas_call x1, Pallas kernels, shards_fast(): pl.pallas_call(sum_kernel, grid_spec=pltpu.PrefetchScalarGridSpec(num_sca...  14 us
    pallas_call x1, Pallas kernels, shards_fast(): pl.pallas_call(last_kernel, grid=(2,), in_specs=[whole(packs, ROWS, width...  7.11 us
  transfers between devices with their start and end apart: 2, of which 0 were waited for; matrix products, arithmetic and copies ran while one was open for 0% of the time, Pallas kernels for 4%

profile of v3, /device:TPU:8, one launch (start us, length us, event | category | flops | bytes accessed | tf_op | source)
XLA Modules:
  0.0 349.8 jit_solution(5724136572423258661)
XLA Ops:
  0.6 1.4 copy.27.task_experts
  2.0 165.8 %front.1 = (bf16[4,8,512,256]{3,2,1,0:T(8,128)(2,1)}, bf16[4,8,256,512]{3,2,1,0:T(8,128)(2,1)}, bf16[4,8,224,512]{3,2,1,0:T(8,128)(2,1)}, bf16[4,8,224,512]{3,2,...) custom-call(s32[64]{0:T(128)} %pack_task.5, ...), custom_call_target="tpu_custom_call" | custom-call | tf_op jit(solution)/shard_map/front/pallas_call | solution.py:1474
  167.8 2.1 collective-permute-start
  169.9 0.3 collective-permute-start.1
  170.2 0.6 pad_add_fusion.where
  170.8 14.0 %sums.1 = (bf16[2,16,32,16,128]{4,3,2,1,0:T(8,128)(2,1)}, f32[32,64,512]{2,1,0:T(8,128)}, bf16[32,64,512]{2,1,0:T(8,128)(2,1)}) custom-call(s32[64]{0:T(128)} %pack_task.5, s32[24,2]{1,0:T(8,128)} %copy.27.task_experts, s32[3]{0:T(128)} %pad_add_fusion.where, bf16[4,8,512,256]{3,2,1,0:T(8,128)(2,1)} %get-tuple-element.35.in_terms, ...), custom_call_target="tpu_custom_call" | custom-call | flops 10000000000 | bytes 40000000 | tf_op jit(solution)/shard_map/sums/pallas_call | solution.py:1519
  184.8 0.0 collective-permute-done.got_y
  184.8 0.0 copy-start
  184.8 0.0 collective-permute-done.1.got_x
  184.8 0.0 copy-start.1
  184.8 0.8 copy-done
  185.5 0.2 copy-done.1
  185.7 157.0 %tail.1 = (bf16[2,224,512]{2,1,0:T(8,128)(2,1)}, bf16[2,224,512]{2,1,0:T(8,128)(2,1)}, f32[16,2176]{1,0:T(8,128)}, bf16[32,16,2048]{2,1,0:T(8,128)(2,1)}, bf16[32,64,512]{2,1,0:T(8,128)(2,1)}) custom-call(s32[64]{0:T(128)} %pack_task.5, s32[24,2]{1,0:T(8,128)} %copy.27.task_experts, bf16[2,216,512]{2,1,0:T(8,128)(2,1)} %tok.3, bf16[2,216,512]{2,1,0:T(8,128)(2,1)} %cot.1, ...), custom_call_target="tpu_custom_call" | custom-call | tf_op jit(solution)/shard_map/tail/pallas_call | solution.py:1551
  342.7 7.1 %last.1 = (bf16[2,216,512]{2,1,0:T(8,128)(2,1)}, bf16[2,216,512]{2,1,0:T(8,128)(2,1)}, f32[16,1536]{1,0:T(8,128)}, f32[16,512]{1,0:T(8,128)}, f32[16,32]{1,0:T(8...) custom-call(bf16[2,224,512]{2,1,0:T(8,128)(2,1)} %get-tuple-element., ...), custom_call_target="tpu_custom_call" | custom-call | tf_op jit(solution)/shard_map/last/pallas_call | solution.py:1605
Async XLA Ops:
  167.8 16.9 %collective-permute-start = (bf16[2,224,512]{2,1,0:T(8,128)(2,1)}, bf16[2,224,512]{2,1,0:T(8,128)(2,1)S(1)}, u32[]{:S(2)}, u32[]{:S(2)}) collective-permute-start(bf16[2,224,512]{2,1,0:T(8,128)(2,1)} %get-tuple-element.39), channel_id=1, source_target_pairs={{0,4},{1,5},{2,6},{3,7},{4,0},{5,1},{6,2},{7,3},{8,12},{9,13},{10,... | collective-permute-start | bytes 1376264 | tf_op jit(solution)/shard_map/ppermute | solution.py:1513
  169.9 14.9 %collective-permute-start.1 = (bf16[2,224,512]{2,1,0:T(8,128)(2,1)}, bf16[2,224,512]{2,1,0:T(8,128)(2,1)S(1)}, u32[]{:S(2)}, u32[]{:S(2)}) collective-permute-start(bf16[2,224,512]{2,1,0:T(8,128)(2,1)} %get-tuple-element.40), channel_id=1, source_target_pairs={{0,2},{1,3},{2,0},{3,1},{4,6},{5,7},{6,4},{7,5},{8,10},{9,11},{10,... | collective-permute-start | bytes 1376264 | tf_op jit(solution)/shard_map/ppermute | solution.py:1514
  184.8 0.8 copy-start
  184.8 0.9 copy-start.1

commit v4 on v3

--- a/solution.py
+++ b/solution.py
@@ -368,29 +368,29 @@
 EARLY = ((0, 3), (1, 3))
 
 FRONT_STEPS = (
-    (DOWN,), (COWN, 0), (WIN, 3, 0), (WIN, 0, 2), (DPLANE, 1), (DPLANE, 2), (DPLANE, 3), (WIN, 1, 3),
-    (COWN, 1), (WIN, 1, 1), (DCORNER, 2), (DCORNER, 0), (DCORNER, 3), (WIN, 3, 2), (CNEAR, 0), (CMZ, 0, 1, 0),
-    (CNEAR, 1), (WIN, 0, 1), (DLAST, 3), (DCORNER, 1), (CMZ, 0, 1, 1), (WIN, 2, 2), (WIN, 2, 0), (WIN, 0, 3),
-    (WO,), (CMZ, 1, 1, 0), (DLAST, 2), (CMZ, 0, 2, 0), (WIN, 1, 0), (DLAST, 0), (DLAST, 1), (WIN, 2, 1),
-    (CMZ, 1, 1, 1), (CMZ, 0, 2, 1), (DWAIT,), (WIN, 1, 2), (ATT, 0), (WIN, 2, 3), (WIN, 3, 1), (ATT, 1),
-    (RPLANE, 1, 0), (CMZ, 1, 2, 1), (WIN, 3, 3), (RPLANE, 1, 1), (RCORNER, 0, 0), (WINWAIT,), (RPLANE, 2, 1),
-    (RPLANE, 2, 0), (CMZ, 1, 2, 0), (WSIBWAIT,), (RCORNER, 1, 1), (RCORNER, 1, 0), (WAVE, 0, 0),
-    (RCORNER, 0, 1), (RCORNER, 2, 1), (RPLANE, 3, 1), (WAVE, 1, 1), (RCORNER, 2, 0), (RPLANE, 3, 0),
-    (WAVE, 1, 0), (CMZ, 1, 3, 0), (WAVE, 2, 1), (CMZ, 0, 3, 0), (RCORNER, 3, 1), (WAVE, 2, 0), (CMZ, 1, 3, 1),
-    (RCORNER, 3, 0), (WAVE, 0, 1), (CMZ, 0, 3, 1), (WAVE, 3, 0), (WAVE, 3, 1),
+    (DOWN,), (WIN, 3, 2), (WIN, 2, 0), (COWN, 1), (COWN, 0), (DPLANE, 1), (CMZ, 0, 1, 1), (WIN, 0, 2),
+    (DPLANE, 2), (DPLANE, 3), (CNEAR, 1), (CNEAR, 0), (WIN, 0, 1), (WIN, 1, 1), (CMZ, 0, 1, 0), (WIN, 1, 3),
+    (WIN, 1, 0), (WO,), (DCORNER, 0), (DCORNER, 1), (DCORNER, 3), (DCORNER, 2), (WIN, 3, 0), (DLAST, 0),
+    (CMZ, 1, 1, 1), (WIN, 2, 1), (CMZ, 1, 1, 0), (WIN, 2, 2), (DLAST, 3), (CMZ, 0, 2, 0), (WIN, 2, 3),
+    (WIN, 3, 1), (CMZ, 0, 2, 1), (DLAST, 1), (DLAST, 2), (DWAIT,), (WIN, 1, 2), (ATT, 0), (RCORNER, 0, 0),
+    (ATT, 1), (RPLANE, 1, 0), (CMZ, 1, 2, 1), (WIN, 3, 3), (RPLANE, 1, 1), (WIN, 0, 3), (RCORNER, 0, 1),
+    (RCORNER, 1, 0), (WINWAIT,), (RPLANE, 2, 1), (RPLANE, 2, 0), (RCORNER, 1, 1), (CMZ, 1, 2, 0), (WSIBWAIT,),
+    (WAVE, 0, 0), (CMZ, 0, 3, 0), (WAVE, 1, 0), (RCORNER, 2, 1), (RPLANE, 3, 1), (WAVE, 1, 1),
+    (RCORNER, 2, 0), (RPLANE, 3, 0), (WAVE, 0, 1), (CMZ, 1, 3, 0), (CMZ, 0, 3, 1), (RCORNER, 3, 1),
+    (WAVE, 2, 1), (CMZ, 1, 3, 1), (RCORNER, 3, 0), (WAVE, 2, 0), (WAVE, 3, 0), (WAVE, 3, 1),
 )
 TAIL_STEPS = (
-    (MHELP, 0, 0), (GFIRST, 0, 0), (PAIR,), (GFIRST, 2, 0), (GFIRST, 0, 1), (ADDPAIR,), (GHELP, 0, 0),
-    (MHELP, 1, 0), (MHELP, 2, 0), (GHELP, 0, 1), (MHELP, 0, 1), (GFIRST, 1, 1), (GFIRST, 1, 0),
-    (GPLANE, 0, 0), (WIN, 0, 1), (GHELP, 2, 0), (GPLANE, 0, 1), (MHELP, 3, 1), (GHELP, 1, 0), (GHELP, 1, 1),
-    (GFIRST, 2, 1), (MFIRST, 0, 0), (GPLANE, 2, 0), (GPLANE, 1, 0), (MFIRST, 0, 1), (WIN, 0, 0),
-    (GHELP, 2, 1), (GPLANE, 1, 1), (MPLANE, 0, 0), (GFIRST, 3, 1), (GFIRST, 3, 0), (MFIRST, 1, 0),
-    (MFIRST, 3, 1), (MPLANE, 0, 1), (GPLANE, 2, 1), (GHELP, 3, 1), (GHELP, 3, 0), (MPLANE, 1, 0),
-    (MFIRST, 1, 1), (WIN, 3, 3), (GPLANE, 3, 1), (MFIRST, 2, 0), (GPLANE, 3, 0), (WIN, 1, 0), (ATT, 0),
-    (MPLANE, 2, 0), (MFIRST, 3, 0), (MFIRST, 2, 1), (MHELP, 3, 0), (MPLANE, 1, 1), (WIN, 2, 2), (WIN, 2, 1),
-    (ATT, 1), (ATT, 2), (WIN, 3, 0), (WIN, 2, 3), (ATT, 3), (WIN, 1, 1), (MHELP, 1, 1), (WIN, 2, 0), (ATT, 4),
-    (ATT, 5), (MPLANE, 3, 0), (MPLANE, 2, 1), (WIN, 3, 2), (WIN, 1, 3), (DENSE,), (MHELP, 2, 1), (WIN, 1, 2),
-    (WIN, 0, 2), (WIN, 3, 1), (MPLANE, 3, 1),
+    (GFIRST, 0, 0), (MHELP, 2, 0), (GFIRST, 1, 0), (MHELP, 3, 0), (PAIR,), (GHELP, 0, 0), (GFIRST, 0, 1),
+    (GHELP, 1, 0), (GHELP, 0, 1), (GFIRST, 2, 0), (ADDPAIR,), (WIN, 0, 1), (GFIRST, 1, 1), (GFIRST, 2, 1),
+    (GPLANE, 0, 0), (MFIRST, 0, 1), (GHELP, 1, 1), (MFIRST, 0, 0), (GPLANE, 0, 1), (GPLANE, 1, 0),
+    (WIN, 0, 0), (MHELP, 2, 1), (GFIRST, 3, 1), (GHELP, 2, 1), (GHELP, 2, 0), (GPLANE, 1, 1), (GFIRST, 3, 0),
+    (MFIRST, 1, 1), (MHELP, 3, 1), (MPLANE, 0, 0), (GPLANE, 2, 1), (MFIRST, 1, 0), (GHELP, 3, 0),
+    (MPLANE, 0, 1), (MHELP, 0, 1), (GPLANE, 2, 0), (MFIRST, 2, 0), (MPLANE, 1, 0), (MFIRST, 2, 1),
+    (MFIRST, 3, 1), (GHELP, 3, 1), (MPLANE, 1, 1), (WIN, 3, 1), (MPLANE, 2, 0), (GPLANE, 3, 0), (WIN, 1, 0),
+    (GPLANE, 3, 1), (MFIRST, 3, 0), (ATT, 0), (WIN, 3, 3), (ATT, 1), (MPLANE, 2, 1), (ATT, 2), (MHELP, 0, 0),
+    (MHELP, 1, 0), (MHELP, 1, 1), (ATT, 3), (WIN, 2, 3), (WIN, 1, 2), (WIN, 3, 2), (WIN, 2, 1), (WIN, 2, 2),
+    (ATT, 4), (ATT, 5), (MPLANE, 3, 0), (WIN, 1, 1), (WIN, 3, 0), (WIN, 1, 3), (WIN, 2, 0), (WIN, 0, 2),
+    (MPLANE, 3, 1), (DENSE,),
 )
 
 
@@ -890,11 +890,11 @@
 
 
 def sum_kernel(
-    pack_task, task_experts, where, in_terms, out_terms, d_in, d_out_own, d_out_far, heads, nexts,
+    pack_task, task_experts, in_terms, out_terms, d_in, d_out_own, d_out_far, heads, nexts,
     total_in, total_out,
 ):
-    group = d_out_own.shape[0]
-    experts = group * pl.num_programs(0)
+    z, g = lax.axis_index("gx"), lax.axis_index("gy")
+    experts = d_out_own.shape[0]
     slots = in_terms.shape[0] * in_terms.shape[1]
 
     @pl.when(pl.program_id(0) == 0)
@@ -904,13 +904,12 @@
             return carry
 
         lax.fori_loop(0, experts, clear, 0)
-        g = where[1]
         step_x, step_y = 2 - 4 * ((g // 2) % 2), 4 - 8 * (g // 4)
 
         def one(slot, carry):
             rel, k, p = slot // 8, (slot // 2) % 4, slot % 2
             at = g + step_x * (rel % 2) + step_y * (rel // 2)
-            task = pack_task[(((where[0] + k) % 4) * 8 + at) * 2 + p]
+            task = pack_task[(((z + k) % 4) * 8 + at) * 2 + p]
             for i in range(2):
                 e = task_experts[task, i]
                 nexts[slot * 2 + i] = heads[e]
@@ -933,11 +932,11 @@
         total_out[...] += new_out
         return nexts[use]
 
-    own = pl.ds(pl.multiple_of(where[2] * HEAD, HEAD), HEAD)
-    far = pl.ds(pl.multiple_of((1 - where[2]) * HEAD, HEAD), HEAD)
+    own = pl.ds(pl.multiple_of((g % 2) * HEAD, HEAD), HEAD)
+    far = pl.ds(pl.multiple_of((1 - g % 2) * HEAD, HEAD), HEAD)
 
     def one_expert(i, carry):
-        head = heads[pl.program_id(0) * group + i]
+        head = heads[i]
 
         @pl.when(head < 0)
         def unused():
@@ -949,14 +948,14 @@
             total_in[...], total_out[...] = terms(head)
             lax.while_loop(lambda use: use >= 0, add_terms, nexts[head])
 
-        low = total_in[...].astype(jnp.bfloat16).reshape(16, 2, 16, SIDE)
+        low = total_in[...].astype(jnp.bfloat16).reshape(-1, 2, 16, SIDE)
         d_in[0, :, i] = low[:, 0]
         d_in[1, :, i] = low[:, 1]
-        d_out_own[i] = total_out[own, :]
+        d_out_own[i] = total_out[own, :].astype(jnp.bfloat16)
         d_out_far[i] = total_out[far, :].astype(jnp.bfloat16)
         return carry
 
-    lax.fori_loop(0, group, one_expert, 0)
+    lax.fori_loop(0, experts, one_expert, 0)
 
 
 class Collect:
@@ -1428,7 +1427,7 @@
             ref[...] = rows[GAIN_ONE + i]
 
     d_in[...] = d_in_low[...].astype(jnp.float32)
-    d_out[...] = d_out_own[...] + d_out_far[...].astype(jnp.float32)
+    d_out[...] = d_out_own[...].astype(jnp.float32) + d_out_far[...].astype(jnp.float32)
 
 
 def shards_fast(
@@ -1457,9 +1456,6 @@
     low, full = jnp.bfloat16, jnp.float32
     flat = jax.ShapeDtypeStruct
     dma = pltpu.SemaphoreType.DMA
-
-    z, g = lax.axis_index("gx"), lax.axis_index("gy")
-    where = jnp.stack([z, g, g % 2])
 
     blocks = flat((4, 4 * packs, ROWS, width), low)
     in_sums = flat((4, 4 * packs, width, 2 * SIDE), low)
@@ -1513,29 +1509,32 @@
     got_y = lax.ppermute(early_y, "gy", [(i, i ^ 4) for i in range(across)])
     got_x = lax.ppermute(early_x, "gy", [(i, i ^ 2) for i in range(across)])
 
-    def by_expert(rows):
-        return pl.BlockSpec((experts // 8, rows, width), lambda e, *unused: (e, 0, 0))
-
+    part = width // 2
+
+    by_columns = pl.BlockSpec((experts, slab_out, part), lambda i, *unused: (0, 0, i))
     d_in, d_out_own, d_out_far = pl.pallas_call(
         sum_kernel,
         grid_spec=pltpu.PrefetchScalarGridSpec(
-            num_scalar_prefetch=3,
-            grid=(8,),
-            in_specs=[vmem] * 2,
+            num_scalar_prefetch=2,
+            grid=(2,),
+            in_specs=[
+                pl.BlockSpec((4, 4 * packs, part, 2 * SIDE), lambda i, *unused: (0, 0, i, 0)),
+                pl.BlockSpec((4, 4 * packs, 2 * SIDE, part), lambda i, *unused: (0, 0, 0, i)),
+            ],
             out_specs=[
-                pl.BlockSpec((2, 16, experts // 8, slab_in, SIDE), lambda e, *unused: (0, 0, e, 0, 0)),
-                by_expert(slab_out), by_expert(slab_out),
+                pl.BlockSpec((2, 8, experts, slab_in, SIDE), lambda i, *unused: (0, i, 0, 0, 0)),
+                by_columns, by_columns,
             ],
             scratch_shapes=[
                 pltpu.SMEM((experts,), jnp.int32),
                 pltpu.SMEM((32 * packs,), jnp.int32),
-                pltpu.VMEM((width, SIDE), full),
-                pltpu.VMEM((SIDE, width), full),
+                pltpu.VMEM((part, SIDE), full),
+                pltpu.VMEM((SIDE, part), full),
             ],
         ),
         out_shape=(
             flat((2, 16, experts, slab_in, SIDE), low),
-            flat((experts, slab_out, width), full),
+            flat((experts, slab_out, width), low),
             flat((experts, slab_out, width), low),
         ),
         compiler_params=pltpu.CompilerParams(vmem_limit_bytes=60 << 20),
@@ -1543,7 +1542,7 @@
             flops=10**10, bytes_accessed=40 * 10**6, transcendentals=0
         ),
         name="sums",
-    )(pack_task, task_experts, where, in_terms, out_terms)
+    )(pack_task, task_experts, in_terms, out_terms)
 
     parts = pltpu.VMEM((4 * packs, ROWS, width), low)
     slices = pltpu.VMEM((4, slab_in, dense_width), low)

time: 352 us -> 338 us (0.960)
  Pallas kernels: 344 us -> 330 us
    pallas_call x1, Pallas kernels: 157 us -> 151 us  [shards_fast(): pl.pallas_call(tail_kernel, out_shape=(flat((packs, ROWS, width), low), f...]
    pallas_call x1, Pallas kernels: 166 us -> 160 us  [shards_fast(): pl.pallas_call(front_kernel, out_shape=(in_sums, out_sums, blocks, blocks...]
where the time goes in v4:
time: 338 us; the launch traced here: 335 us
  Pallas kernels  330 us (98%)
    pallas_call x1, Pallas kernels, shards_fast(): pl.pallas_call(front_kernel, out_shape=(in_sums, out_sums, blocks, blocks...  160 us
    pallas_call x1, Pallas kernels, shards_fast(): pl.pallas_call(tail_kernel, out_shape=(flat((packs, ROWS, width), low), f...  151 us
    pallas_call x1, Pallas kernels, shards_fast(): pl.pallas_call(sum_kernel, grid_spec=pltpu.PrefetchScalarGridSpec(num_sca...  12.6 us
  transfers between devices with their start and end apart: 2, of which 0 were waited for; matrix products, arithmetic and copies ran while one was open for 0% of the time, Pallas kernels for 4%

profile of v4, /device:TPU:8, one launch (start us, length us, event | category | flops | bytes accessed | tf_op | source)
XLA Modules:
  0.0 335.4 jit_solution(8159575049067956783)
XLA Ops:
  0.6 1.4 copy.27.task_experts
  2.0 160.1 %front.1 = (bf16[4,8,512,256]{3,2,1,0:T(8,128)(2,1)}, bf16[4,8,256,512]{3,2,1,0:T(8,128)(2,1)}, bf16[4,8,224,512]{3,2,1,0:T(8,128)(2,1)}, bf16[4,8,224,512]{3,2,...) custom-call(s32[64]{0:T(128)} %pack_task.5, ...), custom_call_target="tpu_custom_call" | custom-call | tf_op jit(solution)/shard_map/front/pallas_call | solution.py:1470
  162.1 1.3 collective-permute-start
  163.4 1.2 collective-permute-start.1
  164.6 12.6 %sums.1 = (bf16[2,16,32,16,128]{4,3,2,1,0:T(8,128)(2,1)}, bf16[32,64,512]{2,1,0:T(8,128)(2,1)}, bf16[32,64,512]{2,1,0:T(8,128)(2,1)}) custom-call(s32[64]{0:T(128)} %pack_task.5, s32[24,2]{1,0:T(8,128)} %copy.27.task_experts, bf16[4,8,512,256]{3,2,1,0:T(8,128)(2,1)} %get-tuple-element.35.in_terms, bf16[4,8,256,512]{3,2,1,0:T(8,128)(2,1)} %get-tuple-element.36.out_terms), custom_call_target="tpu_custom_call" | custom-call | flops 10000000000 | bytes 40000000 | tf_op jit(solution)/shard_map/sums/pallas_call | solution.py:1515
  177.2 0.0 collective-permute-done.got_y
  177.2 0.0 copy-start
  177.2 0.0 collective-permute-done.1.got_x
  177.2 0.0 copy-start.1
  177.2 0.7 copy-done
  178.0 0.2 copy-done.1
  178.1 150.7 %tail.1 = (bf16[2,224,512]{2,1,0:T(8,128)(2,1)}, bf16[2,224,512]{2,1,0:T(8,128)(2,1)}, f32[16,2176]{1,0:T(8,128)}, bf16[32,16,2048]{2,1,0:T(8,128)(2,1)}, bf16[32,64,512]{2,1,0:T(8,128)(2,1)}) custom-call(s32[64]{0:T(128)} %pack_task.5, s32[24,2]{1,0:T(8,128)} %copy.27.task_experts, bf16[2,216,512]{2,1,0:T(8,128)(2,1)} %tok.3, bf16[2,216,512]{2,1,0:T(8,128)(2,1)} %cot.1, ...), custom_call_target="tpu_custom_call" | custom-call | tf_op jit(solution)/shard_map/tail/pallas_call | solution.py:1550
  328.9 6.5 %last.1 = (bf16[2,216,512]{2,1,0:T(8,128)(2,1)}, bf16[2,216,512]{2,1,0:T(8,128)(2,1)}, f32[16,1536]{1,0:T(8,128)}, f32[16,512]{1,0:T(8,128)}, f32[16,32]{1,0:T(8...) custom-call(bf16[2,224,512]{2,1,0:T(8,128)(2,1)} %get-tuple-element., ...), custom_call_target="tpu_custom_call" | custom-call | tf_op jit(solution)/shard_map/last/pallas_call | solution.py:1604
Async XLA Ops:
  162.1 15.1 %collective-permute-start = (bf16[2,224,512]{2,1,0:T(8,128)(2,1)}, bf16[2,224,512]{2,1,0:T(8,128)(2,1)S(1)}, u32[]{:S(2)}, u32[]{:S(2)}) collective-permute-start(bf16[2,224,512]{2,1,0:T(8,128)(2,1)} %get-tuple-element.39), channel_id=1, source_target_pairs={{0,4},{1,5},{2,6},{3,7},{4,0},{5,1},{6,2},{7,3},{8,12},{9,13},{10,... | collective-permute-start | bytes 1376264 | tf_op jit(solution)/shard_map/ppermute | solution.py:1509
  163.4 13.8 %collective-permute-start.1 = (bf16[2,224,512]{2,1,0:T(8,128)(2,1)}, bf16[2,224,512]{2,1,0:T(8,128)(2,1)S(1)}, u32[]{:S(2)}, u32[]{:S(2)}) collective-permute-start(bf16[2,224,512]{2,1,0:T(8,128)(2,1)} %get-tuple-element.40), channel_id=1, source_target_pairs={{0,2},{1,3},{2,0},{3,1},{4,6},{5,7},{6,4},{7,5},{8,10},{9,11},{10,... | collective-permute-start | bytes 1376264 | tf_op jit(solution)/shard_map/ppermute | solution.py:1510
  177.2 0.8 copy-start
  177.2 0.9 copy-start.1

commit v5 on v4

--- a/solution.py
+++ b/solution.py
@@ -368,7 +368,7 @@
 EARLY = ((0, 3), (1, 3))
 
 FRONT_STEPS = (
-    (DOWN,), (WIN, 3, 2), (WIN, 2, 0), (COWN, 1), (COWN, 0), (DPLANE, 1), (CMZ, 0, 1, 1), (WIN, 0, 2),
+    (DOWN,), (COWN, 1), (COWN, 0), (WIN, 3, 2), (WIN, 2, 0), (DPLANE, 1), (CMZ, 0, 1, 1), (WIN, 0, 2),
     (DPLANE, 2), (DPLANE, 3), (CNEAR, 1), (CNEAR, 0), (WIN, 0, 1), (WIN, 1, 1), (CMZ, 0, 1, 0), (WIN, 1, 3),
     (WIN, 1, 0), (WO,), (DCORNER, 0), (DCORNER, 1), (DCORNER, 3), (DCORNER, 2), (WIN, 3, 0), (DLAST, 0),
     (CMZ, 1, 1, 1), (WIN, 2, 1), (CMZ, 1, 1, 0), (WIN, 2, 2), (DLAST, 3), (CMZ, 0, 2, 0), (WIN, 2, 3),
@@ -429,7 +429,7 @@
     def pair(self, pack_task, task_experts, rel, k, p):
         at = self.at[0] + self.step_x * (rel % 2) + self.step_y * (rel // 2)
         task = pack_task[(self.plane(k) * 8 + at) * 2 + p]
-        return task_experts[task, 0], task_experts[task, 1]
+        return task_experts[0, task], task_experts[1, task]
 
     def greet(self):
         barrier = pltpu.get_barrier_semaphore()
@@ -439,7 +439,9 @@
                 barrier, inc=1, device_id=self.device(rel, k), device_id_type=MESH
             )
         pl.semaphore_signal(barrier, inc=1, device_id=self.sibling, device_id_type=MESH)
-        pl.semaphore_wait(barrier, len(others) + 1)
+
+    def meet(self):
+        pl.semaphore_wait(pltpu.get_barrier_semaphore(), 16)
 
 
 def send(started, src, dst, send_sem, recv_sem, device):
@@ -647,6 +649,7 @@
     core_send, core_recv, in_send, in_recv, pair_send, pair_recv, local_sem, out_sem, early_sem,
 ):
     place = Place()
+    place.greet()
     width, experts = tok.shape[2], route_own.shape[1]
     other = 1 - place.core
 
@@ -669,8 +672,10 @@
     square[: gain_one_own.shape[0], :experts] = route_own[...].astype(jnp.float32)
     dense[own, :, 4 * width :] = square[: gain_one_own.shape[0], :].astype(jnp.bfloat16)
     for p in range(2):
-        cot_all[0, p] = lengthened(cot_own, p).astype(jnp.bfloat16)
-    place.greet()
+        cot_all[0, p] = cot_own[p]
+    same_documents(segments, flat_ids, tall_ids)
+    gate_row[...] = jnp.zeros_like(gate_row)
+    place.meet()
 
     dense_tree = Spread(
         place,
@@ -707,8 +712,6 @@
         to_core(0, 0)
         local_copy(w_in.at[:, :, pl.ds(pl.multiple_of(place.chip(0, 0) * SIDE, SIDE), SIDE)],
                    w_in_all.at[place.chip(0, 0), place.core])
-        same_documents(segments, flat_ids, tall_ids)
-        gate_row[...] = jnp.zeros_like(gate_row)
 
     def dplane(j):
         dense_tree.plane(j, 0)
@@ -763,7 +766,7 @@
         mid = block + dot(heads[p], w_attn)
         middle[p] = mid
         unit, unused = norm_parts(mid)
-        routed_all[0, p] = jnp.where(real_rows(), unit * row[2] + row[3], 0.0).astype(jnp.bfloat16)
+        routed_all[0, p] = (unit * row[2] + row[3])[:PACK].astype(jnp.bfloat16)
         routed_tree.own(p, routed_all.at[0, p])
 
     def win(rel, j):
@@ -816,7 +819,7 @@
             pair = place.pair(pack_task, task_experts, rel, place.nearest(j), p)
             rows, cots = routed_all[rel, at], cot_all[rel, at]
             gated, grad_pre, mixed, grad = expert_block(
-                pair, rows, cots, w_in_all, w_out_all, dense, gate_row
+                pair, rows, cots, w_in_all, w_out_all, dense, gate_row.at[rel]
             )
             mixed_all[rel, at] = mixed
             grad_all[rel, at] = grad
@@ -882,10 +885,10 @@
     grad_pre = (gates * back_act * slope).astype(jnp.bfloat16)
     product = (act * back_act).astype(jnp.bfloat16)
     signs = jnp.broadcast_to(jnp.where(lane < SIDE, 1.0, -1.0), (8, slab)).astype(jnp.bfloat16)
-    gate_row[:, :ROWS] = contract_cols(signs, product)
+    gate_row[:, :PACK] = contract_cols(signs, product)
     mixed = dot(gated, w_out).astype(jnp.bfloat16)
     grads = contract_cols(grad_pre, w_in)
-    grad = jnp.concatenate([grads[:PACK], gate_row[...]], axis=0).astype(jnp.bfloat16)
+    grad = jnp.concatenate([grads, gate_row[...]], axis=0).astype(jnp.bfloat16)
     return gated, grad_pre, mixed, grad
 
 
@@ -911,7 +914,7 @@
             at = g + step_x * (rel % 2) + step_y * (rel // 2)
             task = pack_task[(((z + k) % 4) * 8 + at) * 2 + p]
             for i in range(2):
-                e = task_experts[task, i]
+                e = task_experts[i, task]
                 nexts[slot * 2 + i] = heads[e]
                 heads[e] = slot * 2 + i
             return carry
@@ -1215,6 +1218,8 @@
         turned[GAIN_ONE + i : GAIN_ONE + i + 1, :] for i in range(4)
     )
 
+    place.meet()
+
     def pair():
         send(
             pair_started, d_in.at[1 - place.core], in_far, pair_send.at[0], pair_recv.at[0],
@@ -1248,7 +1253,7 @@
     def mplane(j, p):
         mixes.plane(j, p, m_out)
         if j == 3:
-            mixed[p] = (middle[p] + m_out[...]).astype(jnp.bfloat16)
+            mixed[p] = (middle[p, :PACK] + m_out[...]).astype(jnp.bfloat16)
 
     def add_to(p, columns, value):
         if p == 0:
@@ -1409,7 +1414,7 @@
 
 
 def last_kernel(
-    mixed_tall, d_tok_tall, d_dense, d_in_low, d_out_own, d_out_far,
+    mixed_own, d_tok_tall, d_dense, d_in_low, d_out_own, d_out_far,
     mixed, d_tok, d_qkv, d_attn, d_route, d_in, d_out, gain_one, bias_one, gain_two, bias_two,
 ):
     width, experts = mixed.shape[2], d_route.shape[1]
@@ -1417,7 +1422,7 @@
     @pl.when(pl.program_id(0) == 0)
     def small():
         for p in range(mixed.shape[0]):
-            mixed[p] = mixed_tall[p, :PACK]
+            mixed[p] = mixed_own[p]
             d_tok[p] = d_tok_tall[p, :PACK]
         d_qkv[...] = d_dense[:, : 3 * width]
         d_attn[...] = d_dense[:, 3 * width : 4 * width]
@@ -1456,8 +1461,10 @@
     low, full = jnp.bfloat16, jnp.float32
     flat = jax.ShapeDtypeStruct
     dma = pltpu.SemaphoreType.DMA
-
-    blocks = flat((4, 4 * packs, ROWS, width), low)
+    by_rank = task_experts.T
+
+    blocks = flat((4, 4 * packs, length, width), low)
+    tall_blocks = flat((4, 4 * packs, ROWS, width), low)
     in_sums = flat((4, 4 * packs, width, 2 * SIDE), low)
     out_sums = flat((4, 4 * packs, 2 * SIDE, width), low)
 
@@ -1470,7 +1477,7 @@
     ) = pl.pallas_call(
         front_kernel,
         out_shape=(
-            in_sums, out_sums, blocks, blocks,
+            in_sums, out_sums, blocks, tall_blocks,
             flat((32, slab_in, dense_width), low),
             early_blocks, early_blocks,
             flat((packs, ROWS, 3 * width), low),
@@ -1486,12 +1493,12 @@
             pltpu.VMEM((2, experts, slab_out, width), low),
             pltpu.VMEM((2, 4, width, 2 * SIDE), low),
             pltpu.VMEM((2, 4, 2 * SIDE, width), low),
-            held(blocks), held(blocks),
+            held(blocks), held(tall_blocks),
             pltpu.VMEM((SIDE, width), full),
             pltpu.VMEM((SIDE, SIDE), full),
             pltpu.VMEM((8, 2 * SIDE), full),
             pltpu.VMEM((2 * SIDE, 8), full),
-            pltpu.VMEM((8, width), full),
+            pltpu.VMEM((4, 8, width), full),
             dma((7, 8)), dma((4, 8)), dma((5, 8)), dma((4, 8)), dma((5, 4)), dma((4, 4)),
             dma((4, 4)), dma((4, 4)), dma((4, 4)), dma((4, 4)), dma((2,)), dma((2,)), dma((3,)),
             dma((32,)), dma((2, len(EARLY))),
@@ -1501,7 +1508,7 @@
         ),
         name="front",
     )(
-        pack_task, task_experts, tokens, segment_ids, w_qkv, w_attn_out, w_router,
+        pack_task, by_rank, tokens, segment_ids, w_qkv, w_attn_out, w_router,
         norm1_gain, norm1_bias, norm2_gain, norm2_bias, cotangent, w_expert_in, w_expert_out,
     )
 
@@ -1542,15 +1549,15 @@
             flops=10**10, bytes_accessed=40 * 10**6, transcendentals=0
         ),
         name="sums",
-    )(pack_task, task_experts, in_terms, out_terms)
+    )(pack_task, by_rank, in_terms, out_terms)
 
     parts = pltpu.VMEM((4 * packs, ROWS, width), low)
     slices = pltpu.VMEM((4, slab_in, dense_width), low)
     sliced = pltpu.VMEM((16, slab_in, dense_width), low)
-    mixed_tall, d_tok_tall, d_dense, d_in_all, d_out_all = pl.pallas_call(
+    mixed_own, d_tok_tall, d_dense, d_in_all, d_out_all = pl.pallas_call(
         tail_kernel,
         out_shape=(
-            flat((packs, ROWS, width), low),
+            flat((packs, length, width), low),
             flat((packs, ROWS, width), low),
             flat((slab_in, dense_width), full),
             flat((experts, slab_in, hidden), low),
@@ -1561,12 +1568,12 @@
         scratch_shapes=[
             pltpu.VMEM((2, 4 * packs, ROWS, width), low), parts, parts, parts,
             pltpu.VMEM((1, 5 * packs, ROWS, width), low),
-            pltpu.VMEM((2, 4 * packs, ROWS, width), low),
-            pltpu.VMEM((2, 4 * packs, ROWS, width), low),
-            pltpu.VMEM((packs, ROWS, width), low),
-            pltpu.VMEM((2, 5 * packs, ROWS, width), low),
-            pltpu.VMEM((ROWS, width), full),
-            pltpu.VMEM((ROWS, width), full),
+            pltpu.VMEM((2, 4 * packs, length, width), low),
+            pltpu.VMEM((2, 4 * packs, length, width), low),
+            pltpu.VMEM((packs, length, width), low),
+            pltpu.VMEM((2, 5 * packs, length, width), low),
+            pltpu.VMEM((length, width), full),
+            pltpu.VMEM((length, width), full),
             pltpu.VMEM((packs, ROWS, width), full),
             pltpu.VMEM((ROWS, width), full),
             pltpu.VMEM((ROWS, width), low),
@@ -1589,7 +1596,7 @@
         ),
         name="tail",
     )(
-        pack_task, task_experts, tokens, cotangent, segment_ids, proj, heads, middle, dense,
+        pack_task, by_rank, tokens, cotangent, segment_ids, proj, heads, middle, dense,
         grad_part, mixed_part, d_in, d_out_far, got_y, got_x,
     )
 
@@ -1605,7 +1612,7 @@
         last_kernel,
         grid=(2,),
         in_specs=[
-            whole(packs, ROWS, width), whole(packs, ROWS, width), whole(slab_in, dense_width),
+            whole(packs, length, width), whole(packs, ROWS, width), whole(slab_in, dense_width),
             some(slab_in, hidden), some(slab_out, width), some(slab_out, width),
         ],
         out_specs=(
@@ -1621,7 +1628,7 @@
         ) + (flat((slab_in,), full),) * 4,
         compiler_params=pltpu.CompilerParams(vmem_limit_bytes=60 << 20),
         name="last",
-    )(mixed_tall, d_tok_tall, d_dense, d_in_all, d_out_own, d_out_all)
+    )(mixed_own, d_tok_tall, d_dense, d_in_all, d_out_own, d_out_all)
 
 
 def solution(mesh):

time: 338 us -> 331 us (0.979)
  Pallas kernels: 330 us -> 324 us
    pallas_call x3, Pallas kernels: 317 us -> 312 us  [the longest x1 157 us: shards_fast(): pl.pallas_call(front_kernel, out_shape=(in_sums, out_sums, blocks, tall_b...]
where the time goes in v5:
time: 331 us; the launch traced here: 328 us
  Pallas kernels  324 us (98%)
    pallas_call x1, Pallas kernels, shards_fast(): pl.pallas_call(front_kernel, out_shape=(in_sums, out_sums, blocks, tall_b...  157 us
    pallas_call x1, Pallas kernels, shards_fast(): pl.pallas_call(tail_kernel, out_shape=(flat((packs, length, width), low),...  148 us
    pallas_call x1, Pallas kernels, shards_fast(): pl.pallas_call(sum_kernel, grid_spec=pltpu.PrefetchScalarGridSpec(num_sca...  12.6 us
  transfers between devices with their start and end apart: 2, of which 0 were waited for; matrix products, arithmetic and copies ran while one was open for 0% of the time, Pallas kernels for 4%

profile of v5, /device:TPU:8, one launch (start us, length us, event | category | flops | bytes accessed | tf_op | source)
XLA Modules:
  0.0 328.0 jit_solution(9791191443877804385)
XLA Ops:
  0.6 156.7 %front.1 = (bf16[4,8,512,256]{3,2,1,0:T(8,128)(2,1)}, bf16[4,8,256,512]{3,2,1,0:T(8,128)(2,1)}, bf16[4,8,216,512]{3,2,1,0:T(8,128)(2,1)}, bf16[4,8,224,512]{3,2,...) custom-call(s32[64]{0:T(128)} %pack_task.5, ...), custom_call_target="tpu_custom_call" | custom-call | tf_op jit(solution)/shard_map/front/pallas_call | solution.py:1477
  157.3 2.3 collective-permute-start
  159.6 0.0 collective-permute-start.1
  159.7 12.6 %sums.1 = (bf16[2,16,32,16,128]{4,3,2,1,0:T(8,128)(2,1)}, bf16[32,64,512]{2,1,0:T(8,128)(2,1)}, bf16[32,64,512]{2,1,0:T(8,128)(2,1)}) custom-call(s32[64]{0:T(128)} %pack_task.5, s32[2,24]{1,0:T(2,128)} %bitcast.2, bf16[4,8,512,256]{3,2,1,0:T(8,128)(2,1)} %get-tuple-element.35.in_terms, bf16[4,8,256,512]{3,2,1,0:T(8,128)(2,1)} %get-tuple-element.36.out_terms), custom_call_target="tpu_custom_call" | custom-call | flops 10000000000 | bytes 40000000 | tf_op jit(solution)/shard_map/sums/pallas_call | solution.py:1522
  172.2 0.0 collective-permute-done.got_y
  172.3 0.0 copy-start
  172.3 0.0 collective-permute-done.1.got_x
  172.3 0.0 copy-start.1
  172.3 0.7 copy-done
  173.0 0.2 copy-done.1
  173.2 148.3 %tail.1 = (bf16[2,216,512]{2,1,0:T(8,128)(2,1)}, bf16[2,224,512]{2,1,0:T(8,128)(2,1)}, f32[16,2176]{1,0:T(8,128)}, bf16[32,16,2048]{2,1,0:T(8,128)(2,1)}, bf16[32,64,512]{2,1,0:T(8,128)(2,1)}) custom-call(s32[64]{0:T(128)} %pack_task.5, s32[2,24]{1,0:T(2,128)} %bitcast.3, bf16[2,216,512]{2,1,0:T(8,128)(2,1)} %tok.3, bf16[2,216,512]{2,1,0:T(8,128)(2,1)} %cot.1, ...), custom_call_target="tpu_custom_call" | custom-call | tf_op jit(solution)/shard_map/tail/pallas_call | solution.py:1557
  321.5 6.5 %last.1 = (bf16[2,216,512]{2,1,0:T(8,128)(2,1)}, bf16[2,216,512]{2,1,0:T(8,128)(2,1)}, f32[16,1536]{1,0:T(8,128)}, f32[16,512]{1,0:T(8,128)}, f32[16,32]{1,0:T(8...) custom-call(bf16[2,216,512]{2,1,0:T(8,128)(2,1)} %get-tuple-element., ...), custom_call_target="tpu_custom_call" | custom-call | tf_op jit(solution)/shard_map/last/pallas_call | solution.py:1611
Async XLA Ops:
  157.3 14.9 %collective-permute-start = (bf16[2,224,512]{2,1,0:T(8,128)(2,1)}, bf16[2,224,512]{2,1,0:T(8,128)(2,1)S(1)}, u32[]{:S(2)}, u32[]{:S(2)}) collective-permute-start(bf16[2,224,512]{2,1,0:T(8,128)(2,1)} %get-tuple-element.39), channel_id=1, source_target_pairs={{0,4},{1,5},{2,6},{3,7},{4,0},{5,1},{6,2},{7,3},{8,12},{9,13},{10,... | collective-permute-start | bytes 1376264 | tf_op jit(solution)/shard_map/ppermute | solution.py:1516
  159.6 12.6 %collective-permute-start.1 = (bf16[2,224,512]{2,1,0:T(8,128)(2,1)}, bf16[2,224,512]{2,1,0:T(8,128)(2,1)S(1)}, u32[]{:S(2)}, u32[]{:S(2)}) collective-permute-start(bf16[2,224,512]{2,1,0:T(8,128)(2,1)} %get-tuple-element.40), channel_id=1, source_target_pairs={{0,2},{1,3},{2,0},{3,1},{4,6},{5,7},{6,4},{7,5},{8,10},{9,11},{10,... | collective-permute-start | bytes 1376264 | tf_op jit(solution)/shard_map/ppermute | solution.py:1517
  172.3 0.8 copy-start
  172.3 0.9 copy-start.1

commit v6 on v5

--- a/solution.py
+++ b/solution.py
@@ -368,29 +368,29 @@
 EARLY = ((0, 3), (1, 3))
 
 FRONT_STEPS = (
-    (DOWN,), (COWN, 1), (COWN, 0), (WIN, 3, 2), (WIN, 2, 0), (DPLANE, 1), (CMZ, 0, 1, 1), (WIN, 0, 2),
-    (DPLANE, 2), (DPLANE, 3), (CNEAR, 1), (CNEAR, 0), (WIN, 0, 1), (WIN, 1, 1), (CMZ, 0, 1, 0), (WIN, 1, 3),
-    (WIN, 1, 0), (WO,), (DCORNER, 0), (DCORNER, 1), (DCORNER, 3), (DCORNER, 2), (WIN, 3, 0), (DLAST, 0),
-    (CMZ, 1, 1, 1), (WIN, 2, 1), (CMZ, 1, 1, 0), (WIN, 2, 2), (DLAST, 3), (CMZ, 0, 2, 0), (WIN, 2, 3),
-    (WIN, 3, 1), (CMZ, 0, 2, 1), (DLAST, 1), (DLAST, 2), (DWAIT,), (WIN, 1, 2), (ATT, 0), (RCORNER, 0, 0),
-    (ATT, 1), (RPLANE, 1, 0), (CMZ, 1, 2, 1), (WIN, 3, 3), (RPLANE, 1, 1), (WIN, 0, 3), (RCORNER, 0, 1),
-    (RCORNER, 1, 0), (WINWAIT,), (RPLANE, 2, 1), (RPLANE, 2, 0), (RCORNER, 1, 1), (CMZ, 1, 2, 0), (WSIBWAIT,),
-    (WAVE, 0, 0), (CMZ, 0, 3, 0), (WAVE, 1, 0), (RCORNER, 2, 1), (RPLANE, 3, 1), (WAVE, 1, 1),
-    (RCORNER, 2, 0), (RPLANE, 3, 0), (WAVE, 0, 1), (CMZ, 1, 3, 0), (CMZ, 0, 3, 1), (RCORNER, 3, 1),
-    (WAVE, 2, 1), (CMZ, 1, 3, 1), (RCORNER, 3, 0), (WAVE, 2, 0), (WAVE, 3, 0), (WAVE, 3, 1),
+    (DOWN,), (WIN, 2, 0), (COWN, 0), (COWN, 1), (CMZ, 0, 1, 1), (DPLANE, 1), (WIN, 2, 2), (DPLANE, 3),
+    (DPLANE, 2), (CNEAR, 0), (DCORNER, 0), (CNEAR, 1), (WIN, 1, 2), (DCORNER, 2), (WIN, 1, 3), (WIN, 0, 2),
+    (WIN, 1, 1), (CMZ, 0, 1, 0), (DCORNER, 3), (DCORNER, 1), (WIN, 3, 0), (DLAST, 0), (CMZ, 1, 1, 1),
+    (WIN, 3, 2), (DLAST, 3), (WIN, 2, 1), (DLAST, 1), (DLAST, 2), (WIN, 0, 1), (WIN, 3, 3), (WIN, 1, 0),
+    (CMZ, 1, 1, 0), (DWAIT,), (WO,), (CMZ, 0, 2, 0), (WIN, 2, 3), (WIN, 3, 1), (CMZ, 0, 2, 1), (ATT, 0),
+    (RCORNER, 0, 0), (ATT, 1), (RPLANE, 1, 0), (CMZ, 1, 2, 1), (RCORNER, 1, 0), (RCORNER, 0, 1),
+    (RPLANE, 1, 1), (WIN, 0, 3), (RPLANE, 2, 0), (WINWAIT,), (RPLANE, 2, 1), (WSIBWAIT,), (RCORNER, 1, 1),
+    (CMZ, 1, 2, 0), (WAVE, 0, 0), (CMZ, 0, 3, 1), (CMZ, 0, 3, 0), (WAVE, 1, 0), (RCORNER, 2, 0),
+    (RCORNER, 2, 1), (RPLANE, 3, 1), (WAVE, 0, 1), (RPLANE, 3, 0), (WAVE, 1, 1), (CMZ, 1, 3, 0), (WAVE, 2, 1),
+    (CMZ, 1, 3, 1), (RCORNER, 3, 0), (WAVE, 2, 0), (RCORNER, 3, 1), (WAVE, 3, 0), (WAVE, 3, 1),
 )
 TAIL_STEPS = (
-    (GFIRST, 0, 0), (MHELP, 2, 0), (GFIRST, 1, 0), (MHELP, 3, 0), (PAIR,), (GHELP, 0, 0), (GFIRST, 0, 1),
-    (GHELP, 1, 0), (GHELP, 0, 1), (GFIRST, 2, 0), (ADDPAIR,), (WIN, 0, 1), (GFIRST, 1, 1), (GFIRST, 2, 1),
-    (GPLANE, 0, 0), (MFIRST, 0, 1), (GHELP, 1, 1), (MFIRST, 0, 0), (GPLANE, 0, 1), (GPLANE, 1, 0),
-    (WIN, 0, 0), (MHELP, 2, 1), (GFIRST, 3, 1), (GHELP, 2, 1), (GHELP, 2, 0), (GPLANE, 1, 1), (GFIRST, 3, 0),
-    (MFIRST, 1, 1), (MHELP, 3, 1), (MPLANE, 0, 0), (GPLANE, 2, 1), (MFIRST, 1, 0), (GHELP, 3, 0),
-    (MPLANE, 0, 1), (MHELP, 0, 1), (GPLANE, 2, 0), (MFIRST, 2, 0), (MPLANE, 1, 0), (MFIRST, 2, 1),
-    (MFIRST, 3, 1), (GHELP, 3, 1), (MPLANE, 1, 1), (WIN, 3, 1), (MPLANE, 2, 0), (GPLANE, 3, 0), (WIN, 1, 0),
-    (GPLANE, 3, 1), (MFIRST, 3, 0), (ATT, 0), (WIN, 3, 3), (ATT, 1), (MPLANE, 2, 1), (ATT, 2), (MHELP, 0, 0),
-    (MHELP, 1, 0), (MHELP, 1, 1), (ATT, 3), (WIN, 2, 3), (WIN, 1, 2), (WIN, 3, 2), (WIN, 2, 1), (WIN, 2, 2),
-    (ATT, 4), (ATT, 5), (MPLANE, 3, 0), (WIN, 1, 1), (WIN, 3, 0), (WIN, 1, 3), (WIN, 2, 0), (WIN, 0, 2),
-    (MPLANE, 3, 1), (DENSE,),
+    (GFIRST, 0, 0), (PAIR,), (GFIRST, 1, 0), (GFIRST, 0, 1), (MHELP, 0, 1), (GHELP, 0, 0), (GHELP, 1, 0),
+    (GHELP, 0, 1), (GFIRST, 2, 0), (ADDPAIR,), (WIN, 0, 1), (GFIRST, 1, 1), (GFIRST, 2, 1), (GHELP, 1, 1),
+    (GPLANE, 0, 0), (MFIRST, 0, 1), (MFIRST, 0, 0), (WIN, 0, 0), (GPLANE, 0, 1), (MHELP, 2, 1),
+    (GPLANE, 1, 0), (GFIRST, 3, 1), (GHELP, 2, 0), (GHELP, 2, 1), (GFIRST, 3, 0), (GPLANE, 1, 1),
+    (MFIRST, 1, 1), (MFIRST, 1, 0), (MHELP, 3, 0), (MPLANE, 0, 0), (MPLANE, 0, 1), (GPLANE, 2, 1),
+    (MHELP, 2, 0), (MHELP, 3, 1), (GHELP, 3, 0), (MFIRST, 2, 0), (GPLANE, 2, 0), (MHELP, 1, 0),
+    (MPLANE, 1, 0), (MFIRST, 2, 1), (MPLANE, 1, 1), (GHELP, 3, 1), (MFIRST, 3, 1), (WIN, 3, 1),
+    (MPLANE, 2, 0), (GPLANE, 3, 0), (GPLANE, 3, 1), (ATT, 0), (WIN, 3, 3), (WIN, 1, 0), (MFIRST, 3, 0),
+    (ATT, 1), (MPLANE, 2, 1), (WIN, 2, 3), (WIN, 2, 1), (ATT, 2), (ATT, 3), (WIN, 3, 2), (MHELP, 0, 0),
+    (WIN, 1, 2), (ATT, 4), (MPLANE, 3, 0), (MHELP, 1, 1), (ATT, 5), (WIN, 1, 3), (WIN, 1, 1), (WIN, 2, 0),
+    (WIN, 2, 2), (WIN, 3, 0), (MPLANE, 3, 1), (WIN, 0, 2), (DENSE,),
 )
 
 

time: 331 us -> 329 us (level)
  no operation moved by 1% of the time
where the time goes in v6:
time: 329 us
  Pallas kernels  325 us (99%)
    pallas_call x1, Pallas kernels, shards_fast(): pl.pallas_call(front_kernel, out_shape=(in_sums, out_sums, blocks, tall_b...  159 us
    pallas_call x1, Pallas kernels, shards_fast(): pl.pallas_call(tail_kernel, out_shape=(flat((packs, length, width), low),...  148 us
    pallas_call x1, Pallas kernels, shards_fast(): pl.pallas_call(sum_kernel, grid_spec=pltpu.PrefetchScalarGridSpec(num_sca...  12.4 us
  transfers between devices with their start and end apart: 2, of which 0 were waited for; matrix products, arithmetic and copies ran while one was open for 0% of the time, Pallas kernels for 4%

profile of v6, /device:TPU:8, one launch (start us, length us, event | category | flops | bytes accessed | tf_op | source)
XLA Modules:
  0.0 328.7 jit_solution(874970447684922070)
XLA Ops:
  0.6 158.9 %front.1 = (bf16[4,8,512,256]{3,2,1,0:T(8,128)(2,1)}, bf16[4,8,256,512]{3,2,1,0:T(8,128)(2,1)}, bf16[4,8,216,512]{3,2,1,0:T(8,128)(2,1)}, bf16[4,8,224,512]{3,2,...) custom-call(s32[64]{0:T(128)} %pack_task.5, ...), custom_call_target="tpu_custom_call" | custom-call | tf_op jit(solution)/shard_map/front/pallas_call | solution.py:1477
  159.5 0.8 collective-permute-start
  160.3 1.0 collective-permute-start.1
  161.3 12.4 %sums.1 = (bf16[2,16,32,16,128]{4,3,2,1,0:T(8,128)(2,1)}, bf16[32,64,512]{2,1,0:T(8,128)(2,1)}, bf16[32,64,512]{2,1,0:T(8,128)(2,1)}) custom-call(s32[64]{0:T(128)} %pack_task.5, s32[2,24]{1,0:T(2,128)} %bitcast.2, bf16[4,8,512,256]{3,2,1,0:T(8,128)(2,1)} %get-tuple-element.35.in_terms, bf16[4,8,256,512]{3,2,1,0:T(8,128)(2,1)} %get-tuple-element.36.out_terms), custom_call_target="tpu_custom_call" | custom-call | flops 10000000000 | bytes 40000000 | tf_op jit(solution)/shard_map/sums/pallas_call | solution.py:1522
  173.7 0.0 collective-permute-done.got_y
  173.7 0.0 copy-start
  173.7 0.0 collective-permute-done.1.got_x
  173.7 0.0 copy-start.1
  173.7 0.7 copy-done
  174.5 0.2 copy-done.1
  174.6 147.5 %tail.1 = (bf16[2,216,512]{2,1,0:T(8,128)(2,1)}, bf16[2,224,512]{2,1,0:T(8,128)(2,1)}, f32[16,2176]{1,0:T(8,128)}, bf16[32,16,2048]{2,1,0:T(8,128)(2,1)}, bf16[32,64,512]{2,1,0:T(8,128)(2,1)}) custom-call(s32[64]{0:T(128)} %pack_task.5, s32[2,24]{1,0:T(2,128)} %bitcast.3, bf16[2,216,512]{2,1,0:T(8,128)(2,1)} %tok.3, bf16[2,216,512]{2,1,0:T(8,128)(2,1)} %cot.1, ...), custom_call_target="tpu_custom_call" | custom-call | tf_op jit(solution)/shard_map/tail/pallas_call | solution.py:1557
  322.2 6.5 %last.1 = (bf16[2,216,512]{2,1,0:T(8,128)(2,1)}, bf16[2,216,512]{2,1,0:T(8,128)(2,1)}, f32[16,1536]{1,0:T(8,128)}, f32[16,512]{1,0:T(8,128)}, f32[16,32]{1,0:T(8...) custom-call(bf16[2,216,512]{2,1,0:T(8,128)(2,1)} %get-tuple-element., ...), custom_call_target="tpu_custom_call" | custom-call | tf_op jit(solution)/shard_map/last/pallas_call | solution.py:1611
Async XLA Ops:
  159.5 14.2 %collective-permute-start = (bf16[2,224,512]{2,1,0:T(8,128)(2,1)}, bf16[2,224,512]{2,1,0:T(8,128)(2,1)S(1)}, u32[]{:S(2)}, u32[]{:S(2)}) collective-permute-start(bf16[2,224,512]{2,1,0:T(8,128)(2,1)} %get-tuple-element.39), channel_id=1, source_target_pairs={{0,4},{1,5},{2,6},{3,7},{4,0},{5,1},{6,2},{7,3},{8,12},{9,13},{10,... | collective-permute-start | bytes 1376264 | tf_op jit(solution)/shard_map/ppermute | solution.py:1516
  160.3 13.4 %collective-permute-start.1 = (bf16[2,224,512]{2,1,0:T(8,128)(2,1)}, bf16[2,224,512]{2,1,0:T(8,128)(2,1)S(1)}, u32[]{:S(2)}, u32[]{:S(2)}) collective-permute-start(bf16[2,224,512]{2,1,0:T(8,128)(2,1)} %get-tuple-element.40), channel_id=1, source_target_pairs={{0,2},{1,3},{2,0},{3,1},{4,6},{5,7},{6,4},{7,5},{8,10},{9,11},{10,... | collective-permute-start | bytes 1376264 | tf_op jit(solution)/shard_map/ppermute | solution.py:1517
  173.7 0.8 copy-start
  173.7 0.9 copy-start.1

commit v7 on v6

--- a/solution.py
+++ b/solution.py
@@ -919,7 +919,7 @@
                 heads[e] = slot * 2 + i
             return carry
 
-        lax.fori_loop(0, slots, one, 0)
+        lax.fori_loop(0, slots, one, 0, unroll=4)
 
     def terms(use):
         slot = use // 2

time: 329 us -> 329 us (level)
  no operation moved by 1% of the time
where the time goes in v7:
time: 329 us
  Pallas kernels  325 us (99%)
    pallas_call x1, Pallas kernels, shards_fast(): pl.pallas_call(front_kernel, out_shape=(in_sums, out_sums, blocks, tall_b...  159 us
    pallas_call x1, Pallas kernels, shards_fast(): pl.pallas_call(tail_kernel, out_shape=(flat((packs, length, width), low),...  148 us
    pallas_call x1, Pallas kernels, shards_fast(): pl.pallas_call(sum_kernel, grid_spec=pltpu.PrefetchScalarGridSpec(num_sca...  12.3 us
  transfers between devices with their start and end apart: 2, of which 0 were waited for; matrix products, arithmetic and copies ran while one was open for 0% of the time, Pallas kernels for 4%

profile of v7, /device:TPU:8, one launch (start us, length us, event | category | flops | bytes accessed | tf_op | source)
XLA Modules:
  0.0 328.6 jit_solution(2618651202273538070)
XLA Ops:
  0.6 158.8 %front.1 = (bf16[4,8,512,256]{3,2,1,0:T(8,128)(2,1)}, bf16[4,8,256,512]{3,2,1,0:T(8,128)(2,1)}, bf16[4,8,216,512]{3,2,1,0:T(8,128)(2,1)}, bf16[4,8,224,512]{3,2,...) custom-call(s32[64]{0:T(128)} %pack_task.5, ...), custom_call_target="tpu_custom_call" | custom-call | tf_op jit(solution)/shard_map/front/pallas_call | solution.py:1477
  159.5 0.8 collective-permute-start
  160.3 1.0 collective-permute-start.1
  161.3 12.3 %sums.1 = (bf16[2,16,32,16,128]{4,3,2,1,0:T(8,128)(2,1)}, bf16[32,64,512]{2,1,0:T(8,128)(2,1)}, bf16[32,64,512]{2,1,0:T(8,128)(2,1)}) custom-call(s32[64]{0:T(128)} %pack_task.5, s32[2,24]{1,0:T(2,128)} %bitcast.2, bf16[4,8,512,256]{3,2,1,0:T(8,128)(2,1)} %get-tuple-element.35.in_terms, bf16[4,8,256,512]{3,2,1,0:T(8,128)(2,1)} %get-tuple-element.36.out_terms), custom_call_target="tpu_custom_call" | custom-call | flops 10000000000 | bytes 40000000 | tf_op jit(solution)/shard_map/sums/pallas_call | solution.py:1522
  173.7 0.0 collective-permute-done.got_y
  173.7 0.0 copy-start
  173.7 0.0 collective-permute-done.1.got_x
  173.7 0.0 copy-start.1
  173.7 0.7 copy-done
  174.4 0.2 copy-done.1
  174.6 147.5 %tail.1 = (bf16[2,216,512]{2,1,0:T(8,128)(2,1)}, bf16[2,224,512]{2,1,0:T(8,128)(2,1)}, f32[16,2176]{1,0:T(8,128)}, bf16[32,16,2048]{2,1,0:T(8,128)(2,1)}, bf16[32,64,512]{2,1,0:T(8,128)(2,1)}) custom-call(s32[64]{0:T(128)} %pack_task.5, s32[2,24]{1,0:T(2,128)} %bitcast.3, bf16[2,216,512]{2,1,0:T(8,128)(2,1)} %tok.3, bf16[2,216,512]{2,1,0:T(8,128)(2,1)} %cot.1, ...), custom_call_target="tpu_custom_call" | custom-call | tf_op jit(solution)/shard_map/tail/pallas_call | solution.py:1557
  322.1 6.5 %last.1 = (bf16[2,216,512]{2,1,0:T(8,128)(2,1)}, bf16[2,216,512]{2,1,0:T(8,128)(2,1)}, f32[16,1536]{1,0:T(8,128)}, f32[16,512]{1,0:T(8,128)}, f32[16,32]{1,0:T(8...) custom-call(bf16[2,216,512]{2,1,0:T(8,128)(2,1)} %get-tuple-element., ...), custom_call_target="tpu_custom_call" | custom-call | tf_op jit(solution)/shard_map/last/pallas_call | solution.py:1611
Async XLA Ops:
  159.5 14.2 %collective-permute-start = (bf16[2,224,512]{2,1,0:T(8,128)(2,1)}, bf16[2,224,512]{2,1,0:T(8,128)(2,1)S(1)}, u32[]{:S(2)}, u32[]{:S(2)}) collective-permute-start(bf16[2,224,512]{2,1,0:T(8,128)(2,1)} %get-tuple-element.39), channel_id=1, source_target_pairs={{0,4},{1,5},{2,6},{3,7},{4,0},{5,1},{6,2},{7,3},{8,12},{9,13},{10,... | collective-permute-start | bytes 1376264 | tf_op jit(solution)/shard_map/ppermute | solution.py:1516
  160.3 13.3 %collective-permute-start.1 = (bf16[2,224,512]{2,1,0:T(8,128)(2,1)}, bf16[2,224,512]{2,1,0:T(8,128)(2,1)S(1)}, u32[]{:S(2)}, u32[]{:S(2)}) collective-permute-start(bf16[2,224,512]{2,1,0:T(8,128)(2,1)} %get-tuple-element.40), channel_id=1, source_target_pairs={{0,2},{1,3},{2,0},{3,1},{4,6},{5,7},{6,4},{7,5},{8,10},{9,11},{10,... | collective-permute-start | bytes 1376264 | tf_op jit(solution)/shard_map/ppermute | solution.py:1517
  173.7 0.8 copy-start
  173.7 0.9 copy-start.1
